TPU v7x, 128 devices: a whole 4x4x4 slice. The times are simulated.
128 devices in a mesh: pp: 2 (over core), fsdp: 16 (over y, x), tp: 4 (over z).
Axes of the slice: x: 4, y: 4, z: 4, core: 2. Of those that a mesh axis runs over, the one named last changes fastest.
Arguments:
- inputs: bfloat16 [2, 512, 8192], P(None, 'tp', 'fsdp'), may hold values from -12 to 12
- head_grad: bfloat16 [2, 512, 8192], P(None, 'tp', 'fsdp'), may hold values from -0.3 to 0.3
- noise_mask: int32 [2, 512], P(None, 'tp'), may hold values 0 or 1
- lengths: int32 [2, 16, 2], replicated, may hold values from 1 to 24, 32 in all within a row
- rewards: int32 [2, 16, 2], replicated, may hold values from 0 to 3
- groups: int32 [2, 16, 2], replicated, may hold values from 0 to 31, as said below
- query_weight: bfloat16 [2, 8192, 4096], P('pp', 'fsdp', 'tp'), may hold values from -0.0625 to 0.0625
- key_weight: bfloat16 [2, 8192, 1024], P('pp', 'fsdp', 'tp'), may hold values from -0.0625 to 0.0625
- value_weight: bfloat16 [2, 8192, 1024], P('pp', 'fsdp', 'tp'), may hold values from -1 to 1
- out_weight: bfloat16 [2, 4096, 8192], P('pp', 'tp', 'fsdp'), may hold values from -1 to 1
Outputs:
- query_weight_grad: float32 [2, 8192, 4096], P('pp', 'fsdp', 'tp')
- key_weight_grad: float32 [2, 8192, 1024], P('pp', 'fsdp', 'tp')
- value_weight_grad: float32 [2, 8192, 1024], P('pp', 'fsdp', 'tp')
- out_weight_grad: float32 [2, 4096, 8192], P('pp', 'tp', 'fsdp')
Inputs may be any that keep to these rules, and one draw needn't show every extreme that they name: `groups`: every group value names exactly 2 completions.
All inputs are finite; a program needn't handle non-finite values. No bound on the sum of `noise_mask` on one device may be relied on, other than what follows from the above.
Results may differ from a plain program's by a relative error of at most 0.013.
Values may be sent and summed in bfloat16 or wider, within the bound.
A program may use at most 128 MiB of HBM per device.

v0:
```python
import jax
import jax.numpy as jnp
from jax import lax
from jax.sharding import PartitionSpec as P

MODEL_WIDTH = 8192
HEAD_WIDTH = 128
SLOT = 32


epsilon = 1e-06
masked_score = -1e30


def from_behind(value, axis, steps):
    count = lax.axis_size(axis)
    initial, last = (max(0, -steps), min(count, count - steps))
    return lax.ppermute(value, axis, [(source, source + steps) for source in range(initial, last)])


def segments(lengths):
    segment_ends = jnp.cumsum(lengths, -1)
    position = jnp.arange(SLOT, dtype=jnp.int32)
    return jnp.sum((segment_ends[..., None, :] <= position[:, None]).astype(jnp.int32), -1)


def token_weights(lengths, rewards, groups):
    group_total = 2 * lengths.shape[1]
    reward_flat = rewards.reshape(-1).astype(jnp.float32)
    member = (
        groups.reshape(-1)[:, None] == jnp.arange(group_total, dtype=jnp.int32)[None, :]
    ).astype(jnp.float32)
    member_count = jnp.sum(member, 0)
    group_mean = jnp.sum(member * reward_flat[:, None], 0) / member_count
    centered = reward_flat - jnp.sum(member * group_mean[None, :], 1)
    variance = jnp.sum(member * (centered * centered)[:, None], 0) / member_count
    spread_own = jnp.sum(member * jnp.sqrt(variance)[None, :], 1)
    advantage = (centered / jnp.maximum(spread_own, 1.0)).reshape(lengths.shape)
    segment = segments(lengths)
    choose = (segment[..., None] == jnp.arange(lengths.shape[2], dtype=jnp.int32)).astype(
        jnp.float32
    )
    token_adv = jnp.sum(choose * advantage[:, :, None, :], -1)
    token_len = jnp.sum(choose * lengths[:, :, None, :].astype(jnp.float32), -1)
    return (token_adv * SLOT / token_len).reshape(lengths.shape[0], -1)


def split_heads(query_rows, key_rows, value_rows):
    batch_count, slot_len = (query_rows.shape[0], query_rows.shape[1])
    kv_heads = key_rows.shape[-1] // HEAD_WIDTH
    group_heads = query_rows.shape[-1] // HEAD_WIDTH // kv_heads
    query_heads = query_rows.reshape(
        batch_count, slot_len, kv_heads, group_heads, HEAD_WIDTH
    ).astype(jnp.float32)
    key_heads = key_rows.reshape(batch_count, slot_len, kv_heads, HEAD_WIDTH).astype(jnp.float32)
    value_heads = value_rows.reshape(batch_count, slot_len, kv_heads, HEAD_WIDTH).astype(
        jnp.float32
    )
    return (query_heads, key_heads, value_heads)


def attend(query_rows, key_rows, value_rows, segment):
    query_heads, key_heads, value_heads = split_heads(query_rows, key_rows, value_rows)
    score_scale = HEAD_WIDTH ** (-0.5)
    scores = jnp.einsum("bikgd,bjkd->bkgij", query_heads, key_heads) * score_scale
    same_doc = segment[:, None, None, :, None] == segment[:, None, None, None, :]
    scores = jnp.where(same_doc, scores, masked_score)
    attn_probs = jax.nn.softmax(scores, axis=-1)
    rounded = lax.optimization_barrier(attn_probs.astype(jnp.bfloat16)).astype(jnp.float32)
    mixture = jnp.einsum("bkgij,bjkd->bikgd", rounded, value_heads)
    return (mixture.reshape(query_rows.shape).astype(jnp.bfloat16), attn_probs)


def attend_back(query_rows, key_rows, value_rows, attn_probs, head_out_grad):
    query_heads, key_heads, value_heads = split_heads(query_rows, key_rows, value_rows)
    score_scale = HEAD_WIDTH ** (-0.5)
    grad_heads = head_out_grad.reshape(query_heads.shape).astype(jnp.float32)
    rounded = lax.optimization_barrier(attn_probs.astype(jnp.bfloat16)).astype(jnp.float32)
    prob_grad = jnp.einsum("bikgd,bjkd->bkgij", grad_heads, value_heads)
    value_grad = jnp.einsum("bkgij,bikgd->bjkd", rounded, grad_heads)
    score_grad = attn_probs * (prob_grad - jnp.sum(prob_grad * attn_probs, -1, keepdims=True))
    score_grad = lax.optimization_barrier(score_grad.astype(jnp.bfloat16)).astype(jnp.float32)
    query_grad = jnp.einsum("bkgij,bjkd->bikgd", score_grad, key_heads) * score_scale
    key_grad = jnp.einsum("bkgij,bikgd->bjkd", score_grad, query_heads) * score_scale
    return (
        query_grad.reshape(query_rows.shape).astype(jnp.bfloat16),
        key_grad.reshape(key_rows.shape).astype(jnp.bfloat16),
        value_grad.reshape(value_rows.shape).astype(jnp.bfloat16),
    )


def front(stream, query_layer, key_layer, value_layer, segment):
    stream_float = stream.astype(jnp.float32)
    squares = lax.psum(jnp.sum(stream_float * stream_float, -1), "fsdp")
    inv_rms = lax.rsqrt(squares / MODEL_WIDTH + epsilon)
    normed = (stream_float * inv_rms[:, None]).astype(jnp.bfloat16)
    normed_all = lax.all_gather(normed, "tp", axis=0, tiled=True)
    query_cols = query_layer.shape[1]
    key_cols = key_layer.shape[1]
    projected = lax.psum_scatter(
        jnp.concatenate(
            [
                jnp.dot(normed_all, query_layer, preferred_element_type=jnp.float32),
                jnp.dot(normed_all, key_layer, preferred_element_type=jnp.float32),
                jnp.dot(normed_all, value_layer, preferred_element_type=jnp.float32),
            ],
            1,
        ),
        "fsdp",
        scatter_dimension=0,
        tiled=True,
    )
    query_rows = projected[:, :query_cols].astype(jnp.bfloat16)
    key_rows = projected[:, query_cols : query_cols + key_cols].astype(jnp.bfloat16)
    value_rows = projected[:, query_cols + key_cols :].astype(jnp.bfloat16)
    head_out, attn_probs = attend(query_rows[None], key_rows[None], value_rows[None], segment)
    return (inv_rms, normed_all, query_rows, key_rows, value_rows, attn_probs, head_out[0])


def spread(head_out):
    return lax.all_gather(head_out, "fsdp", axis=0, tiled=True)


def finish(stream, heads_all, out_layer):
    summed = lax.psum_scatter(
        jnp.dot(heads_all, out_layer, preferred_element_type=jnp.float32),
        "tp",
        scatter_dimension=0,
        tiled=True,
    )
    return (stream.astype(jnp.float32) + summed).astype(jnp.bfloat16)


def back(
    out_grad,
    stream,
    inv_rms,
    normed_all,
    query_rows,
    key_rows,
    value_rows,
    attn_probs,
    heads_all,
    query_layer,
    key_layer,
    value_layer,
    out_layer,
):
    grad_all = lax.all_gather(out_grad, "tp", axis=0, tiled=True)
    out_weight_grad = jnp.einsum(
        "tq,td->qd", heads_all, grad_all, preferred_element_type=jnp.float32
    )
    head_out_grad = lax.psum_scatter(
        jnp.einsum("td,qd->tq", grad_all, out_layer, preferred_element_type=jnp.float32),
        "fsdp",
        scatter_dimension=0,
        tiled=True,
    ).astype(jnp.bfloat16)
    query_grad, key_grad, value_grad = attend_back(
        query_rows[None], key_rows[None], value_rows[None], attn_probs, head_out_grad[None]
    )
    query_all, key_all, value_gathered = (
        lax.all_gather(query_grad[0], "fsdp", axis=0, tiled=True),
        lax.all_gather(key_grad[0], "fsdp", axis=0, tiled=True),
        lax.all_gather(value_grad[0], "fsdp", axis=0, tiled=True),
    )
    query_weight_grad = jnp.einsum(
        "tm,tq->mq", normed_all, query_all, preferred_element_type=jnp.float32
    )
    key_weight_grad = jnp.einsum(
        "tm,tq->mq", normed_all, key_all, preferred_element_type=jnp.float32
    )
    value_weight_grad = jnp.einsum(
        "tm,tq->mq", normed_all, value_gathered, preferred_element_type=jnp.float32
    )
    normed_grad = lax.psum_scatter(
        jnp.einsum("tq,mq->tm", query_all, query_layer, preferred_element_type=jnp.float32)
        + jnp.einsum("tq,mq->tm", key_all, key_layer, preferred_element_type=jnp.float32)
        + jnp.einsum("tq,mq->tm", value_gathered, value_layer, preferred_element_type=jnp.float32),
        "tp",
        scatter_dimension=0,
        tiled=True,
    )
    stream_float = stream.astype(jnp.float32)
    grad_dot = lax.psum(jnp.sum(normed_grad * stream_float, -1), "fsdp")
    input_grad = (
        out_grad.astype(jnp.float32)
        + inv_rms[:, None] * normed_grad
        - stream_float * (inv_rms**3 * grad_dot / MODEL_WIDTH)[:, None]
    ).astype(jnp.bfloat16)
    return (input_grad, (query_weight_grad, key_weight_grad, value_weight_grad, out_weight_grad))


def keep_item(store, index_now, value_now, active):
    return store.at[index_now].set(jnp.where(active, value_now, store[index_now]))


def local(
    inputs,
    head_grad,
    noise_mask,
    lengths,
    rewards,
    groups,
    query_weight,
    key_weight,
    value_weight,
    out_weight,
):
    query_layer, key_layer = (query_weight[0], key_weight[0])
    value_layer, out_layer = (value_weight[0], out_weight[0])
    section_index = lax.axis_index("pp")
    sections = lax.axis_size("pp")
    micro_count, row_count = (inputs.shape[0], inputs.shape[1])
    shard_index = lax.axis_index("fsdp")
    segment_all = segments(lengths)
    weight_all = token_weights(lengths, rewards, groups)
    own_weights = lax.dynamic_slice_in_dim(
        weight_all, lax.axis_index("tp") * row_count, row_count, 1
    ) * noise_mask.astype(jnp.float32)
    top_grad = (-own_weights[:, :, None] * head_grad.astype(jnp.float32)).astype(jnp.bfloat16)
    tick_total = micro_count + sections - 1
    incoming = jnp.zeros_like(inputs[0])
    inputs_kept = jnp.zeros_like(inputs)
    for tick_index in range(tick_total):
        micro_now = tick_index - section_index
        active = (micro_now >= 0) & (micro_now < micro_count)
        slot_micro = jnp.clip(micro_now, 0, micro_count - 1)
        stream = jnp.where(section_index == 0, inputs[min(tick_index, micro_count - 1)], incoming)
        segment = segment_all[slot_micro, shard_index][None]
        inv_rms, normed_all, query_rows, key_rows, value_rows, attn_probs, head_out = front(
            stream, query_layer, key_layer, value_layer, segment
        )
        heads_all = spread(head_out)
        following = finish(stream, heads_all, out_layer)
        inputs_kept = keep_item(inputs_kept, slot_micro, stream, active)
        if tick_index + 1 < tick_total:
            incoming = from_behind(following, "pp", 1)
    totals = (
        jnp.zeros(query_layer.shape, jnp.float32),
        jnp.zeros(key_layer.shape, jnp.float32),
        jnp.zeros(value_layer.shape, jnp.float32),
        jnp.zeros(out_layer.shape, jnp.float32),
    )
    incoming = jnp.zeros_like(inputs[0])
    for tick_index in range(tick_total):
        micro_now = tick_index - (sections - 1 - section_index)
        active = (micro_now >= 0) & (micro_now < micro_count)
        slot_micro = jnp.clip(micro_now, 0, micro_count - 1)
        out_grad = jnp.where(section_index == sections - 1, top_grad[slot_micro], incoming)
        stream = inputs_kept[slot_micro]
        segment = segment_all[slot_micro, shard_index][None]
        inv_rms, normed_all, query_rows, key_rows, value_rows, attn_probs, head_out = front(
            stream, query_layer, key_layer, value_layer, segment
        )
        heads_all = spread(head_out)
        input_grad, terms = back(
            out_grad,
            stream,
            inv_rms,
            normed_all,
            query_rows,
            key_rows,
            value_rows,
            attn_probs,
            heads_all,
            query_layer,
            key_layer,
            value_layer,
            out_layer,
        )
        totals = tuple((total + jnp.where(active, term, 0.0) for total, term in zip(totals, terms)))
        if tick_index + 1 < tick_total:
            incoming = from_behind(input_grad, "pp", -1)
    return (totals[0][None], totals[1][None], totals[2][None], totals[3][None])


def solution(mesh):
    return jax.shard_map(
        local,
        mesh=mesh,
        in_specs=(
            P(None, "tp", "fsdp"),
            P(None, "tp", "fsdp"),
            P(None, "tp"),
            P(),
            P(),
            P(),
            P("pp", "fsdp", "tp"),
            P("pp", "fsdp", "tp"),
            P("pp", "fsdp", "tp"),
            P("pp", "tp", "fsdp"),
        ),
        out_specs=(
            P("pp", "fsdp", "tp"),
            P("pp", "fsdp", "tp"),
            P("pp", "fsdp", "tp"),
            P("pp", "tp", "fsdp"),
        ),
        check_vma=False,
    )
```

profile of v0, /device:TPU:0, one launch (start us, length us, event | category | flops | bytes accessed | tf_op | source)
XLA Modules:
  0.0 1341.3 jit_solution(5943113684509119962)
XLA Ops:
  8.3 40.7 %psum.49 = f32[128]{0:T(128)S(1)} all-reduce(f32[128]{0:T(128)S(1)} %fusion.74), channel_id=1, replica_groups=mesh['pp'=2,'fsdp'=16,'tp'=4] {'fsdp'}, use_global_device_ids=true, to_apply=%region_3.4 | all-reduce | flops 128 | bytes 1024 | tf_op jit(solution)/shard_map/psum | solution.py:94
  50.1 14.1 %all_gather.66 = bf16[512,512]{1,0:T(8,128)(2,1)S(1)} all-gather(bf16[128,512]{1,0:T(8,128)(2,1)S(1)} %fusion.75), channel_id=1, replica_groups=mesh['pp'=2,'fsdp'=16,'tp'=4] {'tp'}, dimensions={0}, use_global_device_ids=true | all-gather | bytes 655360 | tf_op jit(solution)/shard_map/all_gather | solution.py:97
  65.6 2.0 pad_maximum_fusion
  68.9 70.4 %reduce-scatter.13.cloned.1.call-done = f32[32,1536]{1,0:T(8,128)} async-done(((f32[512,1536]{1,0:T(8,128)}), f32[32,1536]{1,0:T(8,128)}) %reduce-scatter.13.cloned.1.call-update) | async-done | bytes 196624 | tf_op jit(solution)/shard_map/reduce_scatter | solution.py:100
  141.7 42.2 %all-gather.10.cloned.1.call-done = bf16[512,1024]{1,0:T(8,128)(2,1)} async-done(((bf16[32,1024]{1,0:T(8,128)(2,1)}), bf16[512,1024]{1,0:T(8,128)(2,1)}) %all-gather.10.cloned.1.call-update) | async-done | bytes 1048592 | tf_op jit(solution)/shard_map/all_gather | solution.py:121
  183.9 2.9 fusion.52
  186.9 23.1 %reduce-scatter.15.cloned.1.call-done = f32[128,512]{1,0:T(8,128)} async-done(((f32[512,512]{1,0:T(8,128)}), f32[128,512]{1,0:T(8,128)}) %reduce-scatter.15.cloned.1.call-update) | async-done | bytes 262160 | tf_op jit(solution)/shard_map/reduce_scatter | solution.py:125
  211.0 1.3 collective-permute-start
  213.4 40.3 %psum.50 = f32[128]{0:T(128)S(1)} all-reduce(f32[128]{0:T(128)S(1)} %get-tuple-element.54), channel_id=1, replica_groups=mesh['pp'=2,'fsdp'=16,'tp'=4] {'fsdp'}, use_global_device_ids=true, to_apply=%region_12.13 | all-reduce | flops 128 | bytes 1024 | tf_op jit(solution)/shard_map/psum | solution.py:94
  253.8 12.8 all_gather.68
  267.9 2.0 pad_maximum_fusion.1
  271.2 69.2 %reduce-scatter.17.cloned.1.call-done = f32[32,1536]{1,0:T(8,128)} async-done(((f32[512,1536]{1,0:T(8,128)}), f32[32,1536]{1,0:T(8,128)}) %reduce-scatter.17.cloned.1.call-update) | async-done | bytes 196624 | tf_op jit(solution)/shard_map/reduce_scatter | solution.py:100
  343.6 41.5 %all-gather.12.cloned.1.call-done = bf16[512,1024]{1,0:T(8,128)(2,1)} async-done(((bf16[32,1024]{1,0:T(8,128)(2,1)}), bf16[512,1024]{1,0:T(8,128)(2,1)}) %all-gather.12.cloned.1.call-update) | async-done | bytes 1048592 | tf_op jit(solution)/shard_map/all_gather | solution.py:121
  385.1 2.9 fusion.50
  389.6 15.2 %all-gather = bf16[1,512,512]{2,1,0:T(8,128)(2,1)S(1)} all-gather(bf16[1,128,512]{2,1,0:T(8,128)(2,1)S(1)} %dynamic-slice_select_fusion), channel_id=2, replica_groups=mesh['pp'=2,'fsdp'=16,'tp'=4] {'tp'}, dimensions={1}, use_global_device_ids=true | all-gather | bytes 655360 | tf_op jit(solution)/shard_map/all_gather | solution.py:149
  404.8 2.1 fusion.48
  408.6 3.4 reduce-scatter.19.cloned.1.call-done
  413.0 1.3 collective-permute-start.1
  416.0 40.2 %psum.51 = f32[128]{0:T(128)S(1)} all-reduce(f32[128]{0:T(128)S(1)} %fusion.77), channel_id=1, replica_groups=mesh['pp'=2,'fsdp'=16,'tp'=4] {'fsdp'}, use_global_device_ids=true, to_apply=%region_18.19 | all-reduce | flops 128 | bytes 1024 | tf_op jit(solution)/shard_map/psum | solution.py:94
  456.3 12.8 all_gather.70
  470.4 2.0 pad_maximum_fusion.2
  472.4 16.9 %reduce-scatter.23.cloned.1.call-done = f32[32,1024]{1,0:T(8,128)} async-done(((f32[512,1024]{1,0:T(8,128)}), f32[32,1024]{1,0:T(8,128)}) %reduce-scatter.23.cloned.1.call-update) | async-done | bytes 131088 | tf_op jit(solution)/shard_map/reduce_scatter | solution.py:153
  490.3 77.8 %reduce-scatter.21.cloned.1.call-done = f32[32,1536]{1,0:T(8,128)} async-done(((f32[512,1536]{1,0:T(8,128)}), f32[32,1536]{1,0:T(8,128)}) %reduce-scatter.21.cloned.1.call-update) | async-done | bytes 196624 | tf_op jit(solution)/shard_map/reduce_scatter | solution.py:100
  571.5 23.1 %all_gather.74 = bf16[512,256]{1,0:T(8,128)(2,1)S(1)} all-gather(bf16[32,256]{1,0:T(8,128)(2,1)S(1)} %bitcast.420), channel_id=1, replica_groups=mesh['pp'=2,'fsdp'=16,'tp'=4] {'fsdp'}, dimensions={0}, use_global_device_ids=true | all-gather | bytes 278528 | tf_op jit(solution)/shard_map/all_gather | solution.py:164
  594.7 21.7 %all_gather.75 = bf16[512,256]{1,0:T(8,128)(2,1)S(1)} all-gather(bf16[32,256]{1,0:T(8,128)(2,1)S(1)} %bitcast.425), channel_id=1, replica_groups=mesh['pp'=2,'fsdp'=16,'tp'=4] {'fsdp'}, dimensions={0}, use_global_device_ids=true | all-gather | bytes 278528 | tf_op jit(solution)/shard_map/all_gather | solution.py:165
  616.4 1.3 fusion.105
  617.7 1.3 fusion.91
  619.0 3.6 fusion.1
  622.7 23.0 %reduce-scatter.27.cloned.1.call-done = f32[128,512]{1,0:T(8,128)} async-done(((f32[512,512]{1,0:T(8,128)}), f32[128,512]{1,0:T(8,128)}) %reduce-scatter.27.cloned.1.call-update) | async-done | bytes 262160 | tf_op jit(solution)/shard_map/reduce_scatter | solution.py:176
  646.8 40.5 %all-reduce.1 = (f32[128]{0:T(128)S(1)}, f32[128]{0:T(128)S(1)}) all-reduce(f32[128]{0:T(128)S(1)} %get-tuple-element.43, f32[128]{0:T(128)S(1)} %get-tuple-element.42), channel_id=1, replica_groups=mesh['pp'=2,'fsdp'=16,'tp'=4] {'fsdp'}, use_global_device_ids=true, to_apply=%region_32.33 | all-reduce | flops 256 | bytes 2048 | tf_op jit(solution)/shard_map/psum | solution.py:94
  690.2 1.9 collective-permute-done.2
  692.2 13.4 all_gather.76
  706.4 3.3 fusion.46
  709.8 12.9 all_gather.73
  724.1 2.0 pad_maximum_fusion.3
  727.3 51.5 %reduce-scatter.29.cloned.1.call-done = f32[32,1024]{1,0:T(8,128)} async-done(((f32[512,1024]{1,0:T(8,128)}), f32[32,1024]{1,0:T(8,128)}) %reduce-scatter.29.cloned.1.call-update) | async-done | bytes 131088 | tf_op jit(solution)/shard_map/reduce_scatter | solution.py:153
  779.8 77.6 %reduce-scatter.25.cloned.1.call-done = f32[32,1536]{1,0:T(8,128)} async-done(((f32[512,1536]{1,0:T(8,128)}), f32[32,1536]{1,0:T(8,128)}) %reduce-scatter.25.cloned.1.call-update) | async-done | bytes 196624 | tf_op jit(solution)/shard_map/reduce_scatter | solution.py:100
  866.7 23.1 %all_gather.79 = bf16[512,256]{1,0:T(8,128)(2,1)S(1)} all-gather(bf16[32,256]{1,0:T(8,128)(2,1)S(1)} %bitcast.421), channel_id=1, replica_groups=mesh['pp'=2,'fsdp'=16,'tp'=4] {'fsdp'}, dimensions={0}, use_global_device_ids=true | all-gather | bytes 278528 | tf_op jit(solution)/shard_map/all_gather | solution.py:164
  889.7 21.7 %all_gather.80 = bf16[512,256]{1,0:T(8,128)(2,1)S(1)} all-gather(bf16[32,256]{1,0:T(8,128)(2,1)S(1)} %bitcast.426), channel_id=1, replica_groups=mesh['pp'=2,'fsdp'=16,'tp'=4] {'fsdp'}, dimensions={0}, use_global_device_ids=true | all-gather | bytes 278528 | tf_op jit(solution)/shard_map/all_gather | solution.py:165
  911.4 1.3 fusion.101
  912.7 1.3 fusion.87
  914.0 3.6 fusion
  917.7 23.0 %reduce-scatter.33.cloned.1.call-done = f32[128,512]{1,0:T(8,128)} async-done(((f32[512,512]{1,0:T(8,128)}), f32[128,512]{1,0:T(8,128)}) %reduce-scatter.33.cloned.1.call-update) | async-done | bytes 262160 | tf_op jit(solution)/shard_map/reduce_scatter | solution.py:176
  941.7 40.9 %all-reduce = (f32[128]{0:T(128)}, f32[128]{0:T(128)}) all-reduce(f32[128]{0:T(128)S(1)} %get-tuple-element.41, f32[128]{0:T(128)S(1)} %get-tuple-element.40), channel_id=1, replica_groups=mesh['pp'=2,'fsdp'=16,'tp'=4] {'fsdp'}, use_global_device_ids=true, to_apply=%region_42.43 | all-reduce | flops 256 | bytes 2048 | tf_op jit(solution)/shard_map/psum | solution.py:94
  984.0 1.8 fusion.86
  987.1 1.9 collective-permute-done.3
  989.0 13.4 %all_gather.81 = bf16[512,512]{1,0:T(8,128)(2,1)S(1)} all-gather(bf16[128,512]{1,0:T(8,128)(2,1)S(1)} %bitcast_select_fusion), channel_id=1, replica_groups=mesh['pp'=2,'fsdp'=16,'tp'=4] {'tp'}, dimensions={0}, use_global_device_ids=true | all-gather | bytes 655360 | tf_op jit(solution)/shard_map/all_gather | solution.py:149
  1003.3 2.1 fusion.44
  1005.4 13.0 all_gather.78
  1019.7 2.0 pad_maximum_fusion.4
  1024.5 49.9 %reduce-scatter.35.cloned.1.call-done = f32[32,1024]{1,0:T(8,128)} async-done(((f32[512,1024]{1,0:T(8,128)}), f32[32,1024]{1,0:T(8,128)}) %reduce-scatter.35.cloned.1.call-update) | async-done | bytes 131088 | tf_op jit(solution)/shard_map/reduce_scatter | solution.py:153
  1075.4 77.4 %reduce-scatter.31.cloned.1.call-done = f32[32,1536]{1,0:T(8,128)} async-done(((f32[512,1536]{1,0:T(8,128)}), f32[32,1536]{1,0:T(8,128)}) %reduce-scatter.31.cloned.1.call-update) | async-done | bytes 196624 | tf_op jit(solution)/shard_map/reduce_scatter | solution.py:100
  1156.5 2.2 convolution_select_fusion.2
  1159.8 2.1 fusion.193
  1161.9 35.7 %all-gather.20.cloned.1.call-done = bf16[512,1024]{1,0:T(8,128)(2,1)} async-done(((bf16[32,1024]{1,0:T(8,128)(2,1)}), bf16[512,1024]{1,0:T(8,128)(2,1)}) %all-gather.20.cloned.1.call-update) | async-done | bytes 1048592 | tf_op jit(solution)/shard_map/all_gather | solution.py:121
  1197.6 3.3 fusion.66
  1204.2 3.3 fusion.194
  1207.5 34.1 %all-gather.22.cloned.1.call-done = bf16[512,1024]{1,0:T(8,128)(2,1)} async-done(((bf16[32,1024]{1,0:T(8,128)(2,1)}), bf16[512,1024]{1,0:T(8,128)(2,1)}) %all-gather.22.cloned.1.call-update) | async-done | bytes 1048592 | tf_op jit(solution)/shard_map/all_gather | solution.py:121
  1241.7 3.3 fusion.195
  1245.8 23.2 %all_gather.84 = bf16[512,256]{1,0:T(8,128)(2,1)S(1)} all-gather(bf16[32,256]{1,0:T(8,128)(2,1)S(1)} %bitcast.422), channel_id=1, replica_groups=mesh['pp'=2,'fsdp'=16,'tp'=4] {'fsdp'}, dimensions={0}, use_global_device_ids=true | all-gather | bytes 278528 | tf_op jit(solution)/shard_map/all_gather | solution.py:165
  1269.0 21.9 %all_gather.83 = bf16[512,256]{1,0:T(8,128)(2,1)S(1)} all-gather(bf16[32,256]{1,0:T(8,128)(2,1)S(1)} %bitcast.427), channel_id=1, replica_groups=mesh['pp'=2,'fsdp'=16,'tp'=4] {'fsdp'}, dimensions={0}, use_global_device_ids=true | all-gather | bytes 278528 | tf_op jit(solution)/shard_map/all_gather | solution.py:164
  1293.2 4.0 add_bitcast_fusion
  1297.2 33.2 %all-gather.18.cloned.1.call-done = bf16[512,1024]{1,0:T(8,128)(2,1)} async-done(((bf16[32,1024]{1,0:T(8,128)(2,1)}), bf16[512,1024]{1,0:T(8,128)(2,1)}) %all-gather.18.cloned.1.call-update) | async-done | bytes 1048592 | tf_op jit(solution)/shard_map/all_gather | solution.py:163
  1330.4 4.0 add_bitcast_fusion.1
  (332 shorter events, 64.8 us)
Async XLA Ops:
  7.2 57.0 %copy-start = (bf16[1,512,1024]{2,1,0:T(8,128)(2,1)S(1)}, bf16[1,512,1024]{2,1,0:T(8,128)(2,1)}, u32[]{:S(2)}) copy-start(bf16[1,512,1024]{2,1,0:T(8,128)(2,1)} %param.22) | copy-start | bytes 3145732
  7.2 132.1 %reduce-scatter.13.cloned.1.call-start = ((), (), s32[]{:S(2)}) async-start(), calls=%async_computation.12 | async-start | bytes 3342336 | tf_op jit(solution)/shard_map/reduce_scatter | solution.py:100
  50.1 14.9 %copy-start.1 = (bf16[1,512,256]{2,1,0:T(8,128)(2,1)S(1)}, bf16[1,512,256]{2,1,0:T(8,128)(2,1)}, u32[]{:S(2)}) copy-start(bf16[1,512,256]{2,1,0:T(8,128)(2,1)} %param.23) | copy-start | bytes 786436
  67.5 116.4 %copy-start.3 = (bf16[1,1024,512]{2,1,0:T(8,128)(2,1)S(1)}, bf16[1,1024,512]{2,1,0:T(8,128)(2,1)}, u32[]{:S(2)}) copy-start(bf16[1,1024,512]{2,1,0:T(8,128)(2,1)} %param.25) | copy-start | bytes 3145732
  67.6 116.3 %all-gather.10.cloned.1.call-start = ((), (), s32[]{:S(2)}) async-start(), calls=%async_computation.13 | async-start | bytes 1114112 | tf_op jit(solution)/shard_map/all_gather | solution.py:121
  141.6 68.4 %copy-start.12 = (bf16[2,128,512]{2,1,0:T(8,128)(2,1)S(1)}, bf16[2,128,512]{2,1,0:T(8,128)(2,1)}, u32[]{:S(2)}) copy-start(bf16[2,128,512]{2,1,0:T(8,128)(2,1)} %param.16) | copy-start | bytes 786436
  141.6 68.4 %reduce-scatter.15.cloned.1.call-start = ((), (), s32[]{:S(2)}) async-start(), calls=%async_computation.14 | async-start | bytes 1310720 | tf_op jit(solution)/shard_map/reduce_scatter | solution.py:125
  186.8 153.6 %reduce-scatter.17.cloned.1.call-start = ((), (), s32[]{:S(2)}) async-start(), calls=%async_computation.15 | async-start | bytes 3342336 | tf_op jit(solution)/shard_map/reduce_scatter | solution.py:100
  211.0 2.3 collective-permute-start
  269.9 72.9 %copy-start.50 = (s32[2,16,2]{1,2,0:T(2,128)S(1)}, s32[2,16,2]{1,2,0:T(2,128)}, u32[]{:S(2)}) copy-start(s32[2,16,2]{1,2,0:T(2,128)} %param.21) | copy-start | bytes 772
  269.9 73.1 %copy-start.51 = (s32[2,16,2]{1,2,0:T(2,128)S(1)}, s32[2,16,2]{1,2,0:T(2,128)}, u32[]{:S(2)}) copy-start(s32[2,16,2]{1,2,0:T(2,128)} %param.20) | copy-start | bytes 772
  269.9 115.2 %all-gather.12.cloned.1.call-start = ((), (), s32[]{:S(2)}) async-start(), calls=%async_computation.16 | async-start | bytes 1114112 | tf_op jit(solution)/shard_map/all_gather | solution.py:121
  342.7 69.3 %reduce-scatter.19.cloned.1.call-start = ((), (), s32[]{:S(2)}) async-start(), calls=%async_computation.17 | async-start | bytes 1310720 | tf_op jit(solution)/shard_map/reduce_scatter | solution.py:125
  343.6 44.6 %copy-start.43 = (s32[2,16,2]{1,2,0:T(2,128)S(1)}, s32[2,16,2]{1,2,0:T(2,128)}, u32[]{:S(2)}) copy-start(s32[2,16,2]{1,2,0:T(2,128)} %param.19) | copy-start | bytes 772
  343.6 45.1 %copy-start.52 = (s32[2,128]{1,0:T(2,128)S(1)}, s32[2,128]{1,0:T(2,128)}, u32[]{:S(2)}) copy-start(s32[2,128]{1,0:T(2,128)} %param.18) | copy-start | bytes 3076
  343.6 45.1 %copy-start.32 = (bf16[2,128,512]{2,1,0:T(8,128)(2,1)S(1)}, bf16[2,128,512]{2,1,0:T(8,128)(2,1)}, u32[]{:S(2)}) copy-start(bf16[2,128,512]{2,1,0:T(8,128)(2,1)} %param.17) | copy-start | bytes 786436
  388.0 101.3 %reduce-scatter.23.cloned.1.call-start = ((), (), s32[]{:S(2)}) async-start(), calls=%async_computation.19 | async-start | bytes 2228224 | tf_op jit(solution)/shard_map/reduce_scatter | solution.py:153
  404.8 2.1 copy-start.5
  404.8 2.2 copy-start.53
  406.9 161.2 %reduce-scatter.21.cloned.1.call-start = ((), (), s32[]{:S(2)}) async-start(), calls=%async_computation.18 | async-start | bytes 3342336 | tf_op jit(solution)/shard_map/reduce_scatter | solution.py:100
  413.0 2.3 collective-permute-start.1
  472.4 96.8 %copy-start.40 = (pred[32,32]{0,1:T(8,128)(4,1)S(1)}, pred[32,32]{0,1:T(8,128)(4,1)}, u32[]{:S(2)}) copy-start(pred[32,32]{0,1:T(8,128)(4,1)} %get-tuple-element.100) | copy-start | bytes 3076
  472.4 146.6 %all-gather.14.cloned.1.call-start = ((), (), s32[]{:S(2)}) async-start(), calls=%async_computation.20 | async-start | bytes 1114112 | tf_op jit(solution)/shard_map/all_gather | solution.py:163
  569.1 48.6 %copy-start.36 = (bf16[32,2,128]{2,1,0:T(2,128)(2,1)}, bf16[32,2,128]{2,1,0:T(2,128)(2,1)S(1)}, u32[]{:S(2)}) copy-start(bf16[32,2,128]{2,1,0:T(2,128)(2,1)S(1)} %reshape.716) | copy-start | bytes 49156
  569.7 49.3 %copy-start.22 = (bf16[1,2,4,32,32]{3,4,2,1,0:T(8,128)(2,1)}, bf16[1,2,4,32,32]{3,4,2,1,0:T(8,128)(2,1)S(1)}, u32[]{:S(2)}) copy-start(bf16[1,2,4,32,32]{3,4,2,1,0:T(8,128)(2,1)S(1)} %get-tuple-element.65) | copy-start | bytes 49156
  570.7 75.0 %reduce-scatter.27.cloned.1.call-start = ((), (), s32[]{:S(2)}) async-start(), calls=%async_computation.22 | async-start | bytes 1310720 | tf_op jit(solution)/shard_map/reduce_scatter | solution.py:176
  594.7 23.1 %copy-start.19 = (bf16[512,256]{1,0:T(8,128)(2,1)}, bf16[512,256]{1,0:T(8,128)(2,1)S(1)}, u32[]{:S(2)}) copy-start(bf16[512,256]{1,0:T(8,128)(2,1)S(1)} %all_gather.74) | copy-start | bytes 786436
  619.0 68.8 %copy-start.14 = (bf16[2,128,512]{2,1,0:T(8,128)(2,1)S(1)}, bf16[2,128,512]{2,1,0:T(8,128)(2,1)}, u32[]{:S(2)}) copy-start(bf16[2,128,512]{2,1,0:T(8,128)(2,1)} %copy-done.13) | copy-start | bytes 786436
  622.7 156.2 %reduce-scatter.29.cloned.1.call-start = ((), (), s32[]{:S(2)}) async-start(), calls=%async_computation.23 | async-start | bytes 2228224 | tf_op jit(solution)/shard_map/reduce_scatter | solution.py:153
  687.3 4.9 copy-start.48
  688.9 3.2 collective-permute-start.2
  709.8 147.7 %reduce-scatter.25.cloned.1.call-start = ((), (), s32[]{:S(2)}) async-start(), calls=%async_computation.21 | async-start | bytes 3342336 | tf_op jit(solution)/shard_map/reduce_scatter | solution.py:100
  726.1 188.0 %all-gather.16.cloned.1.call-start = ((), (), s32[]{:S(2)}) async-start(), calls=%async_computation.24 | async-start | bytes 1114112 | tf_op jit(solution)/shard_map/all_gather | solution.py:163
  779.8 82.6 %copy-start.35 = (bf16[32,2,4,128]{3,2,1,0:T(4,128)(2,1)}, bf16[32,2,4,128]{3,2,1,0:T(4,128)(2,1)S(1)}, u32[]{:S(2)}) copy-start(bf16[32,2,4,128]{3,2,1,0:T(4,128)(2,1)S(1)} %reshape.723) | copy-start | bytes 196612
  862.5 4.1 copy-start.24
  864.1 76.5 %reduce-scatter.33.cloned.1.call-start = ((), (), s32[]{:S(2)}) async-start(), calls=%async_computation.26 | async-start | bytes 1310720 | tf_op jit(solution)/shard_map/reduce_scatter | solution.py:176
  914.0 69.3 %copy-start.55 = (f32[128]{0:T(128)S(1)}, f32[128]{0:T(128)}, u32[]{:S(2)}) copy-start(f32[128]{0:T(128)} %copy-done.54) | copy-start | bytes 1540
  914.0 70.0 %copy-start.49 = (f32[128]{0:T(128)S(1)}, f32[128]{0:T(128)}, u32[]{:S(2)}) copy-start(f32[128]{0:T(128)} %copy-done.48) | copy-start | bytes 1540
  917.6 156.8 %reduce-scatter.35.cloned.1.call-start = ((), (), s32[]{:S(2)}) async-start(), calls=%async_computation.27 | async-start | bytes 2228224 | tf_op jit(solution)/shard_map/reduce_scatter | solution.py:153
  982.6 20.7 %copy-start.4 = (bf16[1,1024,512]{2,1,0:T(8,128)(2,1)S(1)}, bf16[1,1024,512]{2,1,0:T(8,128)(2,1)}, u32[]{:S(2)}) copy-start(bf16[1,1024,512]{2,1,0:T(8,128)(2,1)} %param.25) | copy-start | bytes 3145732
  985.8 3.2 collective-permute-start.3
  1003.3 2.1 copy-start.29
  1005.4 147.5 %reduce-scatter.31.cloned.1.call-start = ((), (), s32[]{:S(2)}) async-start(), calls=%async_computation.25 | async-start | bytes 3342336 | tf_op jit(solution)/shard_map/reduce_scatter | solution.py:100
  1021.7 1.8 copy-start.25
  1021.7 1.8 copy-start.38
  1021.7 132.2 %copy-start.41 = (pred[32,32]{0,1:T(8,128)(4,1)S(1)}, pred[32,32]{0,1:T(8,128)(4,1)}, u32[]{:S(2)}) copy-start(pred[32,32]{0,1:T(8,128)(4,1)} %get-tuple-element.98) | copy-start | bytes 3076
  1021.7 175.8 %all-gather.20.cloned.1.call-start = ((), (), s32[]{:S(2)}) async-start(), calls=%async_computation.29 | async-start | bytes 1114112 | tf_op jit(solution)/shard_map/all_gather | solution.py:121
  1023.5 218.2 %all-gather.22.cloned.1.call-start = ((), (), s32[]{:S(2)}) async-start(), calls=%async_computation.30 | async-start | bytes 1114112 | tf_op jit(solution)/shard_map/all_gather | solution.py:121
  1024.5 268.7 %all-gather.24.cloned.1.call-start = ((), (), s32[]{:S(2)}) async-start(), calls=%async_computation.31 | async-start | bytes 1114112 | tf_op jit(solution)/shard_map/all_gather | solution.py:121
  1075.4 83.3 %copy-start.20 = (bf16[512,256]{1,0:T(8,128)(2,1)S(1)}, bf16[512,256]{1,0:T(8,128)(2,1)}, u32[]{:S(2)}) copy-start(bf16[512,256]{1,0:T(8,128)(2,1)} %copy-done.19) | copy-start | bytes 786436
  1075.4 79.0 %copy-start.33 = (bf16[32,2,4,128]{3,2,1,0:T(4,128)(2,1)}, bf16[32,2,4,128]{3,2,1,0:T(4,128)(2,1)S(1)}, u32[]{:S(2)}) copy-start(bf16[32,2,4,128]{3,2,1,0:T(4,128)(2,1)S(1)} %reshape.729) | copy-start | bytes 196612
  1154.5 4.2 copy-start.26
  1156.2 174.2 %all-gather.18.cloned.1.call-start = ((), (), s32[]{:S(2)}) async-start(), calls=%async_computation.28 | async-start | bytes 1114112 | tf_op jit(solution)/shard_map/all_gather | solution.py:163
  1156.5 3.3 copy-start.11
  1159.8 37.7 %copy-start.6 = (bf16[1,512,512]{2,1,0:T(8,128)(2,1)S(1)}, bf16[1,512,512]{2,1,0:T(8,128)(2,1)}, u32[]{:S(2)}) copy-start(bf16[1,512,512]{2,1,0:T(8,128)(2,1)} %copy-done.5) | copy-start | bytes 1572868
  1161.9 39.0 %copy-start.16 = (bf16[512,256]{1,0:T(8,128)(2,1)S(1)}, bf16[512,256]{1,0:T(8,128)(2,1)}, u32[]{:S(2)}) copy-start(bf16[512,256]{1,0:T(8,128)(2,1)} %copy-done.15) | copy-start | bytes 786436
  1197.6 3.3 copy-start.31
  1200.9 2.1 copy-start.30
  1204.2 37.5 %copy-start.8 = (bf16[512,512]{1,0:T(8,128)(2,1)S(1)}, bf16[512,512]{1,0:T(8,128)(2,1)}, u32[]{:S(2)}) copy-start(bf16[512,512]{1,0:T(8,128)(2,1)} %copy-done.7) | copy-start | bytes 1572868
  1207.5 37.4 %copy-start.27 = (bf16[1,2,4,32,32]{3,4,2,1,0:T(8,128)(2,1)S(1)}, bf16[1,2,4,32,32]{3,4,2,1,0:T(8,128)(2,1)}, u32[]{:S(2)}) copy-start(bf16[1,2,4,32,32]{3,4,2,1,0:T(8,128)(2,1)} %copy-done.26) | copy-start | bytes 49156
  1207.5 37.4 %copy-start.34 = (bf16[32,2,4,128]{3,2,1,0:T(4,128)(2,1)S(1)}, bf16[32,2,4,128]{3,2,1,0:T(4,128)(2,1)}, u32[]{:S(2)}) copy-start(bf16[32,2,4,128]{3,2,1,0:T(4,128)(2,1)} %copy-done.33) | copy-start | bytes 196612
  1207.5 83.4 %copy-start.17 = (f32[512,256]{1,0:T(8,128)S(1)}, f32[512,256]{1,0:T(8,128)}, u32[]{:S(2)}) copy-start(f32[512,256]{1,0:T(8,128)} %fusion.4) | copy-start | bytes 1572868
  1245.0 47.1 %copy-start.18 = (f32[512,256]{1,0:T(8,128)S(1)}, f32[512,256]{1,0:T(8,128)}, u32[]{:S(2)}) copy-start(f32[512,256]{1,0:T(8,128)} %fusion.7) | copy-start | bytes 1572868
  1245.8 47.4 %copy-start.10 = (bf16[512,512]{1,0:T(8,128)(2,1)S(1)}, bf16[512,512]{1,0:T(8,128)(2,1)}, u32[]{:S(2)}) copy-start(bf16[512,512]{1,0:T(8,128)(2,1)} %copy-done.9) | copy-start | bytes 1572868
  (16 other events, 12.7 us)
Sparse Core Ops, SparseCore 0:
  67.7 71.5 reduce-scatter.12
  142.0 41.8 all-gather.9
  187.0 23.0 reduce-scatter.14
  270.0 70.3 reduce-scatter.16
  343.2 41.8 all-gather.11
  388.1 23.8 reduce-scatter.18
  415.8 73.4 reduce-scatter.22
  493.0 75.0 reduce-scatter.20
  571.0 41.8 all-gather.13
  622.8 22.8 reduce-scatter.26
  709.9 68.9 reduce-scatter.28
  782.4 74.9 reduce-scatter.24
  864.2 41.8 all-gather.15
  917.8 22.8 reduce-scatter.32
  1005.5 68.9 reduce-scatter.34
  1078.0 74.8 reduce-scatter.30
  1155.7 41.8 all-gather.19
  1199.8 41.8 all-gather.21
  1244.0 42.1 all-gather.23
  1288.4 41.9 all-gather.17
where the time goes:
time: 1340 us
  waiting for transfers between devices  756 us (56%)
  blocking collectives  445 us (33%)
  matrix products  69.6 us (5%)
  other arithmetic  33.8 us (3%)
  local copies, waits for them, and re-layouts  15.7 us (1%)
  between operations  15.5 us (1%)
    reduce_scatter x5, waiting for transfers between devices, front(): lax.psum_scatter(jnp.concatenate([jnp.dot(normed_all, query_layer, prefer...  373 us
    psum x5, blocking collectives, front(): squares = lax.psum(jnp.sum(stream_float * stream_float, -1), 'fsdp')  203 us
    all_gather x5, waiting for transfers between devices, spread(): return lax.all_gather(head_out, 'fsdp', axis=0, tiled=True)  154 us
    reduce_scatter x3, waiting for transfers between devices, back(): lax.psum_scatter(jnp.einsum('td,qd->tq', grad_all, out_layer, preferred_e...  118 us
    all_gather x3, blocking collectives, back(): lax.all_gather(key_grad[0], 'fsdp', axis=0, tiled=True)  68.1 us
    all_gather x3, blocking collectives, back(): lax.all_gather(value_grad[0], 'fsdp', axis=0, tiled=True)  66.7 us
    all_gather x5, blocking collectives, front(): normed_all = lax.all_gather(normed, 'tp', axis=0, tiled=True)  65.6 us
    reduce_scatter x2, waiting for transfers between devices, back(): lax.psum_scatter(jnp.einsum('tq,mq->tm', query_all, query_layer, preferre...  45.9 us
  transfers between devices with their start and end apart: 24, of which 21 were waited for; matrix products, arithmetic and copies ran while one was open for 5% of the time, Pallas kernels for 0%

commit v1 on v0

v1 whole, which is shorter than its diff:
```python
import jax
import jax.numpy as jnp
from jax import lax
from jax.sharding import PartitionSpec as P

MODEL_WIDTH = 8192
HEAD_WIDTH = 128
SLOT = 32

epsilon = 1e-06
masked_score = -1e30


def segments(lengths):
    ends = jnp.stack([jnp.sum(lengths[..., : c + 1], -1) for c in range(lengths.shape[-1])], -1)
    position = jnp.arange(SLOT, dtype=jnp.int32)
    return jnp.sum((ends[..., None, :] <= position[:, None]).astype(jnp.int32), -1)


def token_weights(lengths, rewards, groups):
    group_total = 2 * lengths.shape[1]
    reward_flat = rewards.reshape(-1).astype(jnp.float32)
    member = (
        groups.reshape(-1)[:, None] == jnp.arange(group_total, dtype=jnp.int32)[None, :]
    ).astype(jnp.float32)
    member_count = jnp.sum(member, 0)
    group_mean = jnp.sum(member * reward_flat[:, None], 0) / member_count
    centered = reward_flat - jnp.sum(member * group_mean[None, :], 1)
    variance = jnp.sum(member * (centered * centered)[:, None], 0) / member_count
    spread_own = jnp.sum(member * jnp.sqrt(variance)[None, :], 1)
    advantage = (centered / jnp.maximum(spread_own, 1.0)).reshape(lengths.shape)
    segment = segments(lengths)
    choose = (segment[..., None] == jnp.arange(lengths.shape[2], dtype=jnp.int32)).astype(
        jnp.float32
    )
    token_adv = jnp.sum(choose * advantage[:, :, None, :], -1)
    token_len = jnp.sum(choose * lengths[:, :, None, :].astype(jnp.float32), -1)
    return (token_adv * SLOT / token_len).reshape(lengths.shape[0], -1)


def heads_of(rows):
    return rows.reshape(rows.shape[0], -1, HEAD_WIDTH).astype(jnp.float32)


def attend(query_rows, key_rows, value_rows, same_doc):
    keys, values = heads_of(key_rows), heads_of(value_rows)
    count = keys.shape[1]
    queries = heads_of(query_rows).reshape(SLOT, count, -1, HEAD_WIDTH)
    scores = jnp.einsum("ikgd,jkd->kgij", queries, keys) * HEAD_WIDTH**-0.5
    probs = jax.nn.softmax(jnp.where(same_doc, scores, masked_score), axis=-1)
    mixture = jnp.einsum(
        "kgij,jkd->ikgd", probs.astype(jnp.bfloat16).astype(jnp.float32), values
    )
    return mixture.reshape(SLOT, -1).astype(jnp.bfloat16), probs


def attend_back(query_rows, key_rows, value_rows, probs, head_out_grad):
    keys, values = heads_of(key_rows), heads_of(value_rows)
    count = keys.shape[1]
    queries = heads_of(query_rows).reshape(SLOT, count, -1, HEAD_WIDTH)
    grads = heads_of(head_out_grad).reshape(queries.shape)
    rounded = probs.astype(jnp.bfloat16).astype(jnp.float32)
    prob_grad = jnp.einsum("ikgd,jkd->kgij", grads, values)
    value_grad = jnp.einsum("kgij,ikgd->jkd", rounded, grads)
    score_grad = probs * (prob_grad - jnp.sum(prob_grad * probs, -1, keepdims=True))
    score_grad = score_grad.astype(jnp.bfloat16).astype(jnp.float32)
    scale = HEAD_WIDTH**-0.5
    query_grad = jnp.einsum("kgij,jkd->ikgd", score_grad, keys) * scale
    key_grad = jnp.einsum("kgij,ikgd->jkd", score_grad, queries) * scale
    return jnp.concatenate(
        [v.reshape(SLOT, -1).astype(jnp.bfloat16) for v in (query_grad, key_grad, value_grad)], 1
    )


def dot(a, b, contract):
    return lax.dot_general(a, b, (contract, ((), ())), preferred_element_type=jnp.float32)


def scatter(value, axis):
    return lax.psum_scatter(value, axis, scatter_dimension=0, tiled=True)


def gather(value, axis):
    return lax.all_gather(value, axis, axis=0, tiled=True)


def local(
    inputs,
    head_grad,
    noise_mask,
    lengths,
    rewards,
    groups,
    query_weight,
    key_weight,
    value_weight,
    out_weight,
):
    core = lax.axis_index("pp")
    row_count = inputs.shape[1]
    query_cols, key_cols = query_weight.shape[2], key_weight.shape[2]
    cols = query_cols + 2 * key_cols
    own_qkv = jnp.concatenate([query_weight[0], key_weight[0], value_weight[0]], 1)
    own_out = out_weight[0]
    swap = [(0, 1), (1, 0)]
    far_qkv, far_out = lax.ppermute(own_qkv, "pp", swap), lax.ppermute(own_out, "pp", swap)
    qkv = [jnp.where(core == 0, own_qkv, far_qkv), jnp.where(core == 0, far_qkv, own_qkv)]
    out = [jnp.where(core == 0, own_out, far_out), jnp.where(core == 0, far_out, own_out)]

    segment = segments(lengths)[core, lax.axis_index("fsdp")]
    same_doc = segment[:, None] == segment[None, :]
    weight = lax.dynamic_slice_in_dim(
        token_weights(lengths, rewards, groups)[core], lax.axis_index("tp") * row_count, row_count, 0
    ) * noise_mask[core].astype(jnp.float32)
    top_grad = (-weight[:, None] * head_grad[core].astype(jnp.float32)).astype(jnp.bfloat16)

    def project(stream_all, layer):
        wide = stream_all.astype(jnp.float32)
        squares = jnp.sum(wide * wide, -1, keepdims=True)
        partial = jnp.concatenate(
            [
                dot(stream_all, qkv[layer], ((1,), (0,))),
                jnp.broadcast_to(squares, (squares.shape[0], 128)),
            ],
            1,
        )
        summed = scatter(partial, "fsdp")
        inv_rms = lax.rsqrt(summed[:, cols : cols + 1] / MODEL_WIDTH + epsilon)
        rows = (summed[:, :cols] * inv_rms).astype(jnp.bfloat16)
        return (
            inv_rms,
            rows[:, :query_cols],
            rows[:, query_cols : query_cols + key_cols],
            rows[:, query_cols + key_cols :],
        )

    def head_grads(grad_all, layer):
        return scatter(dot(grad_all, out[layer], ((1,), (1,))), "fsdp").astype(jnp.bfloat16)

    stream0 = inputs[core]
    stream0_all = gather(stream0, "tp")
    grad1_all = gather(top_grad, "tp")
    inv0, q0, k0, v0 = project(stream0_all, 0)
    head_grad1 = head_grads(grad1_all, 1)
    head0, probs0 = attend(q0, k0, v0, same_doc)
    heads0_all = gather(head0, "fsdp")
    stream1 = (
        stream0.astype(jnp.float32) + scatter(dot(heads0_all, out[0], ((1,), (0,))), "tp")
    ).astype(jnp.bfloat16)
    stream1_all = gather(stream1, "tp")
    inv1, q1, k1, v1 = project(stream1_all, 1)
    head1, probs1 = attend(q1, k1, v1, same_doc)
    heads1_all = gather(head1, "fsdp")
    grads1 = attend_back(q1, k1, v1, probs1, head_grad1).astype(jnp.float32)
    rows1 = jnp.concatenate([q1, k1, v1], 1).astype(jnp.float32)
    share = inv1 * jnp.sum(grads1 * rows1, -1, keepdims=True) * inv1 / MODEL_WIDTH
    scaled1 = (grads1 * inv1).astype(jnp.bfloat16)
    scaled1_all = gather(scaled1, "fsdp")
    share_all = gather(jnp.broadcast_to(share, (SLOT, 128)), "fsdp")[:, :1]
    part = dot(scaled1_all, qkv[1], ((1,), (1,))) - stream1_all.astype(jnp.float32) * share_all
    grad0 = (top_grad.astype(jnp.float32) + scatter(part, "tp")).astype(jnp.bfloat16)
    grad0_all = gather(grad0, "tp")
    head_grad0 = head_grads(grad0_all, 0)
    grads0 = attend_back(q0, k0, v0, probs0, head_grad0).astype(jnp.float32)
    scaled0_all = gather((grads0 * inv0).astype(jnp.bfloat16), "fsdp")

    def both(first, second):
        own = jnp.where(core == 0, first, second)
        other = lax.ppermute(jnp.where(core == 0, second, first), "pp", swap)
        return jnp.concatenate([own, other], 0)

    streams = both(stream0_all, stream1_all)
    heads = both(heads0_all, heads1_all)
    out_grads = both(grad0_all, grad1_all)
    scaled = both(scaled0_all, scaled1_all)
    qkv_grad = dot(streams, scaled, ((0,), (0,)))
    return (
        qkv_grad[None, :, :query_cols],
        qkv_grad[None, :, query_cols : query_cols + key_cols],
        qkv_grad[None, :, query_cols + key_cols :],
        dot(heads, out_grads, ((0,), (0,)))[None],
    )


def solution(mesh):
    return jax.shard_map(
        local,
        mesh=mesh,
        in_specs=(
            P(None, "tp", "fsdp"),
            P(None, "tp", "fsdp"),
            P(None, "tp"),
            P(),
            P(),
            P(),
            P("pp", "fsdp", "tp"),
            P("pp", "fsdp", "tp"),
            P("pp", "fsdp", "tp"),
            P("pp", "tp", "fsdp"),
        ),
        out_specs=(
            P("pp", "fsdp", "tp"),
            P("pp", "fsdp", "tp"),
            P("pp", "fsdp", "tp"),
            P("pp", "tp", "fsdp"),
        ),
        check_vma=False,
    )
```

time: 1340 us -> 621 us (0.46)
  blocking collectives: 445 us -> 93.9 us
  waiting for transfers between devices: 756 us -> 444 us
  matrix products: 69.6 us -> 28.9 us
    reduce_scatter x12 -> x6, waiting for transfers between devices: 563 us -> 315 us  [scatter(): return lax.psum_scatter(value, axis, scatter_dimension=0, tiled=True)]
    psum x5 -> x0, blocking collectives: 203 us -> none  [front(): squares = lax.psum(jnp.sum(stream_float * stream_float, -1), 'fsdp')]
    all_gather x14 -> x4, blocking collectives: 242 us -> 55.8 us  [gather(): return lax.all_gather(value, axis, axis=0, tiled=True)]
    all_gather x8 -> x4, waiting for transfers between devices: 187 us -> 125 us  [gather(): return lax.all_gather(value, axis, axis=0, tiled=True)]
    dot_general x60 -> x18, matrix products: 69.6 us -> 27.1 us  [the longest x8 21.8 us: dot(): lax.dot_general(a, b, (contract, ((), ())), preferred_element_type=jnp.fl...]
    unnamed x0 -> x1, blocking collectives: none -> 38.1 us
  transfers between devices with their start and end apart: 24 -> 16, of which waited for: 21 -> 13; matrix products, arithmetic and copies ran while one was open for 5% -> 4% of each run, Pallas kernels for 0% -> 0%
where the time goes in v1:
time: 621 us; the launch traced here: 619 us
  waiting for transfers between devices  444 us (71%)
  blocking collectives  93.9 us (15%)
  matrix products  28.9 us (5%)
  other arithmetic  23.2 us (4%)
  between operations  15.5 us (2%)
  local copies, waits for them, and re-layouts  11.8 us (2%)
    reduce_scatter x6, waiting for transfers between devices, scatter(): return lax.psum_scatter(value, axis, scatter_dimension=0, tiled=True)  315 us
    all_gather x4, waiting for transfers between devices, gather(): return lax.all_gather(value, axis, axis=0, tiled=True)  125 us
    all_gather x4, blocking collectives, gather(): return lax.all_gather(value, axis, axis=0, tiled=True)  55.8 us
    unnamed x1, blocking collectives  38.1 us
    dot_general x8, matrix products, dot(): lax.dot_general(a, b, (contract, ((), ())), preferred_element_type=jnp.fl...  21.8 us
  transfers between devices with their start and end apart: 16, of which 13 were waited for; matrix products, arithmetic and copies ran while one was open for 4% of the time, Pallas kernels for 0%

profile of v1, /device:TPU:0, one launch (start us, length us, event | category | flops | bytes accessed | tf_op | source)
XLA Modules:
  0.0 619.1 jit_solution(6315300125879777344)
XLA Ops:
  7.2 1.6 pad_maximum_fusion.2
  9.0 14.3 %all-gather = bf16[1,512,512]{2,1,0:T(8,128)(2,1)S(1)} all-gather(bf16[1,128,512]{2,1,0:T(8,128)(2,1)S(1)} %constant_dynamic-slice_fusion.2), channel_id=3, replica_groups=mesh['pp'=2,'fsdp'=16,'tp'=4] {'tp'}, dimensions={1}, use_global_device_ids=true | all-gather | bytes 655360 | tf_op jit(solution)/shard_map/all_gather | solution.py:84
  23.5 2.0 fusion.13
  25.6 2.0 pad_maximum_fusion
  27.6 0.6 copy-done.21
  28.5 77.1 %reduce-scatter.7.cloned.1.call-done = f32[32,1664]{1,0:T(8,128)} async-done(((f32[512,1664]{1,0:T(8,128)}), f32[32,1664]{1,0:T(8,128)}) %reduce-scatter.7.cloned.1.call-update) | async-done | bytes 213008 | tf_op jit(solution)/shard_map/reduce_scatter | solution.py:80
  105.6 0.8 fusion.78
  106.4 1.0 fusion.59
  107.5 0.3 fusion.123
  107.8 0.6 copy-done.11
  108.7 0.7 convert_element_type.203
  110.3 1.8 collective-permute-done.1
  112.2 39.2 %all-gather.7.cloned.1.call-done = bf16[512,1024]{1,0:T(8,128)(2,1)} async-done(((bf16[32,1024]{1,0:T(8,128)(2,1)}), bf16[512,1024]{1,0:T(8,128)(2,1)}) %all-gather.7.cloned.1.call-update) | async-done | bytes 1048592 | tf_op jit(solution)/shard_map/all_gather | solution.py:84
  151.4 2.9 fusion.53
  155.2 15.4 %all_gather.30 = bf16[512,512]{1,0:T(8,128)(2,1)S(1)} all-gather(bf16[128,512]{1,0:T(8,128)(2,1)S(1)} %fusion.54), channel_id=1, replica_groups=mesh['pp'=2,'fsdp'=16,'tp'=4] {'tp'}, dimensions={0}, use_global_device_ids=true | all-gather | bytes 655360 | tf_op jit(solution)/shard_map/all_gather | solution.py:84
  170.6 2.1 fusion.47
  172.8 5.0 reduce-scatter.9.cloned.1.call-done
  177.8 1.0 fusion.55
  178.8 13.3 %all_gather.29 = bf16[512,512]{1,0:T(8,128)(2,1)S(1)} all-gather(bf16[128,512]{1,0:T(8,128)(2,1)S(1)} %fusion.55), channel_id=1, replica_groups=mesh['pp'=2,'fsdp'=16,'tp'=4] {'tp'}, dimensions={0}, use_global_device_ids=true | all-gather | bytes 655360 | tf_op jit(solution)/shard_map/all_gather | solution.py:84
  192.3 2.7 fusion.50
  195.2 2.0 pad_maximum_fusion.1
  197.2 58.7 %reduce-scatter.13.cloned.1.call-done = f32[32,1024]{1,0:T(8,128)} async-done(((f32[512,1024]{1,0:T(8,128)}), f32[32,1024]{1,0:T(8,128)}) %reduce-scatter.13.cloned.1.call-update) | async-done | bytes 131088 | tf_op jit(solution)/shard_map/reduce_scatter | solution.py:80
  255.9 0.9 convert_element_type.216
  256.8 0.7 reshape.148
  257.5 77.0 %reduce-scatter.11.cloned.1.call-done = f32[32,1664]{1,0:T(8,128)} async-done(((f32[512,1664]{1,0:T(8,128)}), f32[32,1664]{1,0:T(8,128)}) %reduce-scatter.11.cloned.1.call-update) | async-done | bytes 213008 | tf_op jit(solution)/shard_map/reduce_scatter | solution.py:80
  334.5 0.9 fusion.87
  335.4 1.0 fusion.58
  336.4 0.6 slice.70
  337.0 0.9 reshape.146
  338.0 1.6 fusion.128
  339.5 1.2 multiply_reduce_fusion.2
  340.7 0.9 multiply_convert_fusion.2
  341.9 0.4 fusion.39
  342.2 1.9 fusion.38
  344.2 0.7 convert_element_type.220
  344.8 0.7 copy.219
  345.6 1.7 fusion.57
  347.4 1.2 dynamic-slice.1
  349.5 0.2 dynamic-update-slice
  349.7 38.1 %all-reduce = f32[512]{0:T(512)S(1)} all-reduce(f32[512]{0:T(512)S(1)} %dynamic-update-slice), channel_id=4, replica_groups=mesh['pp'=2,'fsdp'=16,'tp'=4] {'fsdp'}, use_global_device_ids=true, to_apply=%add | all-reduce | flops 512 | bytes 4096
  387.8 2.7 all-gather.9.cloned.1.call-done
  390.5 4.2 convolution_subtract_fusion
  394.8 23.2 %reduce-scatter.15.cloned.1.call-done = f32[128,512]{1,0:T(8,128)} async-done(((f32[512,512]{1,0:T(8,128)}), f32[128,512]{1,0:T(8,128)}) %reduce-scatter.15.cloned.1.call-update) | async-done | bytes 262160 | tf_op jit(solution)/shard_map/reduce_scatter | solution.py:80
  418.0 1.1 add_convert_fusion
  419.1 12.8 %all_gather.33 = bf16[512,512]{1,0:T(8,128)(2,1)S(1)} all-gather(bf16[128,512]{1,0:T(8,128)(2,1)S(1)} %add_convert_fusion), channel_id=1, replica_groups=mesh['pp'=2,'fsdp'=16,'tp'=4] {'tp'}, dimensions={0}, use_global_device_ids=true | all-gather | bytes 655360 | tf_op jit(solution)/shard_map/all_gather | solution.py:84
  431.9 2.1 fusion.52
  434.1 73.9 %reduce-scatter.17.cloned.1.call-done = f32[32,1024]{1,0:T(8,128)} async-done(((f32[512,1024]{1,0:T(8,128)}), f32[32,1024]{1,0:T(8,128)}) %reduce-scatter.17.cloned.1.call-update) | async-done | bytes 131088 | tf_op jit(solution)/shard_map/reduce_scatter | solution.py:80
  508.0 0.9 convert_element_type.232
  509.5 0.4 fusion.37
  509.9 0.4 fusion.36
  510.3 0.7 multiply_convert_fusion
  511.4 0.7 convert_element_type.247
  512.1 42.3 %all-gather.11.cloned.1.call-done = bf16[512,1536]{1,0:T(8,128)(2,1)} async-done(((bf16[32,1536]{1,0:T(8,128)(2,1)}), bf16[512,1536]{1,0:T(8,128)(2,1)}) %all-gather.11.cloned.1.call-update) | async-done | bytes 1572880 | tf_op jit(solution)/shard_map/all_gather | solution.py:84
  554.4 3.8 broadcast_select_fusion.1
  558.1 40.8 %all-gather.13.cloned.1.call-done = bf16[512,1024]{1,0:T(8,128)(2,1)} async-done(((bf16[32,1024]{1,0:T(8,128)(2,1)}), bf16[512,1024]{1,0:T(8,128)(2,1)}) %all-gather.13.cloned.1.call-update) | async-done | bytes 1048592 | tf_op jit(solution)/shard_map/all_gather | solution.py:84
  598.9 1.4 broadcast_select_fusion.4
  600.5 0.6 collective-permute-start.5
  601.1 0.3 collective-permute-start.2
  601.4 1.6 collective-permute-done.4
  603.1 0.7 collective-permute-done.5
  603.8 2.6 fusion.10
  606.4 3.3 fusion.2
  609.7 1.5 slice_bitcast_fusion
  611.2 1.0 slice_bitcast_fusion.1
  (151 shorter events, 5.1 us)
Async XLA Ops:
  7.2 1.8 copy-start.8
  7.2 98.4 %reduce-scatter.7.cloned.1.call-start = ((), (), s32[]{:S(2)}) async-start(), calls=%async_computation.6 | async-start | bytes 3620864 | tf_op jit(solution)/shard_map/reduce_scatter | solution.py:80
  7.2 16.2 %copy-start.3 = (bf16[1,512,1024]{2,1,0:T(8,128)(2,1)S(1)}, bf16[1,512,1024]{2,1,0:T(8,128)(2,1)}, u32[]{:S(2)}) copy-start(bf16[1,512,1024]{2,1,0:T(8,128)(2,1)} %param.16) | copy-start | bytes 3145732
  7.2 16.2 %copy-start.6 = (bf16[1,512,256]{2,1,0:T(8,128)(2,1)S(1)}, bf16[1,512,256]{2,1,0:T(8,128)(2,1)}, u32[]{:S(2)}) copy-start(bf16[1,512,256]{2,1,0:T(8,128)(2,1)} %param.18) | copy-start | bytes 786436
  8.8 14.6 %collective-permute-start = (bf16[512,1536]{1,0:T(8,128)(2,1)S(1)}, bf16[512,1536]{1,0:T(8,128)(2,1)}, u32[]{:S(2)}, u32[]{:S(2)}) collective-permute-start(bf16[512,1536]{1,0:T(8,128)(2,1)S(1)} %pad_maximum_fusion.2), channel_id=1, source_target_pairs={{0,64},{64,0},{1,65},{65,1},{2,66},{66,2},{3,67},{67,3},{4,68},{68... | collective-permute-start | bytes 4718600 | tf_op jit(solution)/shard_map/ppermute | solution.py:106
  27.5 0.7 copy-start.21
  27.5 0.8 slice-start
  27.5 81.9 %copy-start = (bf16[1,1024,512]{2,1,0:T(8,128)(2,1)S(1)}, bf16[1,1024,512]{2,1,0:T(8,128)(2,1)}, u32[]{:S(2)}) copy-start(bf16[1,1024,512]{2,1,0:T(8,128)(2,1)} %param.19) | copy-start | bytes 3145732
  27.5 82.0 %copy-start.29 = (s32[2,16,2]{1,2,0:T(2,128)S(1)}, s32[2,16,2]{1,2,0:T(2,128)}, u32[]{:S(2)}) copy-start(s32[2,16,2]{1,2,0:T(2,128)} %param.15) | copy-start | bytes 772
  27.6 82.2 %copy-start.30 = (s32[2,16,2]{1,2,0:T(2,128)S(1)}, s32[2,16,2]{1,2,0:T(2,128)}, u32[]{:S(2)}) copy-start(s32[2,16,2]{1,2,0:T(2,128)} %param.14) | copy-start | bytes 772
  27.6 123.8 %all-gather.7.cloned.1.call-start = ((), (), s32[]{:S(2)}) async-start(), calls=%async_computation.7 | async-start | bytes 1114112 | tf_op jit(solution)/shard_map/all_gather | solution.py:84
  28.5 79.3 %copy-start.28 = (pred[32,32]{0,1:T(8,128)(4,1)}, pred[32,32]{0,1:T(8,128)(4,1)S(1)}, u32[]{:S(2)}) copy-start(pred[32,32]{0,1:T(8,128)(4,1)S(1)} %broadcast_compare_fusion) | copy-start | bytes 3076
  106.4 47.9 %copy-start.18 = (f32[32]{0:T(128)}, f32[32]{0:T(128)S(1)}, u32[]{:S(2)}) copy-start(f32[32]{0:T(128)S(1)} %fusion.78) | copy-start | bytes 388
  107.5 2.8 copy-start.14
  107.8 0.7 copy-start.11
  107.8 2.5 copy-start.24
  109.4 68.4 %reduce-scatter.9.cloned.1.call-start = ((), (), s32[]{:S(2)}) async-start(), calls=%async_computation.8 | async-start | bytes 1310720 | tf_op jit(solution)/shard_map/reduce_scatter | solution.py:80
  109.4 2.7 collective-permute-start.1
  110.3 44.7 %copy-start.31 = (s32[2,128]{1,0:T(2,128)S(1)}, s32[2,128]{1,0:T(2,128)}, u32[]{:S(2)}) copy-start(s32[2,128]{1,0:T(2,128)} %param.12) | copy-start | bytes 3076
  110.3 44.8 %copy-start.10 = (bf16[2,128,512]{2,1,0:T(8,128)(2,1)S(1)}, bf16[2,128,512]{2,1,0:T(8,128)(2,1)}, u32[]{:S(2)}) copy-start(bf16[2,128,512]{2,1,0:T(8,128)(2,1)} %param.11) | copy-start | bytes 786436
  112.2 58.4 %copy-start.1 = (bf16[1024,512]{1,0:T(8,128)(2,1)}, bf16[1024,512]{1,0:T(8,128)(2,1)S(1)}, u32[]{:S(2)}) copy-start(bf16[1024,512]{1,0:T(8,128)(2,1)S(1)} %collective-permute-done.1) | copy-start | bytes 3145732
  154.3 101.5 %reduce-scatter.13.cloned.1.call-start = ((), (), s32[]{:S(2)}) async-start(), calls=%async_computation.10 | async-start | bytes 2228224 | tf_op jit(solution)/shard_map/reduce_scatter | solution.py:80
  155.1 17.6 %copy-start.22 = (f32[128]{0:T(128)}, f32[128]{0:T(128)S(1)}, u32[]{:S(2)}) copy-start(f32[128]{0:T(128)S(1)} %fusion.100) | copy-start | bytes 1540
  172.7 5.1 copy-start.9
  172.7 19.6 %copy-start.7 = (bf16[1,512,256]{2,1,0:T(8,128)(2,1)S(1)}, bf16[1,512,256]{2,1,0:T(8,128)(2,1)}, u32[]{:S(2)}) copy-start(bf16[1,512,256]{2,1,0:T(8,128)(2,1)} %param.17) | copy-start | bytes 786436
  172.7 161.7 %reduce-scatter.11.cloned.1.call-start = ((), (), s32[]{:S(2)}) async-start(), calls=%async_computation.9 | async-start | bytes 3620864 | tf_op jit(solution)/shard_map/reduce_scatter | solution.py:80
  197.1 193.4 %all-gather.9.cloned.1.call-start = ((), (), s32[]{:S(2)}) async-start(), calls=%async_computation.11 | async-start | bytes 1671168 | tf_op jit(solution)/shard_map/all_gather | solution.py:84
  334.5 11.1 %copy-start.5 = (f32[32,1664]{1,0:T(8,128)S(1)}, f32[32,1664]{1,0:T(8,128)}, u32[]{:S(2)}) copy-start(f32[32,1664]{1,0:T(8,128)} %reduce-scatter.11.cloned.1.call-done) | copy-start | bytes 638980
  335.4 2.5 copy-start.20
  337.9 56.8 %copy-start.16 = (bf16[32,2,128]{2,1,0:T(2,128)(2,1)}, bf16[32,2,128]{2,1,0:T(2,128)(2,1)S(1)}, u32[]{:S(2)}) copy-start(bf16[32,2,128]{2,1,0:T(2,128)(2,1)S(1)} %reshape.147) | copy-start | bytes 49156
  339.5 4.6 copy-start.26
  347.3 70.7 %reduce-scatter.15.cloned.1.call-start = ((), (), s32[]{:S(2)}) async-start(), calls=%async_computation.12 | async-start | bytes 1310720 | tf_op jit(solution)/shard_map/reduce_scatter | solution.py:80
  387.8 30.2 %copy-start.23 = (f32[128]{0:T(128)S(1)}, f32[128]{0:T(128)}, u32[]{:S(2)}) copy-start(f32[128]{0:T(128)} %copy-done.22) | copy-start | bytes 1540
  394.7 113.3 %reduce-scatter.17.cloned.1.call-start = ((), (), s32[]{:S(2)}) async-start(), calls=%async_computation.13 | async-start | bytes 2228224 | tf_op jit(solution)/shard_map/reduce_scatter | solution.py:80
  434.0 75.0 %copy-start.12 = (f32[2,4,32,32]{2,3,1,0:T(8,128)S(1)}, f32[2,4,32,32]{2,3,1,0:T(8,128)}, u32[]{:S(2)}) copy-start(f32[2,4,32,32]{2,3,1,0:T(8,128)} %copy-done.11) | copy-start | bytes 98308
  434.0 75.0 %copy-start.15 = (bf16[32,2,128]{2,1,0:T(2,128)(2,1)S(1)}, bf16[32,2,128]{2,1,0:T(2,128)(2,1)}, u32[]{:S(2)}) copy-start(bf16[32,2,128]{2,1,0:T(2,128)(2,1)} %copy-done.14) | copy-start | bytes 49156
  434.0 75.0 %copy-start.25 = (f32[2,4,32]{2,1,0:T(4,128)S(1)}, f32[2,4,32]{2,1,0:T(4,128)}, u32[]{:S(2)}) copy-start(f32[2,4,32]{2,1,0:T(4,128)} %copy-done.24) | copy-start | bytes 3076
  434.0 76.4 %copy-start.19 = (f32[32]{0:T(128)S(1)}, f32[32]{0:T(128)}, u32[]{:S(2)}) copy-start(f32[32]{0:T(128)} %copy-done.18) | copy-start | bytes 388
  434.0 77.2 %copy-start.13 = (f32[2,4,32,32]{2,3,1,0:T(8,128)S(1)}, f32[2,4,32,32]{2,3,1,0:T(8,128)}, u32[]{:S(2)}) copy-start(f32[2,4,32,32]{2,3,1,0:T(8,128)} %get-tuple-element.29) | copy-start | bytes 98308
  434.0 77.2 %copy-start.17 = (bf16[32,2,128]{2,1,0:T(2,128)(2,1)S(1)}, bf16[32,2,128]{2,1,0:T(2,128)(2,1)}, u32[]{:S(2)}) copy-start(bf16[32,2,128]{2,1,0:T(2,128)(2,1)} %copy-done.16) | copy-start | bytes 49156
  434.0 77.2 %copy-start.27 = (f32[2,4,32]{2,1,0:T(4,128)S(1)}, f32[2,4,32]{2,1,0:T(4,128)}, u32[]{:S(2)}) copy-start(f32[2,4,32]{2,1,0:T(4,128)} %copy-done.26) | copy-start | bytes 3076
  434.0 120.3 %all-gather.11.cloned.1.call-start = ((), (), s32[]{:S(2)}) async-start(), calls=%async_computation.14 | async-start | bytes 1671168 | tf_op jit(solution)/shard_map/all_gather | solution.py:84
  511.1 87.9 %all-gather.13.cloned.1.call-start = ((), (), s32[]{:S(2)}) async-start(), calls=%async_computation.15 | async-start | bytes 1114112 | tf_op jit(solution)/shard_map/all_gather | solution.py:84
  512.1 86.8 %copy-start.4 = (bf16[512,1024]{1,0:T(8,128)(2,1)S(1)}, bf16[512,1024]{1,0:T(8,128)(2,1)}, u32[]{:S(2)}) copy-start(bf16[512,1024]{1,0:T(8,128)(2,1)} %all-gather.7.cloned.1.call-done) | copy-start | bytes 3145732
  558.1 48.3 %collective-permute-start.3 = (bf16[512,1536]{1,0:T(8,128)(2,1)}, bf16[512,1536]{1,0:T(8,128)(2,1)}, u32[]{:S(2)}, u32[]{:S(2)}) collective-permute-start(bf16[512,1536]{1,0:T(8,128)(2,1)} %get-tuple-element.11), channel_id=1, source_target_pairs={{0,64},{64,0},{1,65},{65,1},{2,66},{66,2},{3,67},{67,3},{4,68},{68... | collective-permute-start | bytes 4718600 | tf_op jit(solution)/shard_map/ppermute | solution.py:169
  600.3 2.7 collective-permute-start.4
  600.5 3.3 collective-permute-start.5
  601.1 5.3 collective-permute-start.2
  603.8 2.6 copy-start.2
Sparse Core Ops, SparseCore 0:
  27.7 77.7 reduce-scatter.6
  109.5 41.8 all-gather.6
  154.5 23.2 reduce-scatter.8
  181.8 73.9 reduce-scatter.12
  259.1 75.3 reduce-scatter.10
  347.4 43.0 all-gather.8
  394.8 23.1 reduce-scatter.14
  434.2 73.8 reduce-scatter.16
  511.2 43.1 all-gather.10
  556.9 41.9 all-gather.12

commit v2 on v1

v2 whole, which is shorter than its diff:
```python
import jax
import jax.numpy as jnp
from jax import lax
from jax.experimental import pallas as pl
from jax.experimental.pallas import tpu as pltpu
from jax.sharding import PartitionSpec as P

MODEL_WIDTH = 8192
HEAD_WIDTH = 128
SLOT = 32
LANES = 128

epsilon = 1e-06
masked_score = -1e30
MESH = pl.DeviceIdType.MESH
NN = ((1,), (0,))
NT = ((1,), (1,))
TN = ((0,), (0,))


def segments(lengths):
    ends = jnp.stack([jnp.sum(lengths[..., : c + 1], -1) for c in range(lengths.shape[-1])], -1)
    position = jnp.arange(SLOT, dtype=jnp.int32)
    return jnp.sum((ends[..., None, :] <= position[:, None]).astype(jnp.int32), -1)


def token_weights(lengths, rewards, groups):
    group_total = 2 * lengths.shape[1]
    reward_flat = rewards.reshape(-1).astype(jnp.float32)
    member = (
        groups.reshape(-1)[:, None] == jnp.arange(group_total, dtype=jnp.int32)[None, :]
    ).astype(jnp.float32)
    member_count = jnp.sum(member, 0)
    group_mean = jnp.sum(member * reward_flat[:, None], 0) / member_count
    centered = reward_flat - jnp.sum(member * group_mean[None, :], 1)
    variance = jnp.sum(member * (centered * centered)[:, None], 0) / member_count
    spread_own = jnp.sum(member * jnp.sqrt(variance)[None, :], 1)
    advantage = (centered / jnp.maximum(spread_own, 1.0)).reshape(lengths.shape)
    segment = segments(lengths)
    choose = (segment[..., None] == jnp.arange(lengths.shape[2], dtype=jnp.int32)).astype(
        jnp.float32
    )
    token_adv = jnp.sum(choose * advantage[:, :, None, :], -1)
    token_len = jnp.sum(choose * lengths[:, :, None, :].astype(jnp.float32), -1)
    return (token_adv * SLOT / token_len).reshape(lengths.shape[0], -1)


def dot(a, b, contract):
    return lax.dot_general(a, b, (contract, ((), ())), preferred_element_type=jnp.float32)


def split_tile(column):
    high = column.astype(jnp.bfloat16).astype(jnp.float32)
    lane = lax.broadcasted_iota(jnp.int32, (column.shape[0], LANES), 1)
    tile = jnp.where(lane == 0, high, jnp.where(lane == 1, column - high, 0.0))
    return tile.astype(jnp.bfloat16)


RS_QKV0, AG_HEAD0, RS_HEAD1, RS_QKV1, AG_GRAD1, AG_HEAD1, RS_HEAD0, AG_GRAD0 = range(8)
AG_STREAM0, AG_TOP, RS_OUT0, AG_STREAM1, RS_IN1, AG_OUT0 = range(6)


def kernel(
    x_in, g_in, doc, wq, wk, wv, wo,
    xs_out, hs_out, gs_out, dq_out, dk_out, dv_out,
    X, H, G, Q, WQKV, WO, S0, R0, S1, R1, T1, V1, T0, V0, D, E, DH, EH, OWN, ROWS, INV, PROBS,
    fs, fr, zs, zr, ss, sr, ls, lo,
):
    core, f, t = lax.axis_index("pp"), lax.axis_index("fsdp"), lax.axis_index("tp")
    y = f // 4
    far = 1 - core
    slots, shares = R0.shape[0], E.shape[0]
    rows = X.shape[1] // shares
    query_cols, key_cols = wq.shape[2], wk.shape[2]
    cols = query_cols + 2 * key_cols
    cuts = ((wq, 0, query_cols), (wk, query_cols, key_cols), (wv, query_cols + key_cols, key_cols))
    per_block = rows // SLOT

    def block(b):
        return pl.ds(pl.multiple_of(b * rows, rows), rows)

    def slot(s):
        return pl.ds(pl.multiple_of(s * SLOT, SLOT), SLOT)

    def remote(src, dst, send, recv, **at):
        return pltpu.make_async_remote_copy(
            src_ref=src, dst_ref=dst, send_sem=send, recv_sem=recv,
            device_id=at, device_id_type=MESH,
        )

    mine, own = slot(f), block(t)

    loads = [
        pltpu.make_async_copy(x_in.at[core], X.at[0, own], ls.at[0]),
        pltpu.make_async_copy(g_in, G.at[1, own], ls.at[1]),
        pltpu.make_async_copy(wo.at[0], WO.at[core], ls.at[2]),
    ] + [
        pltpu.make_async_copy(w.at[0], WQKV.at[core, :, pl.ds(at, width)], ls.at[3 + i])
        for i, (w, at, width) in enumerate(cuts)
    ]
    for c in loads:
        c.start()

    barrier = pltpu.get_barrier_semaphore()

    def greet_slot(k, _):
        pl.semaphore_signal(
            barrier, inc=1, device_id={"fsdp": lax.rem(f + k, slots)}, device_id_type=MESH
        )
        return 0

    lax.fori_loop(1, slots, greet_slot, 0)
    for k in range(1, shares):
        pl.semaphore_signal(
            barrier, inc=1, device_id={"tp": lax.rem(t + k, shares)}, device_id_type=MESH
        )
    pl.semaphore_signal(barrier, inc=1, device_id={"pp": far}, device_id_type=MESH)
    pl.semaphore_wait(barrier, slots + shares - 1)

    def z_gather(phase, buf):
        for k in (2, 1, 3):
            remote(buf.at[own], buf.at[own], zs.at[phase], zr.at[phase, t], tp=lax.rem(t + k, shares)).start()

    def z_gather_wait(phase, buf, b):
        remote(buf.at[block(b)], buf.at[block(b)], zs.at[phase], zr.at[phase, b], tp=t).wait_recv()

    def z_send(phase, send, recv, b):
        remote(send.at[block(b)], recv.at[t], zs.at[phase], zr.at[phase, t], tp=b).start()

    def z_sum(phase, recv, total):
        for k in (1, 3, 2):
            s = lax.rem(t + k, shares)
            remote(recv.at[s], recv.at[s], zs.at[phase], zr.at[phase, s], tp=t).wait_recv()
            total = total + recv[s].astype(jnp.float32)
        return total

    def f_gather(phase, buf):
        def one(k, _):
            remote(
                buf.at[mine], buf.at[mine], fs.at[phase], fr.at[phase, f], fsdp=lax.rem(f + k, slots)
            ).start()
            return 0

        lax.fori_loop(1, slots, one, 0)

    def f_gather_wait(phase, buf, b):
        for j in range(per_block):
            s = b * per_block + j

            @pl.when(s != f)
            def _():
                remote(
                    buf.at[slot(s)], buf.at[slot(s)], fs.at[phase], fr.at[phase, s], fsdp=f
                ).wait_recv()

    def f_send(phase, send, recv, b):
        for j in range(per_block):
            s = b * per_block + j

            @pl.when(s != f)
            def _():
                remote(send.at[slot(s)], recv.at[f], fs.at[phase], fr.at[phase, f], fsdp=s).start()

    def f_sum(phase, send, recv):
        def one(k, total):
            s = lax.rem(f + k, slots)
            remote(recv.at[s], recv.at[s], fs.at[phase], fr.at[phase, s], fsdp=f).wait_recv()
            return total + recv[s].astype(jnp.float32)

        return lax.fori_loop(1, slots, one, send[mine].astype(jnp.float32))

    def project(layer, phase, gathered, send, recv):
        def one(k, _):
            b = lax.rem(y + k, shares)

            @pl.when(b != t)
            def _():
                z_gather_wait(gathered, X.at[layer], b)

            part = X[layer, block(b)]
            send[block(b), pl.ds(0, cols)] = dot(part, WQKV[layer], NN).astype(jnp.bfloat16)
            wide = part.astype(jnp.float32)
            send[block(b), pl.ds(cols, LANES)] = split_tile(
                jnp.sum(wide * wide, -1, keepdims=True)
            )
            f_send(phase, send, recv, b)
            return 0

        lax.fori_loop(0, shares, one, 0)

    def finish_rows(layer, phase, send, recv):
        summed = f_sum(phase, send, recv)
        squares = summed[:, cols : cols + 1] + summed[:, cols + 1 : cols + 2]
        inv_rms = lax.rsqrt(squares / MODEL_WIDTH + epsilon)
        ROWS[layer] = (summed[:, :cols] * inv_rms).astype(jnp.bfloat16)
        INV[layer] = jnp.broadcast_to(inv_rms, (SLOT, LANES))

    kv_heads = key_cols // HEAD_WIDTH
    group = query_cols // key_cols
    scale = HEAD_WIDTH**-0.5

    def stacked(ref, g):
        return jnp.concatenate(
            [ref[:, (g * group + h) * HEAD_WIDTH : (g * group + h + 1) * HEAD_WIDTH] for h in range(group)], 0
        )

    def key_value(layer, g):
        at = query_cols + g * HEAD_WIDTH
        return (
            ROWS[layer, :, at : at + HEAD_WIDTH],
            ROWS[layer, :, at + key_cols : at + key_cols + HEAD_WIDTH],
        )

    def attend(layer):
        for g in range(kv_heads):
            keys, values = key_value(layer, g)
            scores = dot(stacked(ROWS.at[layer], g), keys, NT) * scale
            scores = jnp.where(doc[...] > 0.5, scores, masked_score)
            raised = jnp.exp(scores - jnp.max(scores, -1, keepdims=True))
            probs = raised / jnp.sum(raised, -1, keepdims=True)
            PROBS[layer, g] = probs
            mixed = dot(probs.astype(jnp.bfloat16), values, NN).astype(jnp.bfloat16)
            for h in range(group):
                H[layer, mine, pl.ds((g * group + h) * HEAD_WIDTH, HEAD_WIDTH)] = mixed[
                    h * SLOT : (h + 1) * SLOT
                ]

    def attend_back(layer, phase, send, recv):
        head_grad = f_sum(phase, send, recv).astype(jnp.bfloat16)
        inv_rms = INV[layer]
        total = jnp.zeros((SLOT, LANES), jnp.float32)

        def put(at, grad, rows_at):
            rounded = grad.astype(jnp.bfloat16).astype(jnp.float32)
            Q[layer, mine, pl.ds(at, HEAD_WIDTH)] = (rounded * inv_rms).astype(jnp.bfloat16)
            return rounded * rows_at.astype(jnp.float32)

        for g in range(kv_heads):
            keys, values = key_value(layer, g)
            queries = stacked(ROWS.at[layer], g)
            grads = stacked(head_grad, g)
            probs = PROBS[layer, g]
            prob_grad = dot(grads, values, NT)
            value_grad = dot(probs.astype(jnp.bfloat16), grads, TN)
            score_grad = probs * (prob_grad - jnp.sum(prob_grad * probs, -1, keepdims=True))
            score_grad = score_grad.astype(jnp.bfloat16)
            query_grad = dot(score_grad, keys, NN) * scale
            key_grad = dot(score_grad, queries, TN) * scale
            for h in range(group):
                part = slice(h * SLOT, (h + 1) * SLOT)
                total = total + put((g * group + h) * HEAD_WIDTH, query_grad[part], queries[part])
            total = total + put(query_cols + g * HEAD_WIDTH, key_grad, keys)
            total = total + put(query_cols + key_cols + g * HEAD_WIDTH, value_grad, values)
        share = inv_rms[:, :1] * inv_rms[:, :1] * jnp.sum(total, -1, keepdims=True) / MODEL_WIDTH
        Q[layer, mine, pl.ds(cols, LANES)] = split_tile(share)

    def head_grads(layer, phase, gathered, send, recv):
        def one(k, _):
            b = lax.rem(y + k, shares)

            @pl.when(b != t)
            def _():
                z_gather_wait(gathered, G.at[layer], b)

            send[block(b)] = dot(G[layer, block(b)], WO[layer], NT).astype(jnp.bfloat16)
            f_send(phase, send, recv, b)
            return 0

        lax.fori_loop(0, shares, one, 0)

    def to_shares(phase, send, recv, term):
        def one(i, _):
            b = lax.rem(t + 1 + lax.rem(i + 1, 3), shares)
            send[block(b)] = term(b).astype(jnp.bfloat16)
            z_send(phase, send, recv, b)
            return 0

        lax.fori_loop(0, shares - 1, one, 0)
        OWN[...] = term(t)

    def out_term(b):
        f_gather_wait(AG_HEAD0, H.at[0], b)
        return dot(H[0, block(b)], WO[0], NN)

    def in_term(b):
        f_gather_wait(AG_GRAD1, Q.at[1], b)
        tile = Q[1, block(b), pl.ds(cols, LANES)].astype(jnp.float32)
        share = tile[:, :1] + tile[:, 1:2]
        back = dot(Q[1, block(b), pl.ds(0, cols)], WQKV[1], NT)
        return back - X[1, block(b)].astype(jnp.float32) * share

    loads[0].wait()
    z_gather(AG_STREAM0, X.at[0])
    swaps = [
        remote(w.at[0], WQKV.at[core, :, pl.ds(at, width)], ss.at[i], sr.at[i], pp=far)
        for i, (w, at, width) in enumerate(cuts)
    ] + [remote(wo.at[0], WO.at[core], ss.at[3], sr.at[3], pp=far)]
    for c in swaps:
        c.start()
    for c in loads[1:]:
        c.wait()
    for c in swaps[:3]:
        c.wait_recv()
    project(0, RS_QKV0, AG_STREAM0, S0, R0)
    z_gather(AG_TOP, G.at[1])
    finish_rows(0, RS_QKV0, S0, R0)
    attend(0)
    f_gather(AG_HEAD0, H.at[0])
    swaps[3].wait_recv()
    to_shares(RS_OUT0, D, E, out_term)
    head_grads(1, RS_HEAD1, AG_TOP, T1, V1)
    stream = X[0, own].astype(jnp.float32) + z_sum(RS_OUT0, E, OWN[...])
    X[1, own] = stream.astype(jnp.bfloat16)
    z_gather(AG_STREAM1, X.at[1])
    project(1, RS_QKV1, AG_STREAM1, S1, R1)

    def hand_over(i, buf, out):
        pair = (
            pltpu.make_async_copy(buf.at[core], out.at[0], lo.at[i]),
            remote(buf.at[far], out.at[1], ss.at[4 + i], sr.at[4 + i], pp=far),
        )
        for c in pair:
            c.start()
        return pair

    pairs = [hand_over(0, X, xs_out)]
    finish_rows(1, RS_QKV1, S1, R1)
    attend(1)
    attend_back(1, RS_HEAD1, T1, V1)
    f_gather(AG_GRAD1, Q.at[1])
    f_gather(AG_HEAD1, H.at[1])
    to_shares(RS_IN1, DH, EH, in_term)
    grad = G[1, own].astype(jnp.float32) + z_sum(RS_IN1, EH, OWN[...])
    G[0, own] = grad.astype(jnp.bfloat16)
    z_gather(AG_OUT0, G.at[0])
    head_grads(0, RS_HEAD0, AG_OUT0, T0, V0)
    pairs.append(hand_over(1, G, gs_out))
    for b in range(shares):
        f_gather_wait(AG_HEAD1, H.at[1], b)
    pairs.append(hand_over(2, H, hs_out))
    attend_back(0, RS_HEAD0, T0, V0)
    f_gather(AG_GRAD0, Q.at[0])
    for b in range(shares):
        f_gather_wait(AG_GRAD0, Q.at[0], b)
    for i, (at, width, out) in enumerate(
        ((0, query_cols, dq_out), (query_cols, key_cols, dk_out), (query_cols + key_cols, key_cols, dv_out))
    ):
        part = Q.at[:, :, pl.ds(at, width)]
        pairs.append(hand_over(3 + i, part, out))

    others = pl.ds(0, (slots - 1) * SLOT)
    for phase, buf in (
        (RS_QKV0, S0), (AG_HEAD0, H.at[0]), (RS_HEAD1, T1), (RS_QKV1, S1),
        (AG_GRAD1, Q.at[1]), (AG_HEAD1, H.at[1]), (RS_HEAD0, T0), (AG_GRAD0, Q.at[0]),
    ):
        remote(buf.at[others], buf.at[others], fs.at[phase], fr.at[phase, 0], fsdp=f).wait_send()
    others = pl.ds(0, (shares - 1) * rows)
    for phase, buf in (
        (AG_STREAM0, X.at[0]), (AG_TOP, G.at[1]), (RS_OUT0, D),
        (AG_STREAM1, X.at[1]), (RS_IN1, DH), (AG_OUT0, G.at[0]),
    ):
        remote(buf.at[others], buf.at[others], zs.at[phase], zr.at[phase, 0], tp=t).wait_send()
    for c in swaps:
        c.wait_send()
    for here, there in pairs:
        here.wait()
        there.wait()


def local(
    inputs,
    head_grad,
    noise_mask,
    lengths,
    rewards,
    groups,
    query_weight,
    key_weight,
    value_weight,
    out_weight,
):
    core = lax.axis_index("pp")
    row_count, width = inputs.shape[1:]
    slots, shares = lax.axis_size("fsdp"), lax.axis_size("tp")
    tokens = row_count * shares
    query_cols, key_cols = query_weight.shape[2], key_weight.shape[2]
    wide = query_cols + 2 * key_cols + LANES
    kv_heads, group = key_cols // HEAD_WIDTH, query_cols // key_cols

    segment = segments(lengths)[core, lax.axis_index("fsdp")]
    same_doc = jnp.tile((segment[:, None] == segment[None, :]).astype(jnp.float32), (group, 1))
    weight = lax.dynamic_slice_in_dim(
        token_weights(lengths, rewards, groups)[core], lax.axis_index("tp") * row_count, row_count, 0
    ) * noise_mask[core].astype(jnp.float32)
    top_grad = (-weight[:, None] * head_grad[core].astype(jnp.float32)).astype(jnp.bfloat16)

    bf16, f32 = jnp.bfloat16, jnp.float32
    any_space = pl.BlockSpec(memory_space=pl.ANY)
    streams, heads, out_grads, query_grads, key_grads, value_grads = pl.pallas_call(
        kernel,
        out_shape=[
            jax.ShapeDtypeStruct((2, tokens, n), bf16)
            for n in (width, query_cols, width, query_cols, key_cols, key_cols)
        ],
        in_specs=[any_space, any_space, pl.BlockSpec(memory_space=pltpu.VMEM)] + [any_space] * 4,
        out_specs=[any_space] * 6,
        scratch_shapes=[
            pltpu.VMEM((2, tokens, width), bf16),
            pltpu.VMEM((2, tokens, query_cols), bf16),
            pltpu.VMEM((2, tokens, width), bf16),
            pltpu.VMEM((2, tokens, wide), bf16),
            pltpu.VMEM((2, width, wide - LANES), bf16),
            pltpu.VMEM((2, query_cols, width), bf16),
            pltpu.VMEM((tokens, wide), bf16),
            pltpu.VMEM((slots, SLOT, wide), bf16),
            pltpu.VMEM((tokens, wide), bf16),
            pltpu.VMEM((slots, SLOT, wide), bf16),
            pltpu.VMEM((tokens, query_cols), bf16),
            pltpu.VMEM((slots, SLOT, query_cols), bf16),
            pltpu.VMEM((tokens, query_cols), bf16),
            pltpu.VMEM((slots, SLOT, query_cols), bf16),
            pltpu.VMEM((tokens, width), bf16),
            pltpu.VMEM((shares, row_count, width), bf16),
            pltpu.VMEM((tokens, width), bf16),
            pltpu.VMEM((shares, row_count, width), bf16),
            pltpu.VMEM((row_count, width), f32),
            pltpu.VMEM((2, SLOT, wide - LANES), bf16),
            pltpu.VMEM((2, SLOT, LANES), f32),
            pltpu.VMEM((2, kv_heads, group * SLOT, SLOT), f32),
            pltpu.SemaphoreType.DMA((8,)),
            pltpu.SemaphoreType.DMA((8, slots)),
            pltpu.SemaphoreType.DMA((6,)),
            pltpu.SemaphoreType.DMA((6, shares)),
            pltpu.SemaphoreType.DMA((10,)),
            pltpu.SemaphoreType.DMA((10,)),
            pltpu.SemaphoreType.DMA((6,)),
            pltpu.SemaphoreType.DMA((6,)),
        ],
        compiler_params=pltpu.CompilerParams(
            collective_id=0, has_side_effects=True, vmem_limit_bytes=56 * 1024 * 1024
        ),
    )(inputs, top_grad, same_doc, query_weight, key_weight, value_weight, out_weight)

    def weight_grad(a, b):
        return lax.dot_general(a, b, (((0, 1), (0, 1)), ((), ())), preferred_element_type=f32)[None]

    return (
        weight_grad(streams, query_grads),
        weight_grad(streams, key_grads),
        weight_grad(streams, value_grads),
        weight_grad(heads, out_grads),
    )


def solution(mesh):
    return jax.shard_map(
        local,
        mesh=mesh,
        in_specs=(
            P(None, "tp", "fsdp"),
            P(None, "tp", "fsdp"),
            P(None, "tp"),
            P(),
            P(),
            P(),
            P("pp", "fsdp", "tp"),
            P("pp", "fsdp", "tp"),
            P("pp", "fsdp", "tp"),
            P("pp", "tp", "fsdp"),
        ),
        out_specs=(
            P("pp", "fsdp", "tp"),
            P("pp", "fsdp", "tp"),
            P("pp", "fsdp", "tp"),
            P("pp", "tp", "fsdp"),
        ),
        check_vma=False,
    )
```

time: 621 us -> 202 us (0.33)
  waiting for transfers between devices: 444 us -> 0 us
  Pallas kernels: 0 us -> 181 us
  blocking collectives: 93.9 us -> 0 us
  other arithmetic: 23.2 us -> 3.87 us
  matrix products: 28.9 us -> 9.78 us
  between operations: 15.5 us -> 0.8 us
  local copies, waits for them, and re-layouts: 11.8 us -> 3.46 us
    reduce_scatter x6 -> x0, waiting for transfers between devices: 315 us -> none  [scatter(): return lax.psum_scatter(value, axis, scatter_dimension=0, tiled=True)]
    pallas_call x0 -> x1, Pallas kernels: none -> 181 us  [local(): pl.pallas_call(kernel, out_shape=[jax.ShapeDtypeStruct((2, tokens, n), bf...]
    all_gather x4 -> x0, waiting for transfers between devices: 125 us -> none  [gather(): return lax.all_gather(value, axis, axis=0, tiled=True)]
    all_gather x4 -> x0, blocking collectives: 55.8 us -> none  [gather(): return lax.all_gather(value, axis, axis=0, tiled=True)]
    unnamed x1 -> x0, blocking collectives: 38.1 us -> none
    dot_general x18 -> x4, matrix products: 27.1 us -> 9.78 us  [weight_grad(): lax.dot_general(a, b, (((0, 1), (0, 1)), ((), ())), preferred_element_typ...]
    convert_element_type x9 -> x1, other arithmetic: 7.59 us -> 0.07 us  [local(): (segment[:, None] == segment[None, :]).astype(jnp.float32)]
  transfers between devices with their start and end apart: 16 -> 0, of which waited for: 13 -> 0; matrix products, arithmetic and copies ran while one was open for 4% -> 0% of each run, Pallas kernels for 0% -> 0%
where the time goes in v2:
time: 202 us; the launch traced here: 199 us
  Pallas kernels  181 us (90%)
  matrix products  9.78 us (5%)
  other arithmetic  3.87 us (2%)
  local copies, waits for them, and re-layouts  3.46 us (2%)
    pallas_call x1, Pallas kernels, local(): pl.pallas_call(kernel, out_shape=[jax.ShapeDtypeStruct((2, tokens, n), bf...  181 us
    dot_general x4, matrix products, weight_grad(): lax.dot_general(a, b, (((0, 1), (0, 1)), ((), ())), preferred_element_typ...  9.78 us

profile of v2, /device:TPU:0, one launch (start us, length us, event | category | flops | bytes accessed | tf_op | source)
XLA Modules:
  0.0 199.3 jit_solution(10614753511943495865)
XLA Ops:
  0.6 0.7 slice.4
  1.3 0.8 fusion.6
  2.1 0.1 convert_reduce_fusion
  2.2 0.1 compare_convert_fusion
  2.3 0.8 copy.34
  3.1 0.1 convert_element_type.53
  3.2 0.8 copy.35
  3.9 0.1 eq.50
  4.0 0.1 convert_reduce_fusion.1
  4.2 0.1 select_reduce_fusion.4
  4.3 0.1 select_reduce_fusion.3
  4.4 0.1 select_reduce_fusion.2
  4.5 0.1 max.13
  4.6 0.1 reduce_sum.104
  4.7 0.1 copy.36
  4.8 0.1 select_reduce_fusion.1
  4.9 0.1 div.30
  5.0 0.8 fusion.5
  5.8 0.6 tile.4
  6.4 1.6 fusion.g_in
  8.1 181.4 %shard_map.129 = (bf16[2,512,512]{2,1,0:T(8,128)(2,1)}, bf16[2,512,1024]{2,1,0:T(8,128)(2,1)}, bf16[2,512,512]{2,1,0:T(8,128)(2,1)}, bf16[2,512,1024]{2,1,0:T(8,...) custom-call(bf16[2,128,512]{2,1,0:T(8,128)(2,1)} %x_in.1, bf16[128,512]{1,0:T(8,128)(2,1)} %fusion.g_in, ...), custom_call_target="tpu_custom_call" | custom-call | tf_op jit(solution)/shard_map/pallas_call | solution.py:399
  189.5 0.0 copy-start
  189.5 0.0 copy-start.4
  189.5 0.0 copy-start.3
  189.5 4.6 %convolution_bitcast_fusion.1 = f32[1,512,1024]{2,1,0:T(8,128)} fusion(bf16[2,512,512]{2,1,0:T(8,128)(2,1)} %get-tuple-element.10, bf16[2,512,1024]{2,1,0:T(8,128)(2,1)} %get-tuple-element.11), kind=kOutput, calls=%fused_computation.1 | convolution fusion | flops 1073741824 | bytes 5242880 | tf_op jit(solution)/shard_map/dot_general | solution.py:445
  194.2 0.0 copy-done
  194.2 0.0 copy-done.4
  194.2 0.0 copy-start.1
  194.2 0.0 copy-start.2
  194.2 1.3 convolution_bitcast_fusion.3
  195.5 0.0 copy-done.3
  195.5 1.3 convolution_bitcast_fusion.2
  196.7 0.0 copy-done.1
  196.7 0.0 copy-done.2
  196.7 2.6 %convolution_bitcast_fusion = f32[1,1024,512]{2,1,0:T(8,128)} fusion(bf16[2,512,1024]{2,1,0:T(8,128)(2,1)S(1)} %copy-done.1, bf16[2,512,512]{2,1,0:T(8,128)(2,1)S(1)} %copy-done.2), kind=kOutput, calls=%fused_computation | convolution fusion | flops 1073741824 | bytes 5242880 | tf_op jit(solution)/shard_map/dot_general | solution.py:445
  (10 shorter events, 0.1 us)
Async XLA Ops:
  189.5 4.7 %copy-start = (bf16[2,512,512]{2,1,0:T(8,128)(2,1)S(1)}, bf16[2,512,512]{2,1,0:T(8,128)(2,1)}, u32[]{:S(2)}) copy-start(bf16[2,512,512]{2,1,0:T(8,128)(2,1)} %get-tuple-element.10) | copy-start | bytes 3145732
  189.5 4.7 %copy-start.4 = (bf16[2,512,256]{2,1,0:T(8,128)(2,1)S(1)}, bf16[2,512,256]{2,1,0:T(8,128)(2,1)}, u32[]{:S(2)}) copy-start(bf16[2,512,256]{2,1,0:T(8,128)(2,1)} %get-tuple-element.12) | copy-start | bytes 1572868
  189.5 5.9 %copy-start.3 = (bf16[2,512,256]{2,1,0:T(8,128)(2,1)S(1)}, bf16[2,512,256]{2,1,0:T(8,128)(2,1)}, u32[]{:S(2)}) copy-start(bf16[2,512,256]{2,1,0:T(8,128)(2,1)} %get-tuple-element.13) | copy-start | bytes 1572868
  194.2 2.6 %copy-start.1 = (bf16[2,512,1024]{2,1,0:T(8,128)(2,1)S(1)}, bf16[2,512,1024]{2,1,0:T(8,128)(2,1)}, u32[]{:S(2)}) copy-start(bf16[2,512,1024]{2,1,0:T(8,128)(2,1)} %get-tuple-element.14) | copy-start | bytes 6291460
  194.2 2.6 %copy-start.2 = (bf16[2,512,512]{2,1,0:T(8,128)(2,1)S(1)}, bf16[2,512,512]{2,1,0:T(8,128)(2,1)}, u32[]{:S(2)}) copy-start(bf16[2,512,512]{2,1,0:T(8,128)(2,1)} %get-tuple-element.15) | copy-start | bytes 3145732

commit v3 on v1

v3 whole, which is shorter than its diff:
```python
import jax
import jax.numpy as jnp
from jax import lax
from jax.experimental import pallas as pl
from jax.experimental.pallas import tpu as pltpu
from jax.sharding import PartitionSpec as P

MODEL_WIDTH = 8192
HEAD_WIDTH = 128
SLOT = 32
LANES = 128

epsilon = 1e-06
masked_score = -1e30
MESH = pl.DeviceIdType.MESH
NN = ((1,), (0,))
NT = ((1,), (1,))
TN = ((0,), (0,))


def segments(lengths):
    ends = jnp.stack([jnp.sum(lengths[..., : c + 1], -1) for c in range(lengths.shape[-1])], -1)
    position = jnp.arange(SLOT, dtype=jnp.int32)
    return jnp.sum((ends[..., None, :] <= position[:, None]).astype(jnp.int32), -1)


def token_weights(lengths, rewards, groups):
    group_total = 2 * lengths.shape[1]
    reward_flat = rewards.reshape(-1).astype(jnp.float32)
    member = (
        groups.reshape(-1)[:, None] == jnp.arange(group_total, dtype=jnp.int32)[None, :]
    ).astype(jnp.float32)
    member_count = jnp.sum(member, 0)
    group_mean = jnp.sum(member * reward_flat[:, None], 0) / member_count
    centered = reward_flat - jnp.sum(member * group_mean[None, :], 1)
    variance = jnp.sum(member * (centered * centered)[:, None], 0) / member_count
    spread_own = jnp.sum(member * jnp.sqrt(variance)[None, :], 1)
    advantage = (centered / jnp.maximum(spread_own, 1.0)).reshape(lengths.shape)
    segment = segments(lengths)
    choose = (segment[..., None] == jnp.arange(lengths.shape[2], dtype=jnp.int32)).astype(
        jnp.float32
    )
    token_adv = jnp.sum(choose * advantage[:, :, None, :], -1)
    token_len = jnp.sum(choose * lengths[:, :, None, :].astype(jnp.float32), -1)
    return (token_adv * SLOT / token_len).reshape(lengths.shape[0], -1)


def dot(a, b, contract):
    return lax.dot_general(a, b, (contract, ((), ())), preferred_element_type=jnp.float32)


RS_QKV0, RS_QKV1, RS_HEAD1, RS_HEAD0, AG_HEAD0, AG_GRAD1, AG_HEAD1, AG_GRAD0 = range(8)
AG_STREAM0, AG_TOP, RS_OUT0, AG_STREAM1, RS_IN1, AG_OUT0 = range(6)
HALVES = (0, 1)
PEERS = (2, 1, 3)
SIDE = 4
SUB = 16


def split_tile(first, second):
    lane = lax.broadcasted_iota(jnp.int32, first.shape[:-1] + (LANES,), first.ndim - 1)
    tile = jnp.zeros(lane.shape, jnp.float32)
    for i, column in enumerate((first, second)):
        high = column.astype(jnp.bfloat16).astype(jnp.float32)
        tile = jnp.where(lane == 2 * i, high, jnp.where(lane == 2 * i + 1, column - high, tile))
    return tile.astype(jnp.bfloat16)


def join_tile(tile):
    tile = tile.astype(jnp.float32)
    return tile[..., 0:1] + tile[..., 1:2], tile[..., 2:3] + tile[..., 3:4]


def kernel(
    x_in, g_in, doc, wq, wk, wv, wo,
    xs_out, hs_out, gs_out, dq_out, dk_out, dv_out,
    X, H, G, Q, W, WO, D, E, DH, EH, ROWS, INV, PROBS, HG, *rest,
):
    scatter_bufs, (fs, fr, zs, zr, ss, sr, ls, lo) = rest[:28], rest[28:]
    rs_bufs = {
        phase: scatter_bufs[7 * i : 7 * i + 7]
        for i, phase in enumerate((RS_QKV0, RS_QKV1, RS_HEAD1, RS_HEAD0))
    }
    core, f, t = lax.axis_index("pp"), lax.axis_index("fsdp"), lax.axis_index("tp")
    far = 1 - core
    y, x = f // SIDE, f % SIDE
    j, g = x // 2, x % 2
    q_wide = wq.shape[2] // 2
    k_wide = wk.shape[2] // 2
    cols = q_wide + 2 * k_wide
    wide = cols + LANES
    group = q_wide // HEAD_WIDTH
    scale = HEAD_WIDTH**-0.5

    def span(which, stride, width, at=0):
        return pl.ds(pl.multiple_of(which * stride + at, LANES), width)

    def other(mine, k):
        return lax.rem(mine + k, SIDE)

    def remote(src, dst, send, recv, **at):
        return pltpu.make_async_remote_copy(
            src_ref=src, dst_ref=dst, send_sem=send, recv_sem=recv,
            device_id=at, device_id_type=MESH,
        )

    cuts = [
        (w, gg * width, gg, at, width)
        for gg in (0, 1)
        for w, at, width in ((wq, 0, q_wide), (wk, q_wide, k_wide), (wv, q_wide + k_wide, k_wide))
    ]
    loads = [pltpu.make_async_copy(x_in.at[core], X.at[0, :, t], ls.at[0])] + [
        pltpu.make_async_copy(
            w.at[0, :, pl.ds(at, width)], W.at[core, gg, :, pl.ds(to, width)], ls.at[1 + i]
        )
        for i, (w, at, gg, to, width) in enumerate(cuts)
    ]
    loads += [
        pltpu.make_async_copy(wo.at[0], WO.at[core], ls.at[7]),
        pltpu.make_async_copy(g_in, G.at[1, :, t], ls.at[8]),
    ]
    for c in loads:
        c.start()

    barrier = pltpu.get_barrier_semaphore()
    for k in (1, 2, 3):
        for at in (
            {"fsdp": y * SIDE + other(x, k)},
            {"fsdp": other(y, k) * SIDE + x},
            {"tp": other(t, k)},
        ):
            pl.semaphore_signal(barrier, inc=1, device_id=at, device_id_type=MESH)
    pl.semaphore_signal(barrier, inc=1, device_id={"pp": far}, device_id_type=MESH)
    pl.semaphore_wait(barrier, 10)

    def z_gather(phase, buf, h):
        for k in PEERS:
            remote(buf.at[h, t], buf.at[h, t], zs.at[phase, h], zr.at[phase, h], tp=other(t, k)).start()

    def z_scatter(phase, send, recv, h):
        for k in PEERS:
            b = other(t, k)
            remote(send.at[h, b], recv.at[h, t], zs.at[phase, h], zr.at[phase, h], tp=b).start()

    def z_all(phase, buf, h):
        three = buf.at[h, pl.ds(0, SIDE - 1)]
        return remote(three, three, zs.at[phase, h], zr.at[phase, h], tp=t)

    def z_sum(phase, send, recv, h, total):
        z_all(phase, recv, h).wait_recv()
        total = total + send[h, t].astype(jnp.float32)
        for k in PEERS:
            total = total + recv[h, other(t, k)].astype(jnp.float32)
        return total.astype(jnp.bfloat16)

    def push(phase, h, kind, src, dst, **at):
        remote(src, dst, fs.at[phase, h, kind], fr.at[phase, h, kind], **at).start()

    def f_all(phase, h, kind):
        S, RA, RB, UA, UB, VA, VB = rs_bufs[
            {AG_HEAD0: RS_HEAD0, AG_HEAD1: RS_HEAD0, AG_GRAD0: RS_QKV0, AG_GRAD1: RS_QKV0}.get(phase, phase)
        ]
        order = (RA, RB, VA, VB) if phase < AG_HEAD0 else (VA, VB, RA, RB)
        three = order[kind].at[h, pl.ds(0, SIDE - 1)]
        return remote(three, three, fs.at[phase, h, kind], fr.at[phase, h, kind], fsdp=f)

    def widths(buf_cols):
        return (wide, cols) if buf_cols == 2 * wide else (q_wide, q_wide)

    def rs_start(phase, h):
        S, RA, RB, UA, UB, VA, VB = rs_bufs[phase]
        ca, cb = widths(S.shape[-1])
        for k in PEERS:
            y2, x2 = other(y, k), other(x, k)
            push(phase, h, 0, S.at[h, y2, :, 0], RA.at[h, y], fsdp=y2 * SIDE + x)
            push(
                phase, h, 1, S.at[h, :, x2 // 2, 1, :, span(x2 % 2, ca, cb)], RB.at[h, x], fsdp=y * SIDE + x2
            )

    def rs_mid(phase, h):
        S, RA, RB, UA, UB, VA, VB = rs_bufs[phase]
        ca, cb = widths(S.shape[-1])
        f_all(phase, h, 0).wait_recv()
        total = S[h, y, :, 0].astype(jnp.float32)
        for k in PEERS:
            total = total + RA[h, other(y, k)].astype(jnp.float32)
        UA[h] = total.astype(jnp.bfloat16)
        for k in PEERS:
            x2 = other(x, k)
            push(
                phase, h, 2, UA.at[h, x2 // 2, :, span(x2 % 2, ca, ca)], VA.at[h, x], fsdp=y * SIDE + x2
            )
        f_all(phase, h, 1).wait_recv()
        total = S[h, :, j, 1, :, span(g, ca, cb)].astype(jnp.float32)
        for k in PEERS:
            total = total + RB[h, other(x, k)].astype(jnp.float32)
        UB[h] = total.astype(jnp.bfloat16)
        for k in PEERS:
            y2 = other(y, k)
            push(phase, h, 3, UB.at[h, y2], VB.at[h, y], fsdp=y2 * SIDE + x)

    def rs_end(phase, h):
        S, RA, RB, UA, UB, VA, VB = rs_bufs[phase]
        ca, cb = widths(S.shape[-1])
        f_all(phase, h, 2).wait_recv()
        first = UA[h, j, :, span(g, ca, ca)].astype(jnp.float32)
        for k in PEERS:
            first = first + VA[h, other(x, k)].astype(jnp.float32)
        f_all(phase, h, 3).wait_recv()
        second = UB[h, y].astype(jnp.float32)
        for k in PEERS:
            second = second + VB[h, other(y, k)].astype(jnp.float32)
        return first, second

    def ag_start(phase, buf, h):
        ca, cb = widths(buf.shape[-1])
        first = buf.at[h, y, j, 0, :, span(g, ca, ca)]
        second = buf.at[h, y, j, 1, :, span(g, ca, cb)]
        for k in PEERS:
            push(phase, h, 0, first, first, fsdp=y * SIDE + other(x, k))
            push(phase, h, 1, second, second, fsdp=other(y, k) * SIDE + x)

    def ag_mid(phase, buf, h):
        ca, cb = widths(buf.shape[-1])
        first = buf.at[h, y, :, 0]
        f_all(phase, h, 0).wait_recv()
        for k in PEERS:
            push(phase, h, 2, first, first, fsdp=other(y, k) * SIDE + x)
        second = buf.at[h, :, j, 1, :, span(g, ca, cb)]
        f_all(phase, h, 1).wait_recv()
        for k in PEERS:
            push(phase, h, 3, second, second, fsdp=y * SIDE + other(x, k))

    def ag_end(phase, h):
        f_all(phase, h, 2).wait_recv()
        f_all(phase, h, 3).wait_recv()

    def flat(value):
        return value.reshape(-1, value.shape[-1])

    def project(layer, gathered, phase, h):
        S = rs_bufs[phase][0]
        z_all(gathered, X.at[layer], h).wait_recv()
        rows = flat(X[layer, h])
        for gg in (0, 1):
            S[h, :, :, :, :, pl.ds(gg * wide, cols)] = (
                dot(rows, W[layer, gg], NN).astype(jnp.bfloat16).reshape(SIDE, 2, 2, SUB, cols)
            )
        squares = []
        for a in (0, 1):
            part = X[layer, h, :, :, a].astype(jnp.float32)
            squares.append(jnp.sum(part * part, -1, keepdims=True))
        tile = split_tile(*squares)
        for gg in (0, 1):
            S[h, :, :, 0, :, pl.ds(gg * wide + cols, LANES)] = tile
        rs_start(phase, h)

    def attend(layer, phase, h):
        first, second = rs_end(phase, h)
        squares = jnp.concatenate(join_tile(first[:, cols:]), 0)
        inv_rms = lax.rsqrt(squares / MODEL_WIDTH + epsilon)
        rows = (jnp.concatenate([first[:, :cols], second], 0) * inv_rms).astype(jnp.bfloat16)
        ROWS[layer, h] = rows
        INV[layer, h] = jnp.broadcast_to(inv_rms, (SLOT, LANES))
        queries = jnp.concatenate([rows[:, i * HEAD_WIDTH : (i + 1) * HEAD_WIDTH] for i in range(group)], 0)
        keys, values = rows[:, q_wide : q_wide + k_wide], rows[:, q_wide + k_wide :]
        scores = dot(queries, keys, NT) * scale
        scores = jnp.where(doc[h] > 0.5, scores, masked_score)
        raised = jnp.exp(scores - jnp.max(scores, -1, keepdims=True))
        probs = raised / jnp.sum(raised, -1, keepdims=True)
        PROBS[layer, h] = probs
        mixed = dot(probs.astype(jnp.bfloat16), values, NN).astype(jnp.bfloat16)
        for i in range(group):
            H[layer, h, y, j, :, :, span(g, q_wide, HEAD_WIDTH, i * HEAD_WIDTH)] = mixed[
                i * SLOT : (i + 1) * SLOT
            ].reshape(2, SUB, HEAD_WIDTH)

    def head_end(phase, h):
        first, second = rs_end(phase, h)
        HG[h] = jnp.concatenate([first, second], 0).astype(jnp.bfloat16)

    def attend_back(layer, h):
        rows, head_grad, inv_rms, probs = ROWS[layer, h], HG[h], INV[layer, h], PROBS[layer, h]

        def stacked(value):
            return jnp.concatenate(
                [value[:, i * HEAD_WIDTH : (i + 1) * HEAD_WIDTH] for i in range(group)], 0
            )

        queries, grads = stacked(rows), stacked(head_grad)
        keys, values = rows[:, q_wide : q_wide + k_wide], rows[:, q_wide + k_wide :]
        prob_grad = dot(grads, values, NT)
        value_grad = dot(probs.astype(jnp.bfloat16), grads, TN)
        score_grad = probs * (prob_grad - jnp.sum(prob_grad * probs, -1, keepdims=True))
        score_grad = score_grad.astype(jnp.bfloat16)
        query_grad = dot(score_grad, keys, NN) * scale
        key_grad = dot(score_grad, queries, TN) * scale
        total = jnp.zeros((SLOT, LANES), jnp.float32)
        parts = [query_grad[i * SLOT : (i + 1) * SLOT] for i in range(group)] + [key_grad, value_grad]
        for i, part in enumerate(parts):
            part = part.astype(jnp.bfloat16).astype(jnp.float32)
            total = total + part * rows[:, i * HEAD_WIDTH : (i + 1) * HEAD_WIDTH].astype(jnp.float32)
            Q[layer, h, y, j, :, :, span(g, wide, HEAD_WIDTH, i * HEAD_WIDTH)] = (
                (part * inv_rms).astype(jnp.bfloat16).reshape(2, SUB, HEAD_WIDTH)
            )
        share = inv_rms[:, :1] * inv_rms[:, :1] * jnp.sum(total, -1, keepdims=True) / MODEL_WIDTH
        Q[layer, h, y, j, 0, :, span(g, wide, LANES, cols)] = split_tile(share[:SUB], share[SUB:])

    def head_grads(layer, gathered, phase, h):
        S = rs_bufs[phase][0]
        z_all(gathered, G.at[layer], h).wait_recv()
        S[h] = dot(flat(G[layer, h]), WO[layer], NT).astype(jnp.bfloat16).reshape(S.shape[1:])
        rs_start(phase, h)

    def project_out(h):
        ag_end(AG_HEAD0, h)
        D[h] = dot(flat(H[0, h]), WO[0], NN).astype(jnp.bfloat16).reshape(D.shape[1:])
        z_scatter(RS_OUT0, D, E, h)

    def project_back(h):
        ag_end(AG_GRAD1, h)
        back = sum(
            dot(flat(Q[1, h, :, :, :, :, pl.ds(gg * wide, cols)]), W[1, gg], NT) for gg in (0, 1)
        ).reshape(DH.shape[1:])
        tiles = [
            Q[1, h, :, :, 0, :, pl.ds(gg * wide + cols, LANES)].astype(jnp.float32) for gg in (0, 1)
        ]
        shares = join_tile(tiles[0] + tiles[1])
        for a in (0, 1):
            term = back[:, :, a] - X[1, h, :, :, a].astype(jnp.float32) * shares[a]
            DH[h, :, :, a] = term.astype(jnp.bfloat16)
        z_scatter(RS_IN1, DH, EH, h)

    pairs = []

    def hand_over(src, dst):
        i = len(pairs)
        pair = (
            pltpu.make_async_copy(src(core), dst(0), lo.at[i]),
            remote(src(far), dst(1), ss.at[i], sr.at[i], pp=far),
        )
        for c in pair:
            c.start()
        pairs.append(pair)

    loads[0].wait()
    for h in HALVES:
        z_gather(AG_STREAM0, X.at[0], h)
    swaps = [
        remote(
            w.at[0, :, pl.ds(at, width)], W.at[core, gg, :, pl.ds(to, width)], ss.at[16 + i], sr.at[16 + i], pp=far
        )
        for i, (w, at, gg, to, width) in enumerate(cuts)
    ] + [remote(wo.at[0], WO.at[core], ss.at[22], sr.at[22], pp=far)]
    for c in swaps:
        c.start()
    for c in loads[1:]:
        c.wait()
    for c in swaps[:6]:
        c.wait_recv()
    for h in HALVES:
        project(0, AG_STREAM0, RS_QKV0, h)
    for h in HALVES:
        z_gather(AG_TOP, G.at[1], h)
    for h in HALVES:
        rs_mid(RS_QKV0, h)
    for h in HALVES:
        attend(0, RS_QKV0, h)
        ag_start(AG_HEAD0, H.at[0], h)
    for h in HALVES:
        ag_mid(AG_HEAD0, H.at[0], h)
    swaps[6].wait_recv()
    for h in HALVES:
        project_out(h)
    for h in HALVES:
        head_grads(1, AG_TOP, RS_HEAD1, h)
    for h in HALVES:
        X[1, h, t] = z_sum(RS_OUT0, D, E, h, X[0, h, t].astype(jnp.float32))
        z_gather(AG_STREAM1, X.at[1], h)
    for h in HALVES:
        rs_mid(RS_HEAD1, h)
    for h in HALVES:
        project(1, AG_STREAM1, RS_QKV1, h)
    hand_over(lambda m: X.at[m], lambda m: xs_out.at[m])
    for h in HALVES:
        head_end(RS_HEAD1, h)
    for h in HALVES:
        rs_mid(RS_QKV1, h)
    for h in HALVES:
        attend(1, RS_QKV1, h)
        attend_back(1, h)
        ag_start(AG_GRAD1, Q.at[1], h)
    for h in HALVES:
        ag_mid(AG_GRAD1, Q.at[1], h)
    for h in HALVES:
        project_back(h)
    for h in HALVES:
        ag_start(AG_HEAD1, H.at[1], h)
    for h in HALVES:
        G[0, h, t] = z_sum(RS_IN1, DH, EH, h, G[1, h, t].astype(jnp.float32))
        z_gather(AG_OUT0, G.at[0], h)
    for h in HALVES:
        ag_mid(AG_HEAD1, H.at[1], h)
    for h in HALVES:
        head_grads(0, AG_OUT0, RS_HEAD0, h)
    hand_over(lambda m: G.at[m], lambda m: gs_out.at[m])
    for h in HALVES:
        rs_mid(RS_HEAD0, h)
    for h in HALVES:
        ag_end(AG_HEAD1, h)
    hand_over(lambda m: H.at[m], lambda m: hs_out.at[m])
    for h in HALVES:
        head_end(RS_HEAD0, h)
        attend_back(0, h)
        ag_start(AG_GRAD0, Q.at[0], h)
    for h in HALVES:
        ag_mid(AG_GRAD0, Q.at[0], h)
    for h in HALVES:
        ag_end(AG_GRAD0, h)
        for at, width, out in ((0, q_wide, dq_out), (q_wide, k_wide, dk_out), (q_wide + k_wide, k_wide, dv_out)):
            for gg in (0, 1):
                hand_over(
                    lambda m: Q.at[m, h, :, :, :, :, pl.ds(gg * wide + at, width)],
                    lambda m: out.at[m, h, :, :, :, :, pl.ds(gg * width, width)],
                )

    for phase in range(8):
        for h in HALVES:
            for kind in range(4):
                f_all(phase, h, kind).wait_send()
    for phase, buf in (
        (AG_STREAM0, X.at[0]), (AG_TOP, G.at[1]), (RS_OUT0, E),
        (AG_STREAM1, X.at[1]), (RS_IN1, EH), (AG_OUT0, G.at[0]),
    ):
        for h in HALVES:
            z_all(phase, buf, h).wait_send()
    for c in swaps:
        c.wait_send()
    for here, there in pairs:
        here.wait()
        there.wait()


def local(
    inputs,
    head_grad,
    noise_mask,
    lengths,
    rewards,
    groups,
    query_weight,
    key_weight,
    value_weight,
    out_weight,
):
    core, f = lax.axis_index("pp"), lax.axis_index("fsdp")
    row_count, width = inputs.shape[1:]
    q_wide, k_wide = query_weight.shape[2] // 2, key_weight.shape[2] // 2
    cols = q_wide + 2 * k_wide
    wide = cols + LANES
    group = q_wide // k_wide
    y, x = f // SIDE, f % SIDE

    segment = lax.dynamic_slice_in_dim(segments(lengths)[core], y * SIDE, SIDE, 0)
    segment = segment.reshape(2, 2, SLOT)[:, x // 2]
    same_doc = (segment[:, :, None] == segment[:, None, :]).astype(jnp.float32)
    same_doc = jnp.tile(same_doc, (1, group, 1))
    weight = lax.dynamic_slice_in_dim(
        token_weights(lengths, rewards, groups)[core], lax.axis_index("tp") * row_count, row_count, 0
    ) * noise_mask[core].astype(jnp.float32)
    top_grad = (-weight[:, None] * head_grad[core].astype(jnp.float32)).astype(jnp.bfloat16)

    bf16, f32 = jnp.bfloat16, jnp.float32
    any_space = pl.BlockSpec(memory_space=pl.ANY)
    rows = (2, SIDE, 2, 2, SUB)

    def scatter_bufs(ca, cb):
        return [
            pltpu.VMEM(shape, bf16)
            for shape in (
                rows + (2 * ca,),
                (2, SIDE, 2, SUB, 2 * ca),
                (2, SIDE, SIDE, SUB, cb),
                (2, 2, SUB, 2 * ca),
                (2, SIDE, SUB, cb),
                (2, SIDE, SUB, ca),
                (2, SIDE, SUB, cb),
            )
        ]

    results = pl.pallas_call(
        kernel,
        out_shape=[
            jax.ShapeDtypeStruct((2,) + rows + (n,), bf16)
            for n in (width, 2 * q_wide, width, 2 * q_wide, 2 * k_wide, 2 * k_wide)
        ],
        in_specs=[any_space, any_space, pl.BlockSpec(memory_space=pltpu.VMEM)] + [any_space] * 4,
        out_specs=[any_space] * 6,
        scratch_shapes=[
            pltpu.VMEM((2,) + rows + (width,), bf16),
            pltpu.VMEM((2,) + rows + (2 * q_wide,), bf16),
            pltpu.VMEM((2,) + rows + (width,), bf16),
            pltpu.VMEM((2,) + rows + (2 * wide,), bf16),
            pltpu.VMEM((2, 2, width, cols), bf16),
            pltpu.VMEM((2, 2 * q_wide, width), bf16),
            pltpu.VMEM(rows + (width,), bf16),
            pltpu.VMEM(rows + (width,), bf16),
            pltpu.VMEM(rows + (width,), bf16),
            pltpu.VMEM(rows + (width,), bf16),
            pltpu.VMEM((2, 2, SLOT, cols), bf16),
            pltpu.VMEM((2, 2, SLOT, LANES), f32),
            pltpu.VMEM((2, 2, group * SLOT, SLOT), f32),
            pltpu.VMEM((2, SLOT, q_wide), bf16),
        ]
        + scatter_bufs(wide, cols) * 2
        + scatter_bufs(q_wide, q_wide) * 2
        + [
            pltpu.SemaphoreType.DMA((8, 2, 4)),
            pltpu.SemaphoreType.DMA((8, 2, 4)),
            pltpu.SemaphoreType.DMA((6, 2)),
            pltpu.SemaphoreType.DMA((6, 2)),
            pltpu.SemaphoreType.DMA((23,)),
            pltpu.SemaphoreType.DMA((23,)),
            pltpu.SemaphoreType.DMA((9,)),
            pltpu.SemaphoreType.DMA((15,)),
        ],
        compiler_params=pltpu.CompilerParams(
            collective_id=0, has_side_effects=True, vmem_limit_bytes=56 * 1024 * 1024
        ),
    )(
        inputs.reshape(2, 2, 2, 2, SUB, width),
        top_grad.reshape(2, 2, 2, SUB, width),
        same_doc,
        query_weight,
        key_weight,
        value_weight,
        out_weight,
    )
    streams, heads, out_grads, query_grads, key_grads, value_grads = (
        r.reshape(-1, r.shape[-1]) for r in results
    )

    def weight_grad(a, b):
        return dot(a, b, TN)[None]

    return (
        weight_grad(streams, query_grads),
        weight_grad(streams, key_grads),
        weight_grad(streams, value_grads),
        weight_grad(heads, out_grads),
    )


def solution(mesh):
    return jax.shard_map(
        local,
        mesh=mesh,
        in_specs=(
            P(None, "tp", "fsdp"),
            P(None, "tp", "fsdp"),
            P(None, "tp"),
            P(),
            P(),
            P(),
            P("pp", "fsdp", "tp"),
            P("pp", "fsdp", "tp"),
            P("pp", "fsdp", "tp"),
            P("pp", "tp", "fsdp"),
        ),
        out_specs=(
            P("pp", "fsdp", "tp"),
            P("pp", "fsdp", "tp"),
            P("pp", "fsdp", "tp"),
            P("pp", "tp", "fsdp"),
        ),
        check_vma=False,
    )
```

time: 621 us -> 130 us (0.21)
  waiting for transfers between devices: 444 us -> 0 us
  Pallas kernels: 0 us -> 111 us
  blocking collectives: 93.9 us -> 0 us
  other arithmetic: 23.2 us -> 2.98 us
  matrix products: 28.9 us -> 9.75 us
  between operations: 15.5 us -> 0.86 us
  local copies, waits for them, and re-layouts: 11.8 us -> 4.42 us
    reduce_scatter x6 -> x0, waiting for transfers between devices: 315 us -> none  [scatter(): return lax.psum_scatter(value, axis, scatter_dimension=0, tiled=True)]
    all_gather x4 -> x0, waiting for transfers between devices: 125 us -> none  [gather(): return lax.all_gather(value, axis, axis=0, tiled=True)]
    pallas_call x0 -> x1, Pallas kernels: none -> 111 us  [local(): pl.pallas_call(kernel, out_shape=[jax.ShapeDtypeStruct((2,) + rows + (n,)...]
    all_gather x4 -> x0, blocking collectives: 55.8 us -> none  [gather(): return lax.all_gather(value, axis, axis=0, tiled=True)]
    unnamed x1 -> x0, blocking collectives: 38.1 us -> none
    dot_general x8 -> x4, matrix products: 21.8 us -> 9.75 us  [dot(): lax.dot_general(a, b, (contract, ((), ())), preferred_element_type=jnp.fl...]
    convert_element_type x9 -> x1, other arithmetic: 7.59 us -> 0.07 us  [local(): same_doc = (segment[:, :, None] == segment[:, None, :]).astype(jnp.float32)]
  transfers between devices with their start and end apart: 16 -> 0, of which waited for: 13 -> 0; matrix products, arithmetic and copies ran while one was open for 4% -> 0% of each run, Pallas kernels for 0% -> 0%
where the time goes in v3:
time: 130 us; the launch traced here: 129 us
  Pallas kernels  111 us (85%)
  matrix products  9.75 us (8%)
  local copies, waits for them, and re-layouts  4.42 us (3%)
  other arithmetic  2.98 us (2%)
    pallas_call x1, Pallas kernels, local(): pl.pallas_call(kernel, out_shape=[jax.ShapeDtypeStruct((2,) + rows + (n,)...  111 us
    dot_general x4, matrix products, dot(): lax.dot_general(a, b, (contract, ((), ())), preferred_element_type=jnp.fl...  9.75 us

profile of v3, /device:TPU:0, one launch (start us, length us, event | category | flops | bytes accessed | tf_op | source)
XLA Modules:
  0.0 128.9 jit_solution(11265613947959359367)
XLA Ops:
  0.6 0.0 copy-start
  0.7 0.7 slice.4
  1.4 0.8 fusion.5
  2.2 0.1 convert_reduce_fusion
  2.3 0.8 copy.26
  3.1 0.1 convert_element_type.55
  3.2 0.8 copy.27
  4.0 0.1 eq.52
  4.1 0.1 convert_reduce_fusion.1
  4.2 0.1 select_reduce_fusion.4
  4.3 0.1 select_reduce_fusion.3
  4.4 0.1 select_reduce_fusion.2
  4.6 0.1 max.13
  4.7 0.1 reduce_sum.104
  4.8 0.1 copy.28
  4.9 0.1 select_reduce_fusion.1
  5.0 0.1 div.45
  5.1 0.8 fusion.4
  5.8 0.1 neg.12
  5.9 0.1 compare_convert_fusion
  6.0 0.7 tile.4
  6.7 0.0 copy-done
  6.7 0.7 fusion.g_in
  7.4 110.9 %shard_map.129 = (bf16[2,2,4,2,2,16,512]{6,5,4,3,2,1,0:T(8,128)(2,1)}, bf16[2,2,4,2,2,16,1024]{6,5,4,3,2,1,0:T(8,128)(2,1)}, bf16[2,2,4,2,2,16,512]{6,5,4,3,2,1,...) custom-call(bf16[2,2,2,2,16,512]{5,4,3,2,1,0:T(8,128)(2,1)} %bitcast, ...), custom_call_target="tpu_custom_call" | custom-call | tf_op jit(solution)/shard_map/pallas_call | solution.py:491
  118.4 0.0 copy-start.1
  118.4 0.0 copy-start.5
  118.4 4.6 %convolution_bitcast_fusion.1 = f32[1,512,1024]{2,1,0:T(8,128)} fusion(bf16[2,2,4,2,2,16,512]{6,5,4,3,2,1,0:T(8,128)(2,1)} %get-tuple-element.10, bf16[2,2,4,2,2,16,1024]{6,5,4,3,2,1,0:T(8,128)(2,1)} %get-tuple-element.11), kind=kOutput, calls=%fused_computation.1 | convolution fusion | flops 1073741824 | bytes 5242880 | tf_op jit(solution)/shard_map/dot_general | solution.py:49
  123.0 0.0 copy-done.1
  123.0 0.0 copy-done.5
  123.0 0.0 copy-start.4
  123.0 1.3 convolution_bitcast_fusion.3
  124.3 0.0 copy-done.4
  124.3 0.0 copy-start.2
  124.3 0.0 copy-start.3
  124.3 1.3 convolution_bitcast_fusion.2
  125.5 0.5 copy-done.2
  126.1 0.3 copy-done.3
  126.3 2.6 %convolution_bitcast_fusion = f32[1,1024,512]{2,1,0:T(8,128)} fusion(bf16[2,2,4,2,2,16,1024]{6,5,4,3,2,1,0:T(8,128)(2,1)S(1)} %copy-done.2, bf16[2,2,4,2,2,16,512]{6,5,4,3,2,1,0:T(8,128)(2,1)S(1)} %copy-done.3), kind=kOutput, calls=%fused_computation | convolution fusion | flops 1073741824 | bytes 5242880 | tf_op jit(solution)/shard_map/dot_general | solution.py:49
  (12 shorter events, 0.1 us)
Async XLA Ops:
  0.6 6.1 %copy-start = (bf16[2,128,512]{2,1,0:T(8,128)(2,1)S(1)}, bf16[2,128,512]{2,1,0:T(8,128)(2,1)}, u32[]{:S(2)}) copy-start(bf16[2,128,512]{2,1,0:T(8,128)(2,1)} %param.11) | copy-start | bytes 786436
  118.4 4.6 %copy-start.1 = (bf16[2,2,4,2,2,16,512]{6,5,4,3,2,1,0:T(8,128)(2,1)S(1)}, bf16[2,2,4,2,2,16,512]{6,5,4,3,2,1,0:T(8,128)(2,1)}, u32[]{:S(2)}) copy-start(bf16[2,2,4,2,2,16,512]{6,5,4,3,2,1,0:T(8,128)(2,1)} %get-tuple-element.10) | copy-start | bytes 3145732
  118.4 4.6 %copy-start.5 = (bf16[2,2,4,2,2,16,256]{6,5,4,3,2,1,0:T(8,128)(2,1)S(1)}, bf16[2,2,4,2,2,16,256]{6,5,4,3,2,1,0:T(8,128)(2,1)}, u32[]{:S(2)}) copy-start(bf16[2,2,4,2,2,16,256]{6,5,4,3,2,1,0:T(8,128)(2,1)} %get-tuple-element.12) | copy-start | bytes 1572868
  123.0 1.3 copy-start.4
  124.3 1.8 %copy-start.2 = (bf16[2,2,4,2,2,16,1024]{6,5,4,3,2,1,0:T(8,128)(2,1)S(1)}, bf16[2,2,4,2,2,16,1024]{6,5,4,3,2,1,0:T(8,128)(2,1)}, u32[]{:S(2)}) copy-start(bf16[2,2,4,2,2,16,1024]{6,5,4,3,2,1,0:T(8,128)(2,1)} %get-tuple-element.14) | copy-start | bytes 6291460
  124.3 2.0 %copy-start.3 = (bf16[2,2,4,2,2,16,512]{6,5,4,3,2,1,0:T(8,128)(2,1)S(1)}, bf16[2,2,4,2,2,16,512]{6,5,4,3,2,1,0:T(8,128)(2,1)}, u32[]{:S(2)}) copy-start(bf16[2,2,4,2,2,16,512]{6,5,4,3,2,1,0:T(8,128)(2,1)} %get-tuple-element.15) | copy-start | bytes 3145732

commit v4 on v3

--- a/solution.py
+++ b/solution.py
@@ -18,38 +18,11 @@
 TN = ((0,), (0,))
 
 
-def segments(lengths):
-    ends = jnp.stack([jnp.sum(lengths[..., : c + 1], -1) for c in range(lengths.shape[-1])], -1)
-    position = jnp.arange(SLOT, dtype=jnp.int32)
-    return jnp.sum((ends[..., None, :] <= position[:, None]).astype(jnp.int32), -1)
-
-
-def token_weights(lengths, rewards, groups):
-    group_total = 2 * lengths.shape[1]
-    reward_flat = rewards.reshape(-1).astype(jnp.float32)
-    member = (
-        groups.reshape(-1)[:, None] == jnp.arange(group_total, dtype=jnp.int32)[None, :]
-    ).astype(jnp.float32)
-    member_count = jnp.sum(member, 0)
-    group_mean = jnp.sum(member * reward_flat[:, None], 0) / member_count
-    centered = reward_flat - jnp.sum(member * group_mean[None, :], 1)
-    variance = jnp.sum(member * (centered * centered)[:, None], 0) / member_count
-    spread_own = jnp.sum(member * jnp.sqrt(variance)[None, :], 1)
-    advantage = (centered / jnp.maximum(spread_own, 1.0)).reshape(lengths.shape)
-    segment = segments(lengths)
-    choose = (segment[..., None] == jnp.arange(lengths.shape[2], dtype=jnp.int32)).astype(
-        jnp.float32
-    )
-    token_adv = jnp.sum(choose * advantage[:, :, None, :], -1)
-    token_len = jnp.sum(choose * lengths[:, :, None, :].astype(jnp.float32), -1)
-    return (token_adv * SLOT / token_len).reshape(lengths.shape[0], -1)
-
-
 def dot(a, b, contract):
     return lax.dot_general(a, b, (contract, ((), ())), preferred_element_type=jnp.float32)
 
 
-RS_QKV0, RS_QKV1, RS_HEAD1, RS_HEAD0, AG_HEAD0, AG_GRAD1, AG_HEAD1, AG_GRAD0 = range(8)
+RS_QKV0, RS_QKV1, RS_HEAD1, RS_HEAD0, AG_HEAD0, AG_GRAD1, AG_HEAD1, AG_GRAD0, AG_FAR0 = range(9)
 AG_STREAM0, AG_TOP, RS_OUT0, AG_STREAM1, RS_IN1, AG_OUT0 = range(6)
 HALVES = (0, 1)
 PEERS = (2, 1, 3)
@@ -71,10 +44,43 @@
     return tile[..., 0:1] + tile[..., 1:2], tile[..., 2:3] + tile[..., 3:4]
 
 
+def token_weights(lengths, rewards, groups, noise, core, t):
+    square = (LANES, LANES)
+    micros, packed, slots = lengths.shape
+    lane = lax.broadcasted_iota(jnp.int32, (1, LANES), 1)
+
+    def row(ref):
+        value = jnp.full((1, LANES), -1, jnp.int32)
+        for m in range(micros):
+            for s in range(slots):
+                for c in range(packed):
+                    value = jnp.where(lane == (m * slots + s) * packed + c, ref[m, c, s], value)
+        return jnp.broadcast_to(value.astype(jnp.float32), square)
+
+    group_row, reward_row, length_row = row(groups), row(rewards), row(lengths)
+    member = (group_row == group_row.T).astype(jnp.float32)
+    reward_column = reward_row.T
+    count = jnp.sum(member, 0, keepdims=True)
+    mean = jnp.sum(member * reward_column, 0, keepdims=True) / count
+    centered = reward_column - mean
+    variance = jnp.sum(member * centered * centered, 0, keepdims=True) / count
+    advantage = (reward_row - mean) / jnp.maximum(jnp.sqrt(variance), 1.0)
+    token = lax.broadcasted_iota(jnp.int32, square, 0)
+    lanes = lax.broadcasted_iota(jnp.int32, square, 1)
+    first = core * slots * packed + (t * (LANES // SLOT) + (token >> 5)) * packed
+    length = jnp.sum(jnp.where(lanes == first, length_row, 0.0), -1, keepdims=True)
+    position = (token & (SLOT - 1)).astype(jnp.float32)
+    chosen = lanes == first + (position >= length).astype(jnp.int32)
+    advantage = jnp.sum(jnp.where(chosen, advantage, 0.0), -1, keepdims=True)
+    length = jnp.sum(jnp.where(chosen, length_row, 0.0), -1, keepdims=True)
+    noise = jnp.broadcast_to(noise[pl.ds(core, 1), :].astype(jnp.float32), square).T
+    return advantage * SLOT / length * noise[:, :1]
+
+
 def kernel(
-    x_in, g_in, doc, wq, wk, wv, wo,
-    xs_out, hs_out, gs_out, dq_out, dk_out, dv_out,
-    X, H, G, Q, W, WO, D, E, DH, EH, ROWS, INV, PROBS, HG, *rest,
+    x_in, g_in, noise, lengths, rewards, groups, wq, wk, wv, wo,
+    dq_out, dk_out, dv_out, do_out,
+    X, H, G, Q, FX, FH, FG, FQ, W, WO, DW, DWO, D, E, DH, EH, ROWS, INV, PROBS, HG, GIN, *rest,
 ):
     scatter_bufs, (fs, fr, zs, zr, ss, sr, ls, lo) = rest[:28], rest[28:]
     rs_bufs = {
@@ -117,7 +123,7 @@
     ]
     loads += [
         pltpu.make_async_copy(wo.at[0], WO.at[core], ls.at[7]),
-        pltpu.make_async_copy(g_in, G.at[1, :, t], ls.at[8]),
+        pltpu.make_async_copy(g_in.at[core], GIN, ls.at[8]),
     ]
     for c in loads:
         c.start()
@@ -127,11 +133,13 @@
         for at in (
             {"fsdp": y * SIDE + other(x, k)},
             {"fsdp": other(y, k) * SIDE + x},
+            {"pp": far, "fsdp": y * SIDE + other(x, k)},
+            {"pp": far, "fsdp": other(y, k) * SIDE + x},
             {"tp": other(t, k)},
         ):
             pl.semaphore_signal(barrier, inc=1, device_id=at, device_id_type=MESH)
     pl.semaphore_signal(barrier, inc=1, device_id={"pp": far}, device_id_type=MESH)
-    pl.semaphore_wait(barrier, 10)
+    pl.semaphore_wait(barrier, 16)
 
     def z_gather(phase, buf, h):
         for k in PEERS:
@@ -230,6 +238,37 @@
         f_all(phase, h, 1).wait_recv()
         for k in PEERS:
             push(phase, h, 3, second, second, fsdp=y * SIDE + other(x, k))
+
+    def last_mid(h):
+        first, second = Q.at[0, h, y, :, 0], Q.at[0, h, :, j, 1, :, span(g, wide, cols)]
+        first_far, second_far = FQ.at[h, y, :, 0], FQ.at[h, :, j, 1, :, span(g, wide, cols)]
+        f_all(AG_GRAD0, h, 0).wait_recv()
+
+        @pl.when(core == 0)
+        def _():
+            for k in PEERS:
+                push(AG_GRAD0, h, 2, first, first, fsdp=other(y, k) * SIDE + x)
+
+        @pl.when(core == 1)
+        def _():
+            for k in PEERS + (0,):
+                push(AG_FAR0, h, 2, first, first_far, pp=far, fsdp=other(y, k) * SIDE + x)
+
+        f_all(AG_GRAD0, h, 1).wait_recv()
+
+        @pl.when(core == 0)
+        def _():
+            for k in PEERS:
+                push(AG_GRAD0, h, 3, second, second, fsdp=y * SIDE + other(x, k))
+
+        @pl.when(core == 1)
+        def _():
+            for k in PEERS + (0,):
+                push(AG_FAR0, h, 3, second, second_far, pp=far, fsdp=y * SIDE + other(x, k))
+
+    def far_all(h, kind):
+        four = rs_bufs[RS_QKV0][1 + (kind - 2)].at[h]
+        return remote(four, four, fs.at[AG_FAR0, h, kind], fr.at[AG_FAR0, h, kind], fsdp=f)
 
     def ag_end(phase, h):
         f_all(phase, h, 2).wait_recv()
@@ -265,7 +304,12 @@
         queries = jnp.concatenate([rows[:, i * HEAD_WIDTH : (i + 1) * HEAD_WIDTH] for i in range(group)], 0)
         keys, values = rows[:, q_wide : q_wide + k_wide], rows[:, q_wide + k_wide :]
         scores = dot(queries, keys, NT) * scale
-        scores = jnp.where(doc[h] > 0.5, scores, masked_score)
+        cut = lengths[core, 0, y * SIDE + 2 * h + j]
+        later = [
+            ((lax.broadcasted_iota(jnp.int32, scores.shape, d) & (SLOT - 1)) >= cut).astype(jnp.int32)
+            for d in (0, 1)
+        ]
+        scores = jnp.where(later[0] == later[1], scores, masked_score)
         raised = jnp.exp(scores - jnp.max(scores, -1, keepdims=True))
         probs = raised / jnp.sum(raised, -1, keepdims=True)
         PROBS[layer, h] = probs
@@ -331,30 +375,46 @@
             DH[h, :, :, a] = term.astype(jnp.bfloat16)
         z_scatter(RS_IN1, DH, EH, h)
 
-    pairs = []
-
-    def hand_over(src, dst):
-        i = len(pairs)
-        pair = (
-            pltpu.make_async_copy(src(core), dst(0), lo.at[i]),
-            remote(src(far), dst(1), ss.at[i], sr.at[i], pp=far),
-        )
-        for c in pair:
-            c.start()
-        pairs.append(pair)
+    def hand_over(i, src, dst):
+        return remote(src, dst, ss.at[i], sr.at[i], pp=far)
+
+    x_far, h_far, g_far = hand_over(7, X.at[far], FX), hand_over(8, H.at[far], FH), hand_over(9, G.at[far], FG)
+    q_far = hand_over(10, Q.at[1], FQ)
+    stores = []
+
+    def store(src, dst):
+        c = pltpu.make_async_copy(src, dst, lo.at[len(stores)])
+        c.start()
+        stores.append(c)
+
+    def weight_grads(h):
+        rows, far_rows = flat(X[core, h]), flat(FX[h])
+        for gg in (0, 1):
+            at = pl.ds(gg * wide, cols)
+            term = dot(rows, flat(Q[core, h, :, :, :, :, at]), TN) + dot(
+                far_rows, flat(FQ[h, :, :, :, :, at]), TN
+            )
+            DW[gg] = term if h == 0 else DW[gg] + term
+            if h == 1:
+                for to, width, out in ((0, q_wide, dq_out), (q_wide, k_wide, dk_out), (q_wide + k_wide, k_wide, dv_out)):
+                    store(DW.at[gg, :, pl.ds(to, width)], out.at[0, :, pl.ds(gg * width, width)])
 
     loads[0].wait()
     for h in HALVES:
         z_gather(AG_STREAM0, X.at[0], h)
     swaps = [
         remote(
-            w.at[0, :, pl.ds(at, width)], W.at[core, gg, :, pl.ds(to, width)], ss.at[16 + i], sr.at[16 + i], pp=far
+            w.at[0, :, pl.ds(at, width)], W.at[core, gg, :, pl.ds(to, width)], ss.at[i], sr.at[i], pp=far
         )
         for i, (w, at, gg, to, width) in enumerate(cuts)
-    ] + [remote(wo.at[0], WO.at[core], ss.at[22], sr.at[22], pp=far)]
+    ] + [remote(wo.at[0], WO.at[core], ss.at[6], sr.at[6], pp=far)]
     for c in swaps:
         c.start()
-    for c in loads[1:]:
+    loads[8].wait()
+    top = token_weights(lengths, rewards, groups, noise, core, t)
+    top = (-top * flat(GIN[...]).astype(jnp.float32)).astype(jnp.bfloat16)
+    G[1, :, t] = top.reshape(GIN.shape)
+    for c in loads[1:8]:
         c.wait()
     for c in swaps[:6]:
         c.wait_recv()
@@ -381,7 +441,7 @@
         rs_mid(RS_HEAD1, h)
     for h in HALVES:
         project(1, AG_STREAM1, RS_QKV1, h)
-    hand_over(lambda m: X.at[m], lambda m: xs_out.at[m])
+    x_far.start()
     for h in HALVES:
         head_end(RS_HEAD1, h)
     for h in HALVES:
@@ -394,6 +454,11 @@
         ag_mid(AG_GRAD1, Q.at[1], h)
     for h in HALVES:
         project_back(h)
+
+    @pl.when(core == 0)
+    def _():
+        q_far.start()
+
     for h in HALVES:
         ag_start(AG_HEAD1, H.at[1], h)
     for h in HALVES:
@@ -403,42 +468,72 @@
         ag_mid(AG_HEAD1, H.at[1], h)
     for h in HALVES:
         head_grads(0, AG_OUT0, RS_HEAD0, h)
-    hand_over(lambda m: G.at[m], lambda m: gs_out.at[m])
+    g_far.start()
+    for h in HALVES:
+        ag_end(AG_HEAD1, h)
+    h_far.start()
+    DWO[...] = dot(flat(H[core]), flat(G[core]), TN)
     for h in HALVES:
         rs_mid(RS_HEAD0, h)
-    for h in HALVES:
-        ag_end(AG_HEAD1, h)
-    hand_over(lambda m: H.at[m], lambda m: hs_out.at[m])
     for h in HALVES:
         head_end(RS_HEAD0, h)
         attend_back(0, h)
         ag_start(AG_GRAD0, Q.at[0], h)
     for h in HALVES:
-        ag_mid(AG_GRAD0, Q.at[0], h)
-    for h in HALVES:
-        ag_end(AG_GRAD0, h)
-        for at, width, out in ((0, q_wide, dq_out), (q_wide, k_wide, dk_out), (q_wide + k_wide, k_wide, dv_out)):
-            for gg in (0, 1):
-                hand_over(
-                    lambda m: Q.at[m, h, :, :, :, :, pl.ds(gg * wide + at, width)],
-                    lambda m: out.at[m, h, :, :, :, :, pl.ds(gg * width, width)],
-                )
-
-    for phase in range(8):
+        last_mid(h)
+    for c in (x_far, h_far, g_far):
+        c.wait_recv()
+    DWO[...] += dot(flat(FH[...]), flat(FG[...]), TN)
+    store(DWO, do_out.at[0])
+    for h in HALVES:
+
+        @pl.when(core == 0)
+        def _():
+            ag_end(AG_GRAD0, h)
+            far_all(h, 2).wait_recv()
+            far_all(h, 3).wait_recv()
+
+        if h == 0:
+
+            @pl.when(core == 1)
+            def _():
+                q_far.wait_recv()
+
+        weight_grads(h)
+
+    for phase in range(AG_GRAD0):
         for h in HALVES:
             for kind in range(4):
                 f_all(phase, h, kind).wait_send()
+    for h in HALVES:
+        for kind in (0, 1):
+            f_all(AG_GRAD0, h, kind).wait_send()
+
+        @pl.when(core == 0)
+        def _():
+            for kind in (2, 3):
+                f_all(AG_GRAD0, h, kind).wait_send()
+
+        @pl.when(core == 1)
+        def _():
+            for kind in (2, 3):
+                far_all(h, kind).wait_send()
+
     for phase, buf in (
         (AG_STREAM0, X.at[0]), (AG_TOP, G.at[1]), (RS_OUT0, E),
         (AG_STREAM1, X.at[1]), (RS_IN1, EH), (AG_OUT0, G.at[0]),
     ):
         for h in HALVES:
             z_all(phase, buf, h).wait_send()
-    for c in swaps:
+    for c in swaps + [x_far, h_far, g_far]:
         c.wait_send()
-    for here, there in pairs:
-        here.wait()
-        there.wait()
+
+    @pl.when(core == 0)
+    def _():
+        q_far.wait_send()
+
+    for c in stores:
+        c.wait()
 
 
 def local(
@@ -453,22 +548,11 @@
     value_weight,
     out_weight,
 ):
-    core, f = lax.axis_index("pp"), lax.axis_index("fsdp")
     row_count, width = inputs.shape[1:]
     q_wide, k_wide = query_weight.shape[2] // 2, key_weight.shape[2] // 2
     cols = q_wide + 2 * k_wide
     wide = cols + LANES
     group = q_wide // k_wide
-    y, x = f // SIDE, f % SIDE
-
-    segment = lax.dynamic_slice_in_dim(segments(lengths)[core], y * SIDE, SIDE, 0)
-    segment = segment.reshape(2, 2, SLOT)[:, x // 2]
-    same_doc = (segment[:, :, None] == segment[:, None, :]).astype(jnp.float32)
-    same_doc = jnp.tile(same_doc, (1, group, 1))
-    weight = lax.dynamic_slice_in_dim(
-        token_weights(lengths, rewards, groups)[core], lax.axis_index("tp") * row_count, row_count, 0
-    ) * noise_mask[core].astype(jnp.float32)
-    top_grad = (-weight[:, None] * head_grad[core].astype(jnp.float32)).astype(jnp.bfloat16)
 
     bf16, f32 = jnp.bfloat16, jnp.float32
     any_space = pl.BlockSpec(memory_space=pl.ANY)
@@ -488,21 +572,29 @@
             )
         ]
 
-    results = pl.pallas_call(
+    return pl.pallas_call(
         kernel,
         out_shape=[
-            jax.ShapeDtypeStruct((2,) + rows + (n,), bf16)
-            for n in (width, 2 * q_wide, width, 2 * q_wide, 2 * k_wide, 2 * k_wide)
+            jax.ShapeDtypeStruct(w.shape, f32)
+            for w in (query_weight, key_weight, value_weight, out_weight)
         ],
-        in_specs=[any_space, any_space, pl.BlockSpec(memory_space=pltpu.VMEM)] + [any_space] * 4,
-        out_specs=[any_space] * 6,
+        in_specs=[any_space, any_space, pl.BlockSpec(memory_space=pltpu.VMEM)]
+        + [pl.BlockSpec(memory_space=pltpu.SMEM)] * 3
+        + [any_space] * 4,
+        out_specs=[any_space] * 4,
         scratch_shapes=[
             pltpu.VMEM((2,) + rows + (width,), bf16),
             pltpu.VMEM((2,) + rows + (2 * q_wide,), bf16),
             pltpu.VMEM((2,) + rows + (width,), bf16),
             pltpu.VMEM((2,) + rows + (2 * wide,), bf16),
+            pltpu.VMEM(rows + (width,), bf16),
+            pltpu.VMEM(rows + (2 * q_wide,), bf16),
+            pltpu.VMEM(rows + (width,), bf16),
+            pltpu.VMEM(rows + (2 * wide,), bf16),
             pltpu.VMEM((2, 2, width, cols), bf16),
             pltpu.VMEM((2, 2 * q_wide, width), bf16),
+            pltpu.VMEM((2, width, cols), f32),
+            pltpu.VMEM((2 * q_wide, width), f32),
             pltpu.VMEM(rows + (width,), bf16),
             pltpu.VMEM(rows + (width,), bf16),
             pltpu.VMEM(rows + (width,), bf16),
@@ -511,43 +603,32 @@
             pltpu.VMEM((2, 2, SLOT, LANES), f32),
             pltpu.VMEM((2, 2, group * SLOT, SLOT), f32),
             pltpu.VMEM((2, SLOT, q_wide), bf16),
+            pltpu.VMEM((2, 2, 2, SUB, width), bf16),
         ]
         + scatter_bufs(wide, cols) * 2
         + scatter_bufs(q_wide, q_wide) * 2
         + [
-            pltpu.SemaphoreType.DMA((8, 2, 4)),
-            pltpu.SemaphoreType.DMA((8, 2, 4)),
+            pltpu.SemaphoreType.DMA((9, 2, 4)),
+            pltpu.SemaphoreType.DMA((9, 2, 4)),
             pltpu.SemaphoreType.DMA((6, 2)),
             pltpu.SemaphoreType.DMA((6, 2)),
-            pltpu.SemaphoreType.DMA((23,)),
-            pltpu.SemaphoreType.DMA((23,)),
+            pltpu.SemaphoreType.DMA((11,)),
+            pltpu.SemaphoreType.DMA((11,)),
             pltpu.SemaphoreType.DMA((9,)),
-            pltpu.SemaphoreType.DMA((15,)),
+            pltpu.SemaphoreType.DMA((7,)),
         ],
         compiler_params=pltpu.CompilerParams(
             collective_id=0, has_side_effects=True, vmem_limit_bytes=56 * 1024 * 1024
         ),
     )(
         inputs.reshape(2, 2, 2, 2, SUB, width),
-        top_grad.reshape(2, 2, 2, SUB, width),
-        same_doc,
+        head_grad.reshape(2, 2, 2, 2, SUB, width),
+        noise_mask,
+        *(jnp.swapaxes(v, 1, 2) for v in (lengths, rewards, groups)),
         query_weight,
         key_weight,
         value_weight,
         out_weight,
-    )
-    streams, heads, out_grads, query_grads, key_grads, value_grads = (
-        r.reshape(-1, r.shape[-1]) for r in results
-    )
-
-    def weight_grad(a, b):
-        return dot(a, b, TN)[None]
-
-    return (
-        weight_grad(streams, query_grads),
-        weight_grad(streams, key_grads),
-        weight_grad(streams, value_grads),
-        weight_grad(heads, out_grads),
     )
 
 

time: 130 us -> 119 us (0.915)
  matrix products: 9.75 us -> 0 us
  other arithmetic: 2.98 us -> 0 us
  local copies, waits for them, and re-layouts: 4.42 us -> 6.23 us
    dot_general x4 -> x0, matrix products: 9.75 us -> none  [dot(): lax.dot_general(a, b, (contract, ((), ())), preferred_element_type=jnp.fl...]
    unnamed x14 -> x10, local copies, waits for them, and re-layouts: 2.33 us -> 6.23 us
    convert_element_type x4 -> x0, other arithmetic: 1.59 us -> none  [the longest x1 0.77 us: token_weights(): token_len = jnp.sum(choose * lengths[:, :, None, :].astype(jnp.float32), -1)]
where the time goes in v4:
time: 119 us
  Pallas kernels  112 us (94%)
  local copies, waits for them, and re-layouts  6.23 us (5%)
    pallas_call x1, Pallas kernels, local(): pl.pallas_call(kernel, out_shape=[jax.ShapeDtypeStruct(w.shape, f32) for...  112 us
    unnamed x10, local copies, waits for them, and re-layouts  6.23 us

profile of v4, /device:TPU:0, one launch (start us, length us, event | category | flops | bytes accessed | tf_op | source)
XLA Modules:
  0.0 118.6 jit_solution(17290382518448297592)
XLA Ops:
  0.6 111.7 %shard_map.129 = (f32[1,512,1024]{2,1,0:T(8,128)}, f32[1,512,256]{2,1,0:T(8,128)}, f32[1,512,256]{2,1,0:T(8,128)}, f32[1,1024,512]{2,1,0:T(8,128)}) custom-call(bf16[2,2,2,2,16,512]{5,4,3,2,1,0:T(8,128)(2,1)} %bitcast.5, bf16[2,2,2,2,16,512]{5,4,3,2,1,0:T(8,128)(2,1)} %bitcast.6, s32[2,128]{1,0:T(2,128)} %noise.1, s32[2,2,16]{2,1,0:T(2,128)} %bitcast.7, ...), custom_call_target="tpu_custom_call" | custom-call | tf_op jit(solution)/shard_map/pallas_call | solution.py:575
  112.3 0.0 copy-start.2
  112.3 0.0 copy-start.1
  112.3 0.0 copy-start
  112.3 3.3 %copy.18 = f32[1,512,1024]{2,1,0:T(8,128)} copy(f32[1,512,1024]{2,1,0:T(8,128)} %get-tuple-element.8) | data formatting | bytes 4194304
  115.7 0.0 copy-done.2
  115.7 0.8 copy.19
  116.5 0.0 copy-done.1
  116.5 0.8 copy.20
  117.3 0.0 copy-done
  117.3 1.3 %copy.21 = f32[1,1024,512]{2,1,0:T(8,128)} copy(f32[1,1024,512]{2,1,0:T(8,128)S(1)} %copy-done) | data formatting | bytes 4194304
Async XLA Ops:
  112.3 3.3 %copy-start.2 = (f32[1,512,256]{2,1,0:T(8,128)S(1)}, f32[1,512,256]{2,1,0:T(8,128)}, u32[]{:S(2)}) copy-start(f32[1,512,256]{2,1,0:T(8,128)} %get-tuple-element.9) | copy-start | bytes 1572868
  112.3 4.1 %copy-start.1 = (f32[1,512,256]{2,1,0:T(8,128)S(1)}, f32[1,512,256]{2,1,0:T(8,128)}, u32[]{:S(2)}) copy-start(f32[1,512,256]{2,1,0:T(8,128)} %get-tuple-element.10) | copy-start | bytes 1572868
  112.3 4.9 %copy-start = (f32[1,1024,512]{2,1,0:T(8,128)S(1)}, f32[1,1024,512]{2,1,0:T(8,128)}, u32[]{:S(2)}) copy-start(f32[1,1024,512]{2,1,0:T(8,128)} %get-tuple-element.11) | copy-start | bytes 6291460

commit v5 on v4

--- a/solution.py
+++ b/solution.py
@@ -80,17 +80,17 @@
 def kernel(
     x_in, g_in, noise, lengths, rewards, groups, wq, wk, wv, wo,
     dq_out, dk_out, dv_out, do_out,
-    X, H, G, Q, FX, FH, FG, FQ, W, WO, DW, DWO, D, E, DH, EH, ROWS, INV, PROBS, HG, GIN, *rest,
+    X, H, G, Q, FX, FH, FG, FQ, W, WO, D, E, DH, EH, ROWS, INV, PROBS, HG, GIN, *rest,
 ):
-    scatter_bufs, (fs, fr, zs, zr, ss, sr, ls, lo) = rest[:28], rest[28:]
+    scatter_bufs, (fs, fr, zs, zr, ss, sr, ls) = rest[:28], rest[28:]
     rs_bufs = {
         phase: scatter_bufs[7 * i : 7 * i + 7]
         for i, phase in enumerate((RS_QKV0, RS_QKV1, RS_HEAD1, RS_HEAD0))
     }
     core, f, t = lax.axis_index("pp"), lax.axis_index("fsdp"), lax.axis_index("tp")
     far = 1 - core
-    y, x = f // SIDE, f % SIDE
-    j, g = x // 2, x % 2
+    y, x = f >> 2, f & 3
+    j, g = x >> 1, x & 1
     q_wide = wq.shape[2] // 2
     k_wide = wk.shape[2] // 2
     cols = q_wide + 2 * k_wide
@@ -102,7 +102,7 @@
         return pl.ds(pl.multiple_of(which * stride + at, LANES), width)
 
     def other(mine, k):
-        return lax.rem(mine + k, SIDE)
+        return (mine + k) & (SIDE - 1)
 
     def remote(src, dst, send, recv, **at):
         return pltpu.make_async_remote_copy(
@@ -182,7 +182,7 @@
             y2, x2 = other(y, k), other(x, k)
             push(phase, h, 0, S.at[h, y2, :, 0], RA.at[h, y], fsdp=y2 * SIDE + x)
             push(
-                phase, h, 1, S.at[h, :, x2 // 2, 1, :, span(x2 % 2, ca, cb)], RB.at[h, x], fsdp=y * SIDE + x2
+                phase, h, 1, S.at[h, :, x2 >> 1, 1, :, span(x2 & 1, ca, cb)], RB.at[h, x], fsdp=y * SIDE + x2
             )
 
     def rs_mid(phase, h):
@@ -196,7 +196,7 @@
         for k in PEERS:
             x2 = other(x, k)
             push(
-                phase, h, 2, UA.at[h, x2 // 2, :, span(x2 % 2, ca, ca)], VA.at[h, x], fsdp=y * SIDE + x2
+                phase, h, 2, UA.at[h, x2 >> 1, :, span(x2 & 1, ca, ca)], VA.at[h, x], fsdp=y * SIDE + x2
             )
         f_all(phase, h, 1).wait_recv()
         total = S[h, :, j, 1, :, span(g, ca, cb)].astype(jnp.float32)
@@ -380,13 +380,6 @@
 
     x_far, h_far, g_far = hand_over(7, X.at[far], FX), hand_over(8, H.at[far], FH), hand_over(9, G.at[far], FG)
     q_far = hand_over(10, Q.at[1], FQ)
-    stores = []
-
-    def store(src, dst):
-        c = pltpu.make_async_copy(src, dst, lo.at[len(stores)])
-        c.start()
-        stores.append(c)
-
     def weight_grads(h):
         rows, far_rows = flat(X[core, h]), flat(FX[h])
         for gg in (0, 1):
@@ -394,10 +387,12 @@
             term = dot(rows, flat(Q[core, h, :, :, :, :, at]), TN) + dot(
                 far_rows, flat(FQ[h, :, :, :, :, at]), TN
             )
-            DW[gg] = term if h == 0 else DW[gg] + term
-            if h == 1:
-                for to, width, out in ((0, q_wide, dq_out), (q_wide, k_wide, dk_out), (q_wide + k_wide, k_wide, dv_out)):
-                    store(DW.at[gg, :, pl.ds(to, width)], out.at[0, :, pl.ds(gg * width, width)])
+            for to, width, out in (
+                (0, q_wide, dq_out), (q_wide, k_wide, dk_out), (q_wide + k_wide, k_wide, dv_out)
+            ):
+                to_at = pl.ds(gg * width, width)
+                part = term[:, to : to + width]
+                out[0, :, to_at] = part if h == 0 else out[0, :, to_at] + part
 
     loads[0].wait()
     for h in HALVES:
@@ -408,18 +403,19 @@
         )
         for i, (w, at, gg, to, width) in enumerate(cuts)
     ] + [remote(wo.at[0], WO.at[core], ss.at[6], sr.at[6], pp=far)]
-    for c in swaps:
+    for c in swaps[:6]:
         c.start()
+    for c in loads[1:8]:
+        c.wait()
+    for c in swaps[:6]:
+        c.wait_recv()
+    for h in HALVES:
+        project(0, AG_STREAM0, RS_QKV0, h)
+    swaps[6].start()
     loads[8].wait()
     top = token_weights(lengths, rewards, groups, noise, core, t)
     top = (-top * flat(GIN[...]).astype(jnp.float32)).astype(jnp.bfloat16)
     G[1, :, t] = top.reshape(GIN.shape)
-    for c in loads[1:8]:
-        c.wait()
-    for c in swaps[:6]:
-        c.wait_recv()
-    for h in HALVES:
-        project(0, AG_STREAM0, RS_QKV0, h)
     for h in HALVES:
         z_gather(AG_TOP, G.at[1], h)
     for h in HALVES:
@@ -472,7 +468,7 @@
     for h in HALVES:
         ag_end(AG_HEAD1, h)
     h_far.start()
-    DWO[...] = dot(flat(H[core]), flat(G[core]), TN)
+    do_out[0] = dot(flat(H[core]), flat(G[core]), TN)
     for h in HALVES:
         rs_mid(RS_HEAD0, h)
     for h in HALVES:
@@ -483,8 +479,7 @@
         last_mid(h)
     for c in (x_far, h_far, g_far):
         c.wait_recv()
-    DWO[...] += dot(flat(FH[...]), flat(FG[...]), TN)
-    store(DWO, do_out.at[0])
+    do_out[0] += dot(flat(FH[...]), flat(FG[...]), TN)
     for h in HALVES:
 
         @pl.when(core == 0)
@@ -531,9 +526,6 @@
     @pl.when(core == 0)
     def _():
         q_far.wait_send()
-
-    for c in stores:
-        c.wait()
 
 
 def local(
@@ -575,13 +567,13 @@
     return pl.pallas_call(
         kernel,
         out_shape=[
-            jax.ShapeDtypeStruct(w.shape, f32)
+            pltpu.VMEM(w.shape, f32)
             for w in (query_weight, key_weight, value_weight, out_weight)
         ],
         in_specs=[any_space, any_space, pl.BlockSpec(memory_space=pltpu.VMEM)]
         + [pl.BlockSpec(memory_space=pltpu.SMEM)] * 3
         + [any_space] * 4,
-        out_specs=[any_space] * 4,
+        out_specs=[pl.BlockSpec(memory_space=pltpu.VMEM)] * 4,
         scratch_shapes=[
             pltpu.VMEM((2,) + rows + (width,), bf16),
             pltpu.VMEM((2,) + rows + (2 * q_wide,), bf16),
@@ -593,8 +585,6 @@
             pltpu.VMEM(rows + (2 * wide,), bf16),
             pltpu.VMEM((2, 2, width, cols), bf16),
             pltpu.VMEM((2, 2 * q_wide, width), bf16),
-            pltpu.VMEM((2, width, cols), f32),
-            pltpu.VMEM((2 * q_wide, width), f32),
             pltpu.VMEM(rows + (width,), bf16),
             pltpu.VMEM(rows + (width,), bf16),
             pltpu.VMEM(rows + (width,), bf16),
@@ -615,7 +605,6 @@
             pltpu.SemaphoreType.DMA((11,)),
             pltpu.SemaphoreType.DMA((11,)),
             pltpu.SemaphoreType.DMA((9,)),
-            pltpu.SemaphoreType.DMA((7,)),
         ],
         compiler_params=pltpu.CompilerParams(
             collective_id=0, has_side_effects=True, vmem_limit_bytes=56 * 1024 * 1024

time: 119 us -> 116 us (0.975)
  local copies, waits for them, and re-layouts: 6.23 us -> 4.23 us
    unnamed x10 -> x4, local copies, waits for them, and re-layouts: 6.23 us -> 4.23 us
where the time goes in v5:
time: 116 us; the launch traced here: 115 us
  Pallas kernels  111 us (96%)
  local copies, waits for them, and re-layouts  4.23 us (4%)
    pallas_call x1, Pallas kernels, local(): pl.pallas_call(kernel, out_shape=[pltpu.VMEM(w.shape, f32) for w in (quer...  111 us
    unnamed x4, local copies, waits for them, and re-layouts  4.23 us

profile of v5, /device:TPU:0, one launch (start us, length us, event | category | flops | bytes accessed | tf_op | source)
XLA Modules:
  0.0 115.5 jit_solution(2898505460749822516)
XLA Ops:
  0.6 110.6 %shard_map.129 = (f32[1,512,1024]{2,1,0:T(8,128)S(1)}, f32[1,512,256]{2,1,0:T(8,128)S(1)}, f32[1,512,256]{2,1,0:T(8,128)S(1)}, f32[1,1024,512]{2,1,0:T(8,128)S(1)}) custom-call(bf16[2,2,2,2,16,512]{5,4,3,2,1,0:T(8,128)(2,1)} %bitcast.5, bf16[2,2,2,2,16,512]{5,4,3,2,1,0:T(8,128)(2,1)} %bitcast.6, s32[2,128]{1,0:T(2,128)} %noise.1, s32[2,2,16]{2,1,0:T(2,128)} %bitcast.7, ...), custom_call_target="tpu_custom_call" | custom-call | tf_op jit(solution)/shard_map/pallas_call | solution.py:567
  111.2 1.3 %copy.18 = f32[1,512,1024]{2,1,0:T(8,128)} copy(f32[1,512,1024]{2,1,0:T(8,128)S(1)} %get-tuple-element.4) | data formatting | bytes 4194304
  112.5 0.8 copy.19
  113.3 0.8 copy.20
  114.1 1.3 %copy.21 = f32[1,1024,512]{2,1,0:T(8,128)} copy(f32[1,1024,512]{2,1,0:T(8,128)S(1)} %get-tuple-element.7) | data formatting | bytes 4194304

commit v6 on v5

--- a/solution.py
+++ b/solution.py
@@ -82,15 +82,17 @@
     dq_out, dk_out, dv_out, do_out,
     X, H, G, Q, FX, FH, FG, FQ, W, WO, D, E, DH, EH, ROWS, INV, PROBS, HG, GIN, *rest,
 ):
-    scatter_bufs, (fs, fr, zs, zr, ss, sr, ls) = rest[:28], rest[28:]
+    scatter_bufs, (fs, fr, zs, zr, ss, sr, ls) = rest[:36], rest[36:]
     rs_bufs = {
-        phase: scatter_bufs[7 * i : 7 * i + 7]
+        phase: scatter_bufs[9 * i : 9 * i + 9]
         for i, phase in enumerate((RS_QKV0, RS_QKV1, RS_HEAD1, RS_HEAD0))
     }
     core, f, t = lax.axis_index("pp"), lax.axis_index("fsdp"), lax.axis_index("tp")
     far = 1 - core
     y, x = f >> 2, f & 3
     j, g = x >> 1, x & 1
+    ways = (((y + 1) & 3, (x + 1) & 3), ((y + 3) & 3, (x + 3) & 3))
+    y_opp, x_opp = (y + 2) & 3, (x + 2) & 3
     q_wide = wq.shape[2] // 2
     k_wide = wk.shape[2] // 2
     cols = q_wide + 2 * k_wide
@@ -165,33 +167,56 @@
         remote(src, dst, fs.at[phase, h, kind], fr.at[phase, h, kind], **at).start()
 
     def f_all(phase, h, kind):
-        S, RA, RB, UA, UB, VA, VB = rs_bufs[
+        S, RA, RB, UA, UB, VA, VB, FA, FB = rs_bufs[
             {AG_HEAD0: RS_HEAD0, AG_HEAD1: RS_HEAD0, AG_GRAD0: RS_QKV0, AG_GRAD1: RS_QKV0}.get(phase, phase)
         ]
-        order = (RA, RB, VA, VB) if phase < AG_HEAD0 else (VA, VB, RA, RB)
-        three = order[kind].at[h, pl.ds(0, SIDE - 1)]
-        return remote(three, three, fs.at[phase, h, kind], fr.at[phase, h, kind], fsdp=f)
+        three = pl.ds(0, SIDE - 1)
+        refs = (RA.at[h], RB.at[h], VA.at[h, three], VB.at[h, three])
+        if phase >= AG_HEAD0:
+            refs = refs[2:] + refs[:2]
+        ref = (refs + (FA.at[h], FB.at[h]))[kind]
+        return remote(ref, ref, fs.at[phase, h, kind], fr.at[phase, h, kind], fsdp=f)
 
     def widths(buf_cols):
         return (wide, cols) if buf_cols == 2 * wide else (q_wide, q_wide)
 
     def rs_start(phase, h):
-        S, RA, RB, UA, UB, VA, VB = rs_bufs[phase]
+        S, RA, RB, UA, UB, VA, VB, FA, FB = rs_bufs[phase]
         ca, cb = widths(S.shape[-1])
-        for k in PEERS:
-            y2, x2 = other(y, k), other(x, k)
-            push(phase, h, 0, S.at[h, y2, :, 0], RA.at[h, y], fsdp=y2 * SIDE + x)
+
+        def second(x2, part):
+            return S.at[h, pl.ds(2 * part, 2), x2 >> 1, 1, :, span(x2 & 1, ca, cb)]
+
+        for d, (y2, x2) in enumerate(ways):
+            push(phase, h, 4, S.at[h, y_opp, d, 0], FA.at[h, d], fsdp=y2 * SIDE + x)
+            push(phase, h, 5, second(x_opp, d), FB.at[h, d], fsdp=y * SIDE + x2)
+        for d, (y2, x2) in enumerate(ways):
+            push(phase, h, 0, S.at[h, y2, 1 - d, 0], RA.at[h, d, 1 - d], fsdp=y2 * SIDE + x)
             push(
-                phase, h, 1, S.at[h, :, x2 >> 1, 1, :, span(x2 & 1, ca, cb)], RB.at[h, x], fsdp=y * SIDE + x2
+                phase, h, 1, second(x2, 1 - d), RB.at[h, d, pl.ds(2 * (1 - d), 2)], fsdp=y * SIDE + x2
             )
 
+    def rs_pass(phase, h):
+        S, RA, RB, UA, UB, VA, VB, FA, FB = rs_bufs[phase]
+        ca, cb = widths(S.shape[-1])
+        f_all(phase, h, 4).wait_recv()
+        for d, (y2, x2) in enumerate(ways):
+            total = S[h, y2, d, 0].astype(jnp.float32) + FA[h, d].astype(jnp.float32)
+            S[h, y2, d, 0] = total.astype(jnp.bfloat16)
+            push(phase, h, 0, S.at[h, y2, d, 0], RA.at[h, d, d], fsdp=y2 * SIDE + x)
+        f_all(phase, h, 5).wait_recv()
+        for d, (y2, x2) in enumerate(ways):
+            at = (h, pl.ds(2 * d, 2), x2 >> 1, 1, slice(None), span(x2 & 1, ca, cb))
+            S[at] = (S[at].astype(jnp.float32) + FB[h, d].astype(jnp.float32)).astype(jnp.bfloat16)
+            push(phase, h, 1, S.at[at], RB.at[h, d, pl.ds(2 * d, 2)], fsdp=y * SIDE + x2)
+
     def rs_mid(phase, h):
-        S, RA, RB, UA, UB, VA, VB = rs_bufs[phase]
+        S, RA, RB, UA, UB, VA, VB, FA, FB = rs_bufs[phase]
         ca, cb = widths(S.shape[-1])
         f_all(phase, h, 0).wait_recv()
         total = S[h, y, :, 0].astype(jnp.float32)
-        for k in PEERS:
-            total = total + RA[h, other(y, k)].astype(jnp.float32)
+        for d in (0, 1):
+            total = total + RA[h, d].astype(jnp.float32)
         UA[h] = total.astype(jnp.bfloat16)
         for k in PEERS:
             x2 = other(x, k)
@@ -200,15 +225,15 @@
             )
         f_all(phase, h, 1).wait_recv()
         total = S[h, :, j, 1, :, span(g, ca, cb)].astype(jnp.float32)
-        for k in PEERS:
-            total = total + RB[h, other(x, k)].astype(jnp.float32)
+        for d in (0, 1):
+            total = total + RB[h, d].astype(jnp.float32)
         UB[h] = total.astype(jnp.bfloat16)
         for k in PEERS:
             y2 = other(y, k)
             push(phase, h, 3, UB.at[h, y2], VB.at[h, y], fsdp=y2 * SIDE + x)
 
     def rs_end(phase, h):
-        S, RA, RB, UA, UB, VA, VB = rs_bufs[phase]
+        S, RA, RB, UA, UB, VA, VB, FA, FB = rs_bufs[phase]
         ca, cb = widths(S.shape[-1])
         f_all(phase, h, 2).wait_recv()
         first = UA[h, j, :, span(g, ca, ca)].astype(jnp.float32)
@@ -232,12 +257,34 @@
         ca, cb = widths(buf.shape[-1])
         first = buf.at[h, y, :, 0]
         f_all(phase, h, 0).wait_recv()
-        for k in PEERS:
-            push(phase, h, 2, first, first, fsdp=other(y, k) * SIDE + x)
+        for y2, _ in ways:
+            push(phase, h, 2, first, first, fsdp=y2 * SIDE + x)
         second = buf.at[h, :, j, 1, :, span(g, ca, cb)]
         f_all(phase, h, 1).wait_recv()
-        for k in PEERS:
-            push(phase, h, 3, second, second, fsdp=y * SIDE + other(x, k))
+        for _, x2 in ways:
+            push(phase, h, 3, second, second, fsdp=y * SIDE + x2)
+
+    def pass_first(phase, buf, h):
+        for d, (y2, _) in enumerate(ways):
+            ref = buf.at[h, ways[1 - d][0], d, 0]
+            push(phase, h, 4, ref, ref, fsdp=y2 * SIDE + x)
+
+    def pass_second(phase, buf, h):
+        ca, cb = widths(buf.shape[-1])
+        for d, (_, x2) in enumerate(ways):
+            x3 = ways[1 - d][1]
+            ref = buf.at[h, pl.ds(2 * d, 2), x3 >> 1, 1, :, span(x3 & 1, ca, cb)]
+            push(phase, h, 5, ref, ref, fsdp=y * SIDE + x2)
+
+    def ag_pass(phase, buf, h):
+        f_all(phase, h, 2).wait_recv()
+        pass_first(phase, buf, h)
+        f_all(phase, h, 3).wait_recv()
+        pass_second(phase, buf, h)
+
+    def ag_end(phase, h):
+        f_all(phase, h, 4).wait_recv()
+        f_all(phase, h, 5).wait_recv()
 
     def last_mid(h):
         first, second = Q.at[0, h, y, :, 0], Q.at[0, h, :, j, 1, :, span(g, wide, cols)]
@@ -246,33 +293,43 @@
 
         @pl.when(core == 0)
         def _():
-            for k in PEERS:
-                push(AG_GRAD0, h, 2, first, first, fsdp=other(y, k) * SIDE + x)
+            for y2, _ in ways:
+                push(AG_GRAD0, h, 2, first, first, fsdp=y2 * SIDE + x)
 
         @pl.when(core == 1)
         def _():
-            for k in PEERS + (0,):
-                push(AG_FAR0, h, 2, first, first_far, pp=far, fsdp=other(y, k) * SIDE + x)
+            for y2 in (ways[0][0], ways[1][0], y):
+                push(AG_FAR0, h, 2, first, first_far, pp=far, fsdp=y2 * SIDE + x)
 
         f_all(AG_GRAD0, h, 1).wait_recv()
 
         @pl.when(core == 0)
         def _():
-            for k in PEERS:
-                push(AG_GRAD0, h, 3, second, second, fsdp=y * SIDE + other(x, k))
+            for _, x2 in ways:
+                push(AG_GRAD0, h, 3, second, second, fsdp=y * SIDE + x2)
 
         @pl.when(core == 1)
         def _():
-            for k in PEERS + (0,):
-                push(AG_FAR0, h, 3, second, second_far, pp=far, fsdp=y * SIDE + other(x, k))
+            for x2 in (ways[0][1], ways[1][1], x):
+                push(AG_FAR0, h, 3, second, second_far, pp=far, fsdp=y * SIDE + x2)
 
     def far_all(h, kind):
-        four = rs_bufs[RS_QKV0][1 + (kind - 2)].at[h]
-        return remote(four, four, fs.at[AG_FAR0, h, kind], fr.at[AG_FAR0, h, kind], fsdp=f)
-
-    def ag_end(phase, h):
-        f_all(phase, h, 2).wait_recv()
-        f_all(phase, h, 3).wait_recv()
+        FA, FB = rs_bufs[RS_QKV0][7:]
+        three = pl.ds(0, SIDE - 1)
+        ref = {
+            2: Q.at[0, h, three, :, 0],
+            3: Q.at[0, h, three, :, :, :, pl.ds(0, cols)],
+            4: FA.at[h],
+            5: FB.at[h],
+        }[kind]
+        return remote(ref, ref, fs.at[AG_FAR0, h, kind], fr.at[AG_FAR0, h, kind], fsdp=f)
+
+    def last_pass(h):
+        ag_pass(AG_GRAD0, Q.at[0], h)
+        far_all(h, 2).wait_recv()
+        pass_first(AG_FAR0, FQ, h)
+        far_all(h, 3).wait_recv()
+        pass_second(AG_FAR0, FQ, h)
 
     def flat(value):
         return value.reshape(-1, value.shape[-1])
@@ -411,6 +468,8 @@
         c.wait_recv()
     for h in HALVES:
         project(0, AG_STREAM0, RS_QKV0, h)
+    for h in HALVES:
+        rs_pass(RS_QKV0, h)
     swaps[6].start()
     loads[8].wait()
     top = token_weights(lengths, rewards, groups, noise, core, t)
@@ -425,6 +484,8 @@
         ag_start(AG_HEAD0, H.at[0], h)
     for h in HALVES:
         ag_mid(AG_HEAD0, H.at[0], h)
+    for h in HALVES:
+        ag_pass(AG_HEAD0, H.at[0], h)
     swaps[6].wait_recv()
     for h in HALVES:
         project_out(h)
@@ -434,9 +495,13 @@
         X[1, h, t] = z_sum(RS_OUT0, D, E, h, X[0, h, t].astype(jnp.float32))
         z_gather(AG_STREAM1, X.at[1], h)
     for h in HALVES:
+        rs_pass(RS_HEAD1, h)
+    for h in HALVES:
+        project(1, AG_STREAM1, RS_QKV1, h)
+    for h in HALVES:
         rs_mid(RS_HEAD1, h)
     for h in HALVES:
-        project(1, AG_STREAM1, RS_QKV1, h)
+        rs_pass(RS_QKV1, h)
     x_far.start()
     for h in HALVES:
         head_end(RS_HEAD1, h)
@@ -449,6 +514,8 @@
     for h in HALVES:
         ag_mid(AG_GRAD1, Q.at[1], h)
     for h in HALVES:
+        ag_pass(AG_GRAD1, Q.at[1], h)
+    for h in HALVES:
         project_back(h)
 
     @pl.when(core == 0)
@@ -466,6 +533,10 @@
         head_grads(0, AG_OUT0, RS_HEAD0, h)
     g_far.start()
     for h in HALVES:
+        ag_pass(AG_HEAD1, H.at[1], h)
+    for h in HALVES:
+        rs_pass(RS_HEAD0, h)
+    for h in HALVES:
         ag_end(AG_HEAD1, h)
     h_far.start()
     do_out[0] = dot(flat(H[core]), flat(G[core]), TN)
@@ -477,6 +548,12 @@
         ag_start(AG_GRAD0, Q.at[0], h)
     for h in HALVES:
         last_mid(h)
+
+    @pl.when(core == 0)
+    def _():
+        for h in HALVES:
+            last_pass(h)
+
     for c in (x_far, h_far, g_far):
         c.wait_recv()
     do_out[0] += dot(flat(FH[...]), flat(FG[...]), TN)
@@ -485,8 +562,8 @@
         @pl.when(core == 0)
         def _():
             ag_end(AG_GRAD0, h)
-            far_all(h, 2).wait_recv()
-            far_all(h, 3).wait_recv()
+            far_all(h, 4).wait_recv()
+            far_all(h, 5).wait_recv()
 
         if h == 0:
 
@@ -498,7 +575,7 @@
 
     for phase in range(AG_GRAD0):
         for h in HALVES:
-            for kind in range(4):
+            for kind in range(6):
                 f_all(phase, h, kind).wait_send()
     for h in HALVES:
         for kind in (0, 1):
@@ -506,8 +583,10 @@
 
         @pl.when(core == 0)
         def _():
-            for kind in (2, 3):
+            for kind in (2, 3, 4, 5):
                 f_all(AG_GRAD0, h, kind).wait_send()
+            for kind in (4, 5):
+                far_all(h, kind).wait_send()
 
         @pl.when(core == 1)
         def _():
@@ -555,12 +634,14 @@
             pltpu.VMEM(shape, bf16)
             for shape in (
                 rows + (2 * ca,),
-                (2, SIDE, 2, SUB, 2 * ca),
-                (2, SIDE, SIDE, SUB, cb),
+                (2, 2, 2, SUB, 2 * ca),
+                (2, 2, SIDE, SUB, cb),
                 (2, 2, SUB, 2 * ca),
                 (2, SIDE, SUB, cb),
                 (2, SIDE, SUB, ca),
                 (2, SIDE, SUB, cb),
+                (2, 2, SUB, 2 * ca),
+                (2, 2, 2, SUB, cb),
             )
         ]
 
@@ -598,8 +679,8 @@
         + scatter_bufs(wide, cols) * 2
         + scatter_bufs(q_wide, q_wide) * 2
         + [
-            pltpu.SemaphoreType.DMA((9, 2, 4)),
-            pltpu.SemaphoreType.DMA((9, 2, 4)),
+            pltpu.SemaphoreType.DMA((9, 2, 6)),
+            pltpu.SemaphoreType.DMA((9, 2, 6)),
             pltpu.SemaphoreType.DMA((6, 2)),
             pltpu.SemaphoreType.DMA((6, 2)),
             pltpu.SemaphoreType.DMA((11,)),

time: 116 us -> 122 us (1.052)
  Pallas kernels: 111 us -> 117 us
    pallas_call x1, Pallas kernels: 111 us -> 117 us  [local(): pl.pallas_call(kernel, out_shape=[pltpu.VMEM(w.shape, f32) for w in (quer...]
where the time goes in v6:
time: 122 us
  Pallas kernels  117 us (96%)
  local copies, waits for them, and re-layouts  4.23 us (3%)
    pallas_call x1, Pallas kernels, local(): pl.pallas_call(kernel, out_shape=[pltpu.VMEM(w.shape, f32) for w in (quer...  117 us
    unnamed x4, local copies, waits for them, and re-layouts  4.23 us

profile of v6, /device:TPU:0, one launch (start us, length us, event | category | flops | bytes accessed | tf_op | source)
XLA Modules:
  0.0 121.7 jit_solution(9407415651498158599)
XLA Ops:
  0.6 116.8 %shard_map.129 = (f32[1,512,1024]{2,1,0:T(8,128)S(1)}, f32[1,512,256]{2,1,0:T(8,128)S(1)}, f32[1,512,256]{2,1,0:T(8,128)S(1)}, f32[1,1024,512]{2,1,0:T(8,128)S(1)}) custom-call(bf16[2,2,2,2,16,512]{5,4,3,2,1,0:T(8,128)(2,1)} %bitcast.5, bf16[2,2,2,2,16,512]{5,4,3,2,1,0:T(8,128)(2,1)} %bitcast.6, s32[2,128]{1,0:T(2,128)} %noise.1, s32[2,2,16]{2,1,0:T(2,128)} %bitcast.7, ...), custom_call_target="tpu_custom_call" | custom-call | tf_op jit(solution)/shard_map/pallas_call | solution.py:648
  117.5 1.3 %copy.18 = f32[1,512,1024]{2,1,0:T(8,128)} copy(f32[1,512,1024]{2,1,0:T(8,128)S(1)} %get-tuple-element.4) | data formatting | bytes 4194304
  118.8 0.8 copy.19
  119.6 0.8 copy.20
  120.4 1.3 %copy.21 = f32[1,1024,512]{2,1,0:T(8,128)} copy(f32[1,1024,512]{2,1,0:T(8,128)S(1)} %get-tuple-element.7) | data formatting | bytes 4194304

commit v7 on v5

--- a/solution.py
+++ b/solution.py
@@ -80,7 +80,7 @@
 def kernel(
     x_in, g_in, noise, lengths, rewards, groups, wq, wk, wv, wo,
     dq_out, dk_out, dv_out, do_out,
-    X, H, G, Q, FX, FH, FG, FQ, W, WO, D, E, DH, EH, ROWS, INV, PROBS, HG, GIN, *rest,
+    X, H, G, Q0, Q1, FX, FH, FG, FQ, W, WO, D, E, DH, EH, ROWS, INV, PROBS, HG, GIN, *rest,
 ):
     scatter_bufs, (fs, fr, zs, zr, ss, sr, ls) = rest[:28], rest[28:]
     rs_bufs = {
@@ -141,24 +141,31 @@
     pl.semaphore_signal(barrier, inc=1, device_id={"pp": far}, device_id_type=MESH)
     pl.semaphore_wait(barrier, 16)
 
-    def z_gather(phase, buf, h):
-        for k in PEERS:
-            remote(buf.at[h, t], buf.at[h, t], zs.at[phase, h], zr.at[phase, h], tp=other(t, k)).start()
-
-    def z_scatter(phase, send, recv, h):
+    def z_gather(phase, buf, h, i):
+        ref = buf.at[h, t, i]
+        for k in PEERS:
+            remote(ref, ref, zs.at[phase, h, i], zr.at[phase, h, i], tp=other(t, k)).start()
+
+    def z_scatter(phase, send, recv, h, i):
         for k in PEERS:
             b = other(t, k)
-            remote(send.at[h, b], recv.at[h, t], zs.at[phase, h], zr.at[phase, h], tp=b).start()
-
-    def z_all(phase, buf, h):
-        three = buf.at[h, pl.ds(0, SIDE - 1)]
-        return remote(three, three, zs.at[phase, h], zr.at[phase, h], tp=t)
-
-    def z_sum(phase, send, recv, h, total):
-        z_all(phase, recv, h).wait_recv()
-        total = total + send[h, t].astype(jnp.float32)
-        for k in PEERS:
-            total = total + recv[h, other(t, k)].astype(jnp.float32)
+            remote(
+                send.at[h, b, i], recv.at[h, t, i], zs.at[phase, h, i], zr.at[phase, h, i], tp=b
+            ).start()
+
+    def z_all(phase, buf, h, i):
+        three = buf.at[h, pl.ds(0, SIDE - 1), i]
+        return remote(three, three, zs.at[phase, h, i], zr.at[phase, h, i], tp=t)
+
+    def z_wait(phase, buf, h):
+        for i in (0, 1):
+            z_all(phase, buf, h, i).wait_recv()
+
+    def z_sum(phase, send, recv, h, i, total):
+        z_all(phase, recv, h, i).wait_recv()
+        total = total + send[h, t, i].astype(jnp.float32)
+        for k in PEERS:
+            total = total + recv[h, other(t, k), i].astype(jnp.float32)
         return total.astype(jnp.bfloat16)
 
     def push(phase, h, kind, src, dst, **at):
@@ -169,11 +176,13 @@
             {AG_HEAD0: RS_HEAD0, AG_HEAD1: RS_HEAD0, AG_GRAD0: RS_QKV0, AG_GRAD1: RS_QKV0}.get(phase, phase)
         ]
         order = (RA, RB, VA, VB) if phase < AG_HEAD0 else (VA, VB, RA, RB)
+        if phase == AG_GRAD0:
+            order = (VB, VB, RB, RB)
         three = order[kind].at[h, pl.ds(0, SIDE - 1)]
         return remote(three, three, fs.at[phase, h, kind], fr.at[phase, h, kind], fsdp=f)
 
     def widths(buf_cols):
-        return (wide, cols) if buf_cols == 2 * wide else (q_wide, q_wide)
+        return (wide, cols) if buf_cols == 2 * wide else (buf_cols // 2, buf_cols // 2)
 
     def rs_start(phase, h):
         S, RA, RB, UA, UB, VA, VB = rs_bufs[phase]
@@ -240,8 +249,8 @@
             push(phase, h, 3, second, second, fsdp=y * SIDE + other(x, k))
 
     def last_mid(h):
-        first, second = Q.at[0, h, y, :, 0], Q.at[0, h, :, j, 1, :, span(g, wide, cols)]
-        first_far, second_far = FQ.at[h, y, :, 0], FQ.at[h, :, j, 1, :, span(g, wide, cols)]
+        first, second = Q0.at[h, y, :, 0], Q0.at[h, :, j, 1, :, span(g, cols, cols)]
+        first_far, second_far = FQ.at[h, y, :, 0], FQ.at[h, :, j, 1, :, span(g, cols, cols)]
         f_all(AG_GRAD0, h, 0).wait_recv()
 
         @pl.when(core == 0)
@@ -267,7 +276,7 @@
                 push(AG_FAR0, h, 3, second, second_far, pp=far, fsdp=y * SIDE + other(x, k))
 
     def far_all(h, kind):
-        four = rs_bufs[RS_QKV0][1 + (kind - 2)].at[h]
+        four = rs_bufs[RS_QKV0][2].at[h]
         return remote(four, four, fs.at[AG_FAR0, h, kind], fr.at[AG_FAR0, h, kind], fsdp=f)
 
     def ag_end(phase, h):
@@ -279,7 +288,7 @@
 
     def project(layer, gathered, phase, h):
         S = rs_bufs[phase][0]
-        z_all(gathered, X.at[layer], h).wait_recv()
+        z_wait(gathered, X.at[layer], h)
         rows = flat(X[layer, h])
         for gg in (0, 1):
             S[h, :, :, :, :, pl.ds(gg * wide, cols)] = (
@@ -324,6 +333,7 @@
         HG[h] = jnp.concatenate([first, second], 0).astype(jnp.bfloat16)
 
     def attend_back(layer, h):
+        Q, stride = ((Q0, cols), (Q1, wide))[layer]
         rows, head_grad, inv_rms, probs = ROWS[layer, h], HG[h], INV[layer, h], PROBS[layer, h]
 
         def stacked(value):
@@ -344,48 +354,56 @@
         for i, part in enumerate(parts):
             part = part.astype(jnp.bfloat16).astype(jnp.float32)
             total = total + part * rows[:, i * HEAD_WIDTH : (i + 1) * HEAD_WIDTH].astype(jnp.float32)
-            Q[layer, h, y, j, :, :, span(g, wide, HEAD_WIDTH, i * HEAD_WIDTH)] = (
+            Q[h, y, j, :, :, span(g, stride, HEAD_WIDTH, i * HEAD_WIDTH)] = (
                 (part * inv_rms).astype(jnp.bfloat16).reshape(2, SUB, HEAD_WIDTH)
             )
-        share = inv_rms[:, :1] * inv_rms[:, :1] * jnp.sum(total, -1, keepdims=True) / MODEL_WIDTH
-        Q[layer, h, y, j, 0, :, span(g, wide, LANES, cols)] = split_tile(share[:SUB], share[SUB:])
+        if layer > 0:
+            share = inv_rms[:, :1] * inv_rms[:, :1] * jnp.sum(total, -1, keepdims=True) / MODEL_WIDTH
+            Q[h, y, j, 0, :, span(g, wide, LANES, cols)] = split_tile(share[:SUB], share[SUB:])
 
     def head_grads(layer, gathered, phase, h):
         S = rs_bufs[phase][0]
-        z_all(gathered, G.at[layer], h).wait_recv()
+        z_wait(gathered, G.at[layer], h)
         S[h] = dot(flat(G[layer, h]), WO[layer], NT).astype(jnp.bfloat16).reshape(S.shape[1:])
         rs_start(phase, h)
 
     def project_out(h):
         ag_end(AG_HEAD0, h)
         D[h] = dot(flat(H[0, h]), WO[0], NN).astype(jnp.bfloat16).reshape(D.shape[1:])
-        z_scatter(RS_OUT0, D, E, h)
+        for i in (0, 1):
+            z_scatter(RS_OUT0, D, E, h, i)
 
     def project_back(h):
         ag_end(AG_GRAD1, h)
         back = sum(
-            dot(flat(Q[1, h, :, :, :, :, pl.ds(gg * wide, cols)]), W[1, gg], NT) for gg in (0, 1)
+            dot(flat(Q1[h, :, :, :, :, pl.ds(gg * wide, cols)]), W[1, gg], NT) for gg in (0, 1)
         ).reshape(DH.shape[1:])
         tiles = [
-            Q[1, h, :, :, 0, :, pl.ds(gg * wide + cols, LANES)].astype(jnp.float32) for gg in (0, 1)
+            Q1[h, :, :, 0, :, pl.ds(gg * wide + cols, LANES)].astype(jnp.float32) for gg in (0, 1)
         ]
         shares = join_tile(tiles[0] + tiles[1])
         for a in (0, 1):
             term = back[:, :, a] - X[1, h, :, :, a].astype(jnp.float32) * shares[a]
             DH[h, :, :, a] = term.astype(jnp.bfloat16)
-        z_scatter(RS_IN1, DH, EH, h)
+        for i in (0, 1):
+            z_scatter(RS_IN1, DH, EH, h, i)
 
     def hand_over(i, src, dst):
         return remote(src, dst, ss.at[i], sr.at[i], pp=far)
 
     x_far, h_far, g_far = hand_over(7, X.at[far], FX), hand_over(8, H.at[far], FH), hand_over(9, G.at[far], FG)
-    q_far = hand_over(10, Q.at[1], FQ)
-    def weight_grads(h):
-        rows, far_rows = flat(X[core, h]), flat(FX[h])
+    q_far = [
+        hand_over(
+            10 + gg, Q1.at[:, :, :, :, :, pl.ds(gg * wide, cols)], FQ.at[:, :, :, :, :, pl.ds(gg * cols, cols)]
+        )
+        for gg in (0, 1)
+    ]
+    def weight_grads(layer, h):
+        Q, stride = ((Q0, cols), (Q1, wide))[layer]
+        rows, far_rows = flat(X[layer, h]), flat(FX[h])
         for gg in (0, 1):
-            at = pl.ds(gg * wide, cols)
-            term = dot(rows, flat(Q[core, h, :, :, :, :, at]), TN) + dot(
-                far_rows, flat(FQ[h, :, :, :, :, at]), TN
+            term = dot(rows, flat(Q[h, :, :, :, :, pl.ds(gg * stride, cols)]), TN) + dot(
+                far_rows, flat(FQ[h, :, :, :, :, pl.ds(gg * cols, cols)]), TN
             )
             for to, width, out in (
                 (0, q_wide, dq_out), (q_wide, k_wide, dk_out), (q_wide + k_wide, k_wide, dv_out)
@@ -396,7 +414,8 @@
 
     loads[0].wait()
     for h in HALVES:
-        z_gather(AG_STREAM0, X.at[0], h)
+        for i in (0, 1):
+            z_gather(AG_STREAM0, X.at[0], h, i)
     swaps = [
         remote(
             w.at[0, :, pl.ds(at, width)], W.at[core, gg, :, pl.ds(to, width)], ss.at[i], sr.at[i], pp=far
@@ -417,7 +436,8 @@
     top = (-top * flat(GIN[...]).astype(jnp.float32)).astype(jnp.bfloat16)
     G[1, :, t] = top.reshape(GIN.shape)
     for h in HALVES:
-        z_gather(AG_TOP, G.at[1], h)
+        for i in (0, 1):
+            z_gather(AG_TOP, G.at[1], h, i)
     for h in HALVES:
         rs_mid(RS_QKV0, h)
     for h in HALVES:
@@ -431,8 +451,9 @@
     for h in HALVES:
         head_grads(1, AG_TOP, RS_HEAD1, h)
     for h in HALVES:
-        X[1, h, t] = z_sum(RS_OUT0, D, E, h, X[0, h, t].astype(jnp.float32))
-        z_gather(AG_STREAM1, X.at[1], h)
+        for i in (0, 1):
+            X[1, h, t, i] = z_sum(RS_OUT0, D, E, h, i, X[0, h, t, i].astype(jnp.float32))
+            z_gather(AG_STREAM1, X.at[1], h, i)
     for h in HALVES:
         rs_mid(RS_HEAD1, h)
     for h in HALVES:
@@ -445,21 +466,23 @@
     for h in HALVES:
         attend(1, RS_QKV1, h)
         attend_back(1, h)
-        ag_start(AG_GRAD1, Q.at[1], h)
-    for h in HALVES:
-        ag_mid(AG_GRAD1, Q.at[1], h)
+        ag_start(AG_GRAD1, Q1, h)
+    for h in HALVES:
+        ag_mid(AG_GRAD1, Q1, h)
     for h in HALVES:
         project_back(h)
 
     @pl.when(core == 0)
     def _():
-        q_far.start()
+        for c in q_far:
+            c.start()
 
     for h in HALVES:
         ag_start(AG_HEAD1, H.at[1], h)
     for h in HALVES:
-        G[0, h, t] = z_sum(RS_IN1, DH, EH, h, G[1, h, t].astype(jnp.float32))
-        z_gather(AG_OUT0, G.at[0], h)
+        for i in (0, 1):
+            G[0, h, t, i] = z_sum(RS_IN1, DH, EH, h, i, G[1, h, t, i].astype(jnp.float32))
+            z_gather(AG_OUT0, G.at[0], h, i)
     for h in HALVES:
         ag_mid(AG_HEAD1, H.at[1], h)
     for h in HALVES:
@@ -474,27 +497,26 @@
     for h in HALVES:
         head_end(RS_HEAD0, h)
         attend_back(0, h)
-        ag_start(AG_GRAD0, Q.at[0], h)
+        ag_start(AG_GRAD0, Q0, h)
     for h in HALVES:
         last_mid(h)
     for c in (x_far, h_far, g_far):
         c.wait_recv()
     do_out[0] += dot(flat(FH[...]), flat(FG[...]), TN)
-    for h in HALVES:
-
-        @pl.when(core == 0)
-        def _():
+    @pl.when(core == 0)
+    def _():
+        for h in HALVES:
             ag_end(AG_GRAD0, h)
             far_all(h, 2).wait_recv()
             far_all(h, 3).wait_recv()
-
-        if h == 0:
-
-            @pl.when(core == 1)
-            def _():
-                q_far.wait_recv()
-
-        weight_grads(h)
+            weight_grads(0, h)
+
+    @pl.when(core == 1)
+    def _():
+        for c in q_far:
+            c.wait_recv()
+        for h in HALVES:
+            weight_grads(1, h)
 
     for phase in range(AG_GRAD0):
         for h in HALVES:
@@ -519,13 +541,28 @@
         (AG_STREAM1, X.at[1]), (RS_IN1, EH), (AG_OUT0, G.at[0]),
     ):
         for h in HALVES:
-            z_all(phase, buf, h).wait_send()
+            for i in (0, 1):
+                z_all(phase, buf, h, i).wait_send()
     for c in swaps + [x_far, h_far, g_far]:
         c.wait_send()
 
     @pl.when(core == 0)
     def _():
-        q_far.wait_send()
+        for c in q_far:
+            c.wait_send()
+
+
+def write_out(*refs):
+    *pairs, sems = refs
+    count = len(pairs) // 2
+    copies = [
+        pltpu.make_async_copy(src, dst, sems.at[i])
+        for i, (src, dst) in enumerate(zip(pairs[:count], pairs[count:]))
+    ]
+    for c in copies:
+        c.start()
+    for c in copies:
+        c.wait()
 
 
 def local(
@@ -564,7 +601,7 @@
             )
         ]
 
-    return pl.pallas_call(
+    results = pl.pallas_call(
         kernel,
         out_shape=[
             pltpu.VMEM(w.shape, f32)
@@ -578,11 +615,12 @@
             pltpu.VMEM((2,) + rows + (width,), bf16),
             pltpu.VMEM((2,) + rows + (2 * q_wide,), bf16),
             pltpu.VMEM((2,) + rows + (width,), bf16),
-            pltpu.VMEM((2,) + rows + (2 * wide,), bf16),
+            pltpu.VMEM(rows + (2 * cols,), bf16),
+            pltpu.VMEM(rows + (2 * wide,), bf16),
             pltpu.VMEM(rows + (width,), bf16),
             pltpu.VMEM(rows + (2 * q_wide,), bf16),
             pltpu.VMEM(rows + (width,), bf16),
-            pltpu.VMEM(rows + (2 * wide,), bf16),
+            pltpu.VMEM(rows + (2 * cols,), bf16),
             pltpu.VMEM((2, 2, width, cols), bf16),
             pltpu.VMEM((2, 2 * q_wide, width), bf16),
             pltpu.VMEM(rows + (width,), bf16),
@@ -600,10 +638,10 @@
         + [
             pltpu.SemaphoreType.DMA((9, 2, 4)),
             pltpu.SemaphoreType.DMA((9, 2, 4)),
-            pltpu.SemaphoreType.DMA((6, 2)),
-            pltpu.SemaphoreType.DMA((6, 2)),
-            pltpu.SemaphoreType.DMA((11,)),
-            pltpu.SemaphoreType.DMA((11,)),
+            pltpu.SemaphoreType.DMA((6, 2, 2)),
+            pltpu.SemaphoreType.DMA((6, 2, 2)),
+            pltpu.SemaphoreType.DMA((12,)),
+            pltpu.SemaphoreType.DMA((12,)),
             pltpu.SemaphoreType.DMA((9,)),
         ],
         compiler_params=pltpu.CompilerParams(
@@ -619,6 +657,14 @@
         value_weight,
         out_weight,
     )
+    return pl.pallas_call(
+        write_out,
+        out_shape=[jax.ShapeDtypeStruct(r.shape, r.dtype) for r in results],
+        in_specs=[any_space] * 4,
+        out_specs=[any_space] * 4,
+        scratch_shapes=[pltpu.SemaphoreType.DMA((4,))],
+        compiler_params=pltpu.CompilerParams(vmem_limit_bytes=1024 * 1024),
+    )(*results)
 
 
 def solution(mesh):

time: 116 us -> 114 us (0.983)
  local copies, waits for them, and re-layouts: 4.23 us -> 0 us
  Pallas kernels: 111 us -> 113 us
    unnamed x4 -> x0, local copies, waits for them, and re-layouts: 4.23 us -> none
    pallas_call x0 -> x1, Pallas kernels: none -> 2.39 us  [local(): pl.pallas_call(write_out, out_shape=[jax.ShapeDtypeStruct(r.shape, r.dtyp...]
where the time goes in v7:
time: 114 us
  Pallas kernels  113 us (99%)
    pallas_call x1, Pallas kernels, local(): pl.pallas_call(kernel, out_shape=[pltpu.VMEM(w.shape, f32) for w in (quer...  111 us
    pallas_call x1, Pallas kernels, local(): pl.pallas_call(write_out, out_shape=[jax.ShapeDtypeStruct(r.shape, r.dtyp...  2.39 us

profile of v7, /device:TPU:0, one launch (start us, length us, event | category | flops | bytes accessed | tf_op | source)
XLA Modules:
  0.0 113.6 jit_solution(1435499491858805462)
XLA Ops:
  0.6 110.6 %shard_map.129 = (f32[1,512,1024]{2,1,0:T(8,128)S(1)}, f32[1,512,256]{2,1,0:T(8,128)S(1)}, f32[1,512,256]{2,1,0:T(8,128)S(1)}, f32[1,1024,512]{2,1,0:T(8,128)S(1)}) custom-call(bf16[2,2,2,2,16,512]{5,4,3,2,1,0:T(8,128)(2,1)} %bitcast.5, bf16[2,2,2,2,16,512]{5,4,3,2,1,0:T(8,128)(2,1)} %bitcast.6, s32[2,128]{1,0:T(2,128)} %noise.1, s32[2,2,16]{2,1,0:T(2,128)} %bitcast.7, ...), custom_call_target="tpu_custom_call" | custom-call | tf_op jit(solution)/shard_map/pallas_call | solution.py:604
  111.2 2.4 %shard_map.130 = (f32[1,512,1024]{2,1,0:T(8,128)}, f32[1,512,256]{2,1,0:T(8,128)}, f32[1,512,256]{2,1,0:T(8,128)}, f32[1,1024,512]{2,1,0:T(8,128)}) custom-call(f32[1,512,1024]{2,1,0:T(8,128)S(1)} %get-tuple-element.8.refs_0_, f32[1,512,256]{2,1,0:T(8,128)S(1)} %get-tuple-element.9.refs_1_, f32[1,512,256]{2,1,0:T(8,128)S(1)} %get-tuple-element.10.refs_2_, ...), custom_call_target="tpu_custom_call" | custom-call | tf_op jit(solution)/shard_map/pallas_call | solution.py:660

commit v8 on v7

--- a/solution.py
+++ b/solution.py
@@ -447,9 +447,9 @@
         ag_mid(AG_HEAD0, H.at[0], h)
     swaps[6].wait_recv()
     for h in HALVES:
+        head_grads(1, AG_TOP, RS_HEAD1, h)
+    for h in HALVES:
         project_out(h)
-    for h in HALVES:
-        head_grads(1, AG_TOP, RS_HEAD1, h)
     for h in HALVES:
         for i in (0, 1):
             X[1, h, t, i] = z_sum(RS_OUT0, D, E, h, i, X[0, h, t, i].astype(jnp.float32))

time: 114 us -> 112 us (0.982)
  Pallas kernels: 113 us -> 111 us
    pallas_call x1, Pallas kernels: 111 us -> 109 us  [local(): pl.pallas_call(kernel, out_shape=[pltpu.VMEM(w.shape, f32) for w in (quer...]
where the time goes in v8:
time: 112 us
  Pallas kernels  111 us (99%)
    pallas_call x1, Pallas kernels, local(): pl.pallas_call(kernel, out_shape=[pltpu.VMEM(w.shape, f32) for w in (quer...  109 us
    pallas_call x1, Pallas kernels, local(): pl.pallas_call(write_out, out_shape=[jax.ShapeDtypeStruct(r.shape, r.dtyp...  2.39 us

profile of v8, /device:TPU:0, one launch (start us, length us, event | category | flops | bytes accessed | tf_op | source)
XLA Modules:
  0.0 111.6 jit_solution(18411085292438967854)
XLA Ops:
  0.6 108.6 %shard_map.129 = (f32[1,512,1024]{2,1,0:T(8,128)S(1)}, f32[1,512,256]{2,1,0:T(8,128)S(1)}, f32[1,512,256]{2,1,0:T(8,128)S(1)}, f32[1,1024,512]{2,1,0:T(8,128)S(1)}) custom-call(bf16[2,2,2,2,16,512]{5,4,3,2,1,0:T(8,128)(2,1)} %bitcast.5, bf16[2,2,2,2,16,512]{5,4,3,2,1,0:T(8,128)(2,1)} %bitcast.6, s32[2,128]{1,0:T(2,128)} %noise.1, s32[2,2,16]{2,1,0:T(2,128)} %bitcast.7, ...), custom_call_target="tpu_custom_call" | custom-call | tf_op jit(solution)/shard_map/pallas_call | solution.py:604
  109.2 2.4 %shard_map.130 = (f32[1,512,1024]{2,1,0:T(8,128)}, f32[1,512,256]{2,1,0:T(8,128)}, f32[1,512,256]{2,1,0:T(8,128)}, f32[1,1024,512]{2,1,0:T(8,128)}) custom-call(f32[1,512,1024]{2,1,0:T(8,128)S(1)} %get-tuple-element.8.refs_0_, f32[1,512,256]{2,1,0:T(8,128)S(1)} %get-tuple-element.9.refs_1_, f32[1,512,256]{2,1,0:T(8,128)S(1)} %get-tuple-element.10.refs_2_, ...), custom_call_target="tpu_custom_call" | custom-call | tf_op jit(solution)/shard_map/pallas_call | solution.py:660

commit v9 on v8

--- a/solution.py
+++ b/solution.py
@@ -143,11 +143,11 @@
 
     def z_gather(phase, buf, h, i):
         ref = buf.at[h, t, i]
-        for k in PEERS:
+        for k in ((2, 1, 3), (2, 3, 1))[h]:
             remote(ref, ref, zs.at[phase, h, i], zr.at[phase, h, i], tp=other(t, k)).start()
 
     def z_scatter(phase, send, recv, h, i):
-        for k in PEERS:
+        for k in ((2, 1, 3), (2, 3, 1))[h]:
             b = other(t, k)
             remote(
                 send.at[h, b, i], recv.at[h, t, i], zs.at[phase, h, i], zr.at[phase, h, i], tp=b
@@ -164,7 +164,7 @@
     def z_sum(phase, send, recv, h, i, total):
         z_all(phase, recv, h, i).wait_recv()
         total = total + send[h, t, i].astype(jnp.float32)
-        for k in PEERS:
+        for k in ((2, 1, 3), (2, 3, 1))[h]:
             total = total + recv[h, other(t, k), i].astype(jnp.float32)
         return total.astype(jnp.bfloat16)
 
@@ -187,7 +187,7 @@
     def rs_start(phase, h):
         S, RA, RB, UA, UB, VA, VB = rs_bufs[phase]
         ca, cb = widths(S.shape[-1])
-        for k in PEERS:
+        for k in ((2, 1, 3), (2, 3, 1))[h]:
             y2, x2 = other(y, k), other(x, k)
             push(phase, h, 0, S.at[h, y2, :, 0], RA.at[h, y], fsdp=y2 * SIDE + x)
             push(
@@ -199,20 +199,20 @@
         ca, cb = widths(S.shape[-1])
         f_all(phase, h, 0).wait_recv()
         total = S[h, y, :, 0].astype(jnp.float32)
-        for k in PEERS:
+        for k in ((2, 1, 3), (2, 3, 1))[h]:
             total = total + RA[h, other(y, k)].astype(jnp.float32)
         UA[h] = total.astype(jnp.bfloat16)
-        for k in PEERS:
+        for k in ((2, 1, 3), (2, 3, 1))[h]:
             x2 = other(x, k)
             push(
                 phase, h, 2, UA.at[h, x2 >> 1, :, span(x2 & 1, ca, ca)], VA.at[h, x], fsdp=y * SIDE + x2
             )
         f_all(phase, h, 1).wait_recv()
         total = S[h, :, j, 1, :, span(g, ca, cb)].astype(jnp.float32)
-        for k in PEERS:
+        for k in ((2, 1, 3), (2, 3, 1))[h]:
             total = total + RB[h, other(x, k)].astype(jnp.float32)
         UB[h] = total.astype(jnp.bfloat16)
-        for k in PEERS:
+        for k in ((2, 1, 3), (2, 3, 1))[h]:
             y2 = other(y, k)
             push(phase, h, 3, UB.at[h, y2], VB.at[h, y], fsdp=y2 * SIDE + x)
 
@@ -221,11 +221,11 @@
         ca, cb = widths(S.shape[-1])
         f_all(phase, h, 2).wait_recv()
         first = UA[h, j, :, span(g, ca, ca)].astype(jnp.float32)
-        for k in PEERS:
+        for k in ((2, 1, 3), (2, 3, 1))[h]:
             first = first + VA[h, other(x, k)].astype(jnp.float32)
         f_all(phase, h, 3).wait_recv()
         second = UB[h, y].astype(jnp.float32)
-        for k in PEERS:
+        for k in ((2, 1, 3), (2, 3, 1))[h]:
             second = second + VB[h, other(y, k)].astype(jnp.float32)
         return first, second
 
@@ -233,7 +233,7 @@
         ca, cb = widths(buf.shape[-1])
         first = buf.at[h, y, j, 0, :, span(g, ca, ca)]
         second = buf.at[h, y, j, 1, :, span(g, ca, cb)]
-        for k in PEERS:
+        for k in ((2, 1, 3), (2, 3, 1))[h]:
             push(phase, h, 0, first, first, fsdp=y * SIDE + other(x, k))
             push(phase, h, 1, second, second, fsdp=other(y, k) * SIDE + x)
 
@@ -241,11 +241,11 @@
         ca, cb = widths(buf.shape[-1])
         first = buf.at[h, y, :, 0]
         f_all(phase, h, 0).wait_recv()
-        for k in PEERS:
+        for k in ((2, 1, 3), (2, 3, 1))[h]:
             push(phase, h, 2, first, first, fsdp=other(y, k) * SIDE + x)
         second = buf.at[h, :, j, 1, :, span(g, ca, cb)]
         f_all(phase, h, 1).wait_recv()
-        for k in PEERS:
+        for k in ((2, 1, 3), (2, 3, 1))[h]:
             push(phase, h, 3, second, second, fsdp=y * SIDE + other(x, k))
 
     def last_mid(h):
@@ -255,7 +255,7 @@
 
         @pl.when(core == 0)
         def _():
-            for k in PEERS:
+            for k in ((2, 1, 3), (2, 3, 1))[h]:
                 push(AG_GRAD0, h, 2, first, first, fsdp=other(y, k) * SIDE + x)
 
         @pl.when(core == 1)
@@ -267,7 +267,7 @@
 
         @pl.when(core == 0)
         def _():
-            for k in PEERS:
+            for k in ((2, 1, 3), (2, 3, 1))[h]:
                 push(AG_GRAD0, h, 3, second, second, fsdp=y * SIDE + other(x, k))
 
         @pl.when(core == 1)
@@ -426,8 +426,12 @@
         c.start()
     for c in loads[1:8]:
         c.wait()
-    for c in swaps[:6]:
-        c.wait_recv()
+
+    @pl.when(core == 1)
+    def _():
+        for c in swaps[:6]:
+            c.wait_recv()
+
     for h in HALVES:
         project(0, AG_STREAM0, RS_QKV0, h)
     swaps[6].start()
@@ -456,6 +460,11 @@
             z_gather(AG_STREAM1, X.at[1], h, i)
     for h in HALVES:
         rs_mid(RS_HEAD1, h)
+    @pl.when(core == 0)
+    def _():
+        for c in swaps[:6]:
+            c.wait_recv()
+
     for h in HALVES:
         project(1, AG_STREAM1, RS_QKV1, h)
     x_far.start()

time: 112 us -> 112 us (level)
  no operation moved by 1% of the time
where the time goes in v9:
time: 112 us
  Pallas kernels  111 us (99%)
    pallas_call x1, Pallas kernels, local(): pl.pallas_call(kernel, out_shape=[pltpu.VMEM(w.shape, f32) for w in (quer...  109 us
    pallas_call x1, Pallas kernels, local(): pl.pallas_call(write_out, out_shape=[jax.ShapeDtypeStruct(r.shape, r.dtyp...  2.39 us

profile of v9, /device:TPU:0, one launch (start us, length us, event | category | flops | bytes accessed | tf_op | source)
XLA Modules:
  0.0 111.6 jit_solution(11886732197377328158)
XLA Ops:
  0.6 108.5 %shard_map.129 = (f32[1,512,1024]{2,1,0:T(8,128)S(1)}, f32[1,512,256]{2,1,0:T(8,128)S(1)}, f32[1,512,256]{2,1,0:T(8,128)S(1)}, f32[1,1024,512]{2,1,0:T(8,128)S(1)}) custom-call(bf16[2,2,2,2,16,512]{5,4,3,2,1,0:T(8,128)(2,1)} %bitcast.5, bf16[2,2,2,2,16,512]{5,4,3,2,1,0:T(8,128)(2,1)} %bitcast.6, s32[2,128]{1,0:T(2,128)} %noise.1, s32[2,2,16]{2,1,0:T(2,128)} %bitcast.7, ...), custom_call_target="tpu_custom_call" | custom-call | tf_op jit(solution)/shard_map/pallas_call | solution.py:613
  109.2 2.4 %shard_map.130 = (f32[1,512,1024]{2,1,0:T(8,128)}, f32[1,512,256]{2,1,0:T(8,128)}, f32[1,512,256]{2,1,0:T(8,128)}, f32[1,1024,512]{2,1,0:T(8,128)}) custom-call(f32[1,512,1024]{2,1,0:T(8,128)S(1)} %get-tuple-element.8.refs_0_, f32[1,512,256]{2,1,0:T(8,128)S(1)} %get-tuple-element.9.refs_1_, f32[1,512,256]{2,1,0:T(8,128)S(1)} %get-tuple-element.10.refs_2_, ...), custom_call_target="tpu_custom_call" | custom-call | tf_op jit(solution)/shard_map/pallas_call | solution.py:669
